TPU v7x, 32 devices: a whole 2x2x4 slice. The times are simulated.
32 devices in a mesh: dp: 4 (over y, core), expert: 8 (over z, x).
Axes of the slice: x: 2, y: 2, z: 4, core: 2. Of those that a mesh axis runs over, the one named last changes fastest.
Arguments:
- tokens: bfloat16 [2, 8192, 1536], P(None, ('dp', 'expert')), may hold values from -6 to 6
- segments: int32 [2, 8192], P(None, ('dp', 'expert')), may hold values from 0 to 3, as said below
- routes: int32 [2, 8192, 4], P(None, ('dp', 'expert')), may hold values from 0 to 31, all different within a row; in each aligned block of 256 rows (0 to 255, 256 to 511, ..., all dimensions but the last counted through in order) at most 64 rows name the same one
- norm_one: bfloat16 [1536], P('dp'), may hold values from 0.099609375 to 1.8984375
- norm_two: bfloat16 [1536], P('dp'), may hold values from 0.099609375 to 1.8984375
- w_query: bfloat16 [1536, 1536], P('dp'), may hold values from -0.15625 to 0.15625
- key_value_weight: bfloat16 [1536, 512], P('dp'), may hold values from -0.15625 to 0.15625
- w_out_attn: bfloat16 [1536, 1536], P('dp'), may hold values from -0.875 to 0.875
- w_router: bfloat16 [1536, 32], P('dp'), may hold values from -0.076171875 to 0.076171875
- w_in: bfloat16 [32, 1536, 1536], P('expert'), may hold values from -0.15625 to 0.15625
- w_out: bfloat16 [32, 768, 1536], P('expert'), may hold values from -0.4375 to 0.4375
- cotangent: bfloat16 [2, 8192, 1536], P(None, ('dp', 'expert')), may hold values from -6 to 6
Outputs:
- output_act: bfloat16 [2, 8192, 1536], P(None, ('dp', 'expert'))
- grad_input: bfloat16 [2, 8192, 1536], P(None, ('dp', 'expert'))
- grad_norm_one: float32 [1536], P('dp')
- grad_norm_two: float32 [1536], P('dp')
- grad_query: float32 [1536, 1536], P('dp')
- grad_keyval: float32 [1536, 512], P('dp')
- grad_out_attn: float32 [1536, 1536], P('dp')
- grad_router: float32 [1536, 32], P('dp')
- grad_w_in: float32 [32, 1536, 1536], P('expert', 'dp')
- grad_w_out: float32 [32, 768, 1536], P('expert', 'dp')
Inputs may be any that keep to these rules, and one draw needn't show every extreme that they name: `routes`: in each aligned block of 256 rows (the tokens of one device in one micro-batch) no expert is named by more than 64 rows, a bound that some block reaches. `segments`: within each sequence of 256 tokens the numbers start at 0, never fall and rise by one at three places; equal numbers mark one document.
All inputs are finite; a program needn't handle non-finite values.
Results may differ from a plain program's by a relative error of at most 0.02.
Values may be sent and summed in bfloat16 or wider, within the bound.
No kernel may reach another device: no remote copies, remote signals or barrier semaphores. Data moves between devices by JAX's collectives and lax.ppermute only.
A program may use at most 320 MiB of HBM per device.

v0:
```python
import functools
import math

import jax
import jax.numpy as jnp
from jax import lax
from jax.experimental import pallas as pl
from jax.experimental.pallas import tpu as pltpu
from jax.sharding import PartitionSpec as P

QUERY_HEADS = 12
KEY_VALUE_HEADS = 2
HEAD_SIZE = 128
FF = 768
TOPK = 4
EXPERTS = 32
EXTRA = 16
PIECES = 3
GROUP = 8

eps_norm = 1e-06
rope_base = 1000000.0
mask_fill = -1e30
highest = lax.Precision.HIGHEST


def rms_scale(tensor):
    return lax.rsqrt(jnp.mean(tensor * tensor, axis=-1, keepdims=True) + eps_norm)


def rope_tables(sequence_length, head_width):
    positions = jnp.arange(sequence_length).astype(jnp.float32)
    frequency = rope_base ** (-(jnp.arange(head_width // 2).astype(jnp.float32) * 2.0) / head_width)
    angles = positions[:, None] * frequency[None, :]
    return (jnp.cos(angles), jnp.sin(angles))

SCORE_SCALE = 1.0 / math.sqrt(HEAD_SIZE)
GELU_SCALE = math.sqrt(2.0 / math.pi)
GELU_CUBE = 0.044715
SMALL_COST = pl.CostEstimate(flops=1_000_000, bytes_accessed=1_000_000, transcendentals=0)


def after(value, *earlier):
    return lax.optimization_barrier((value,) + earlier)[0]


def slot_hits(routes_all, first_expert, local_experts, capacity):
    rows = routes_all.shape[-1]
    names = first_expert + jnp.arange(local_experts, dtype=jnp.int32)
    named = routes_all[:, None].astype(jnp.int32) == names[None, :, None, None]
    member = jnp.any(named, axis=2)
    lower = (jnp.arange(rows)[:, None] < jnp.arange(rows)[None, :]).astype(jnp.bfloat16)
    rank = dot32(member.astype(jnp.bfloat16).reshape(-1, rows), lower).reshape(member.shape)
    slots = jnp.arange(capacity, dtype=jnp.float32)
    return member[:, :, None, :] & (rank[:, :, None, :] == slots[None, None, :, None])


def pack_pieces(values, out_ref, first_row):
    rows = values.shape[1]
    rest = values
    for piece in range(PIECES):
        part = rest.astype(jnp.bfloat16)
        rest = rest - part.astype(jnp.float32)
        for half in range(EXPERTS // EXTRA):
            at = (piece * (EXPERTS // EXTRA) + half) * rows
            out_ref[first_row : first_row + EXTRA, at : at + rows] = part[
                half * EXTRA : (half + 1) * EXTRA
            ]


def dot32(left, right):
    return jnp.dot(left, right, preferred_element_type=jnp.float32)


def dot_nt(left, right):
    return lax.dot_general(
        left, right, (((1,), (1,)), ((), ())), preferred_element_type=jnp.float32
    )


def dot_tn(left, right):
    return lax.dot_general(
        left, right, (((0,), (0,)), ((), ())), preferred_element_type=jnp.float32
    )


def mask_of(seg_col, seg_row):
    rows = seg_col.shape[0]
    query_at = lax.broadcasted_iota(jnp.int32, (rows, rows), 0)
    key_at = lax.broadcasted_iota(jnp.int32, (rows, rows), 1)
    return (seg_col == seg_row) & (query_at >= key_at)


def softmax_rows(query, key, allowed):
    scores = jnp.where(allowed, dot_nt(query, key) * SCORE_SCALE, mask_fill)
    weight = jnp.exp(scores - jnp.max(scores, axis=-1, keepdims=True))
    return weight / jnp.sum(weight, axis=-1, keepdims=True)


def from_blocks(starts_ref, rows_ref, blocks):
    total = None
    for at, block_ref in enumerate(blocks):
        span = block_ref.shape[0]
        columns = pl.ds(pl.multiple_of(starts_ref[at], 128), span)
        part = dot32(rows_ref[:, columns], block_ref[...])
        total = part if total is None else total + part
    return total


def attention_kernel(
    starts_ref,
    tok_ref,
    seg_col_ref,
    seg_row_ref,
    routes_ref,
    cos_ref,
    sin_ref,
    *refs,
):
    weight_refs = refs[:-7]
    xn1_ref, query_ref, keyval_ref, mixed_ref, gates_ref, gates_pack_ref, gains_ref = refs[-7:]

    @pl.when(pl.program_id(0) == 0)
    def _():
        for at, block_ref in enumerate(weight_refs):
            span, columns = block_ref.shape
            pad = block_ref[:, columns - 128 :].astype(jnp.float32).T
            place = pl.ds(pl.multiple_of(starts_ref[at], 128), span)
            gains_ref[:, place] = pad[2 * EXPERTS : 2 * EXPERTS + 8]

    tok = tok_ref[...].astype(jnp.float32)
    xn1_ref[...] = (tok * rms_scale(tok) * gains_ref[0:1, :]).astype(jnp.bfloat16)
    proj = from_blocks(starts_ref, xn1_ref, weight_refs)
    cos, sin = cos_ref[...], sin_ref[...]

    def rotate(part):
        return (part * cos + pltpu.roll(part, HEAD_SIZE // 2, 1) * sin).astype(jnp.bfloat16)

    q_width = QUERY_HEADS * HEAD_SIZE
    k_width = KEY_VALUE_HEADS * HEAD_SIZE
    for head in range(QUERY_HEADS):
        span = slice(head * HEAD_SIZE, (head + 1) * HEAD_SIZE)
        query_ref[:, span] = rotate(proj[:, span])
    for head in range(KEY_VALUE_HEADS):
        span = slice(head * HEAD_SIZE, (head + 1) * HEAD_SIZE)
        keyval_ref[:, span] = rotate(proj[:, q_width:][:, span])
    keyval_ref[:, k_width:] = proj[:, q_width + k_width : q_width + 2 * k_width].astype(
        jnp.bfloat16
    )
    logits = proj[:, q_width + 2 * k_width :]
    columns = lax.broadcasted_iota(jnp.int32, logits.shape, 1)
    named = [columns == routes_ref[:, j : j + 1] for j in range(TOPK)]
    chosen = [jnp.sum(jnp.where(hit, logits, 0.0), axis=-1, keepdims=True) for hit in named]
    top = functools.reduce(jnp.maximum, chosen)
    weight = [jnp.exp(part - top) for part in chosen]
    total = functools.reduce(jnp.add, weight)
    gates = jnp.full(logits.shape, -1.0, jnp.float32)
    for hit, part in zip(named, weight):
        gates = jnp.where(hit, part / total, gates)
    gates_ref[...] = gates
    pack_pieces(gates.T[:EXPERTS], gates_pack_ref, 0)
    allowed = mask_of(seg_col_ref[...], seg_row_ref[...])
    for head in range(QUERY_HEADS):
        span = slice(head * HEAD_SIZE, (head + 1) * HEAD_SIZE)
        group = head // (QUERY_HEADS // KEY_VALUE_HEADS)
        key = keyval_ref[:, group * HEAD_SIZE : (group + 1) * HEAD_SIZE]
        value = keyval_ref[:, k_width + group * HEAD_SIZE : k_width + (group + 1) * HEAD_SIZE]
        probs = softmax_rows(query_ref[:, span], key, allowed)
        mixed_ref[:, span] = dot32(probs.astype(jnp.bfloat16), value).astype(jnp.bfloat16)


def hidden_kernel(starts_ref, mixed_ref, tok_ref, gains_ref, pack_ref, *refs):
    weight_refs = refs[:-2]
    hidden_ref, xn2_ref = refs[-2:]
    rows = tok_ref.shape[0]
    hidden = tok_ref[...].astype(jnp.float32) + from_blocks(
        starts_ref, mixed_ref, weight_refs
    )
    hidden_ref[...] = hidden
    xn2_ref[:rows, :] = (hidden * rms_scale(hidden) * gains_ref[1:2, :]).astype(jnp.bfloat16)
    xn2_ref[rows:, :] = pack_ref[...]


def backward_kernel(
    own_ref,
    left_ref,
    right_ref,
    cot_ref,
    hidden_ref,
    tok_ref,
    query_ref,
    keyval_ref,
    seg_col_ref,
    seg_row_ref,
    gates_ref,
    gains_ref,
    cos_ref,
    sin_ref,
    *refs,
):
    weight_ref, out_weight_ref = refs[:2]
    grad_tok_ref, grad_proj_ref, grad_attn_ref, gain_sum_ref, mixed_grad_ref = refs[2:]
    width = tok_ref.shape[1]
    q_width = QUERY_HEADS * HEAD_SIZE
    k_width = KEY_VALUE_HEADS * HEAD_SIZE
    proj_width = q_width + 2 * k_width
    rows = tok_ref.shape[0]
    sums = [ref[...].astype(jnp.float32) for ref in (own_ref, left_ref, right_ref)]
    sums = sums[0] + sums[1] + sums[2]
    grad_xn2, pack = sums[:rows], sums[rows:]
    halves = EXPERTS // EXTRA
    lines = [
        sum(
            pack[:, (piece * halves + half) * rows : (piece * halves + half + 1) * rows]
            for piece in range(PIECES)
        )
        for half in range(halves)
    ]
    lines.append(jnp.zeros((128 - EXPERTS, rows), jnp.float32))
    grad_gates = jnp.concatenate(lines, axis=0).T
    hidden = hidden_ref[...]
    scale = rms_scale(hidden)
    unit = hidden * scale
    gain_sum_ref[...] = jnp.zeros(gain_sum_ref.shape, jnp.float32)
    gain_sum_ref[1:2, :] = jnp.sum(grad_xn2 * unit, axis=0, keepdims=True)
    grad_unit = grad_xn2 * gains_ref[1:2, :]
    grad_hidden = cot_ref[...].astype(jnp.float32) + scale * (
        grad_unit - unit * jnp.mean(grad_unit * unit, axis=-1, keepdims=True)
    )
    grad_attn_ref[...] = grad_hidden.astype(jnp.bfloat16)
    mixed_grad_ref[...] = dot_nt(grad_attn_ref[...], out_weight_ref[...]).astype(jnp.bfloat16)
    cos, sin = cos_ref[...], sin_ref[...]

    def unrotate(part):
        return (part * cos - pltpu.roll(part, HEAD_SIZE // 2, 1) * sin).astype(jnp.bfloat16)

    allowed = mask_of(seg_col_ref[...], seg_row_ref[...])
    per_group = QUERY_HEADS // KEY_VALUE_HEADS
    for group in range(KEY_VALUE_HEADS):
        key_span = slice(group * HEAD_SIZE, (group + 1) * HEAD_SIZE)
        value_span = slice(k_width + group * HEAD_SIZE, k_width + (group + 1) * HEAD_SIZE)
        key, value = keyval_ref[:, key_span], keyval_ref[:, value_span]
        grad_key = jnp.zeros(key.shape, jnp.float32)
        grad_value = jnp.zeros(key.shape, jnp.float32)
        for head in range(group * per_group, (group + 1) * per_group):
            span = slice(head * HEAD_SIZE, (head + 1) * HEAD_SIZE)
            query, grad_mixed = query_ref[:, span], mixed_grad_ref[:, span]
            probs = softmax_rows(query, key, allowed)
            grad_value += dot_tn(probs.astype(jnp.bfloat16), grad_mixed)
            grad_probs = dot_nt(grad_mixed, value)
            mean = jnp.sum(probs * grad_probs, axis=-1, keepdims=True)
            grad_scores = (probs * (grad_probs - mean)).astype(jnp.bfloat16)
            grad_proj_ref[:, span] = unrotate(dot32(grad_scores, key) * SCORE_SCALE)
            grad_key += dot_tn(grad_scores, query)
        grad_proj_ref[:, q_width + group * HEAD_SIZE : q_width + (group + 1) * HEAD_SIZE] = (
            unrotate(grad_key * SCORE_SCALE)
        )
        first = q_width + k_width + group * HEAD_SIZE
        grad_proj_ref[:, first : first + HEAD_SIZE] = grad_value.astype(jnp.bfloat16)
    gates = jnp.maximum(gates_ref[...], 0.0)
    grad_logits = gates * (grad_gates - jnp.sum(gates * grad_gates, axis=-1, keepdims=True))
    high = grad_logits.astype(jnp.bfloat16).astype(jnp.float32)
    low = pltpu.roll(grad_logits - high, EXPERTS, 1)
    grad_proj_ref[:, proj_width:] = (high + low).astype(jnp.bfloat16)
    grad_xn1 = dot_nt(grad_proj_ref[...], weight_ref[...])
    tok = tok_ref[...].astype(jnp.float32)
    scale = rms_scale(tok)
    unit = tok * scale
    gain_sum_ref[0:1, :] = jnp.sum(grad_xn1 * unit, axis=0, keepdims=True)
    grad_unit = grad_xn1 * gains_ref[0:1, :]
    grad_tok_ref[...] = (
        grad_hidden
        + scale * (grad_unit - unit * jnp.mean(grad_unit * unit, axis=-1, keepdims=True))
    ).astype(jnp.bfloat16)


def ring_order(peers):
    minor = peers // 4
    walk = []
    for col in range(minor):
        line = range(4) if col % 2 == 0 else range(3, -1, -1)
        walk += [row * minor + col for row in line]
    return walk


def ring_step(part, shift, peers):
    order = ring_order(peers)
    pairs = [(order[i], order[(i + shift) % peers]) for i in range(peers)]
    return lax.ppermute(part, "expert", pairs)


class RingGather:
    def __init__(self, part, peers, half):
        self.peers, self.half = peers, half
        self.from_left, self.from_right = [part], [part]
        self.far = None
        self.got = ()

    def step(self, *earlier):
        left, right = self.from_left[-1], self.from_right[-1]
        last = len(self.from_left) == self.peers // 2
        if last:
            left, right = left[: self.half], right[self.half :]
        left, right = self.sent = lax.optimization_barrier((left, right) + earlier)[:2]
        left, right = ring_step(left, 1, self.peers), ring_step(right, -1, self.peers)
        self.got = (left, right)
        if last:
            self.far = (left, right)
        else:
            self.from_left.append(left)
            self.from_right.append(right)
        return self

    def rows(self, k, first, count):
        if k < len(self.from_left):
            return self.from_left[k], first
        if k > self.peers // 2:
            return self.from_right[self.peers - k], first
        if first < self.half:
            return self.far[0], first
        return self.far[1], first - self.half

    def stack_rows(self, first, count):
        found = [self.rows(k, first, count) for k in range(self.peers)]
        return jnp.stack([array[at : at + count] for array, at in found])


class RingScatter:
    def __init__(self, part, far, peers):
        self.part, self.far, self.peers = part, far, peers
        self.at = peers // 2
        self.half = far[0].shape[0]

    def step(self, *earlier):
        peers, k, half = self.peers, self.at, self.half
        if k == peers // 2:
            left, right = lax.optimization_barrier(tuple(self.far) + earlier)[:2]
        else:
            left, right = self.part(k), self.part(peers - k)
            if earlier:
                self.left, self.right = lax.optimization_barrier(
                    (self.left, self.right) + earlier
                )[:2]
            if k == peers // 2 - 1:
                kept = left[half:].astype(jnp.bfloat16), right[:half].astype(jnp.bfloat16)
                left = jnp.concatenate([add_rows(left[:half], self.left), kept[0]], axis=0)
                right = jnp.concatenate([kept[1], add_rows(right[half:], self.right)], axis=0)
            else:
                left, right = add_rows(left, self.left), add_rows(right, self.right)
        left, right = self.sent = lax.optimization_barrier((left, right))
        self.left = ring_step(left, -1, peers)
        self.right = ring_step(right, 1, peers)
        self.got = (self.left, self.right)
        self.at = k - 1
        return self


def add_rows(left, right):
    return (left.astype(jnp.float32) + right.astype(jnp.float32)).astype(jnp.bfloat16)


def expert_kernel(sources, *refs):
    rows_refs = refs[:sources]
    grad_refs = refs[sources : 2 * sources]
    gate_refs = refs[2 * sources : 3 * sources]
    w_in_ref, w_out_ref = refs[3 * sources : 3 * sources + 2]
    (
        back_rows_ref,
        back_grads_ref,
        grad_gate_ref,
        picked_ref,
        grad_result_ref,
        activated_ref,
        grad_pre_ref,
    ) = refs[-7:]
    capacity, width = rows_refs[0].shape
    for k in range(sources):
        picked_ref[pl.ds(k * capacity, capacity), :] = rows_refs[k][...]
    pre_act = dot32(picked_ref[...], w_in_ref[...])
    gate_part = pre_act[:, :FF]
    up_part = pre_act[:, FF:]
    square = gate_part * gate_part
    bend = jnp.tanh(GELU_SCALE * gate_part * (1.0 + GELU_CUBE * square))
    lift = 0.5 * (1.0 + bend)
    gelu_val = gate_part * lift
    slope = lift + 0.5 * gate_part * (1.0 - bend * bend) * (
        GELU_SCALE * (1.0 + 3.0 * GELU_CUBE * square)
    )
    activated_ref[...] = (gelu_val * up_part).astype(jnp.bfloat16)
    result = dot32(activated_ref[...], w_out_ref[...])
    for k in range(sources):
        gates = gate_refs[k][...]
        span = slice(k * capacity, (k + 1) * capacity)
        grad_rows = grad_refs[k][...].astype(jnp.float32)
        grad_gate_ref[span, :] = jnp.sum(result[span] * grad_rows, axis=-1, keepdims=True)
        back_rows_ref[k] = (result[span] * gates).astype(jnp.bfloat16)
        grad_result_ref[span, :] = (grad_rows * gates).astype(jnp.bfloat16)
    grad_act = lax.dot_general(
        grad_result_ref[...],
        w_out_ref[...],
        (((1,), (1,)), ((), ())),
        preferred_element_type=jnp.float32,
    )
    grad_pre_ref[:, :FF] = (grad_act * up_part * slope).astype(jnp.bfloat16)
    grad_pre_ref[:, FF:] = (grad_act * gelu_val).astype(jnp.bfloat16)
    grad_in = lax.dot_general(
        grad_pre_ref[...],
        w_in_ref[...],
        (((1,), (1,)), ((), ())),
        preferred_element_type=jnp.float32,
    ).astype(jnp.bfloat16)
    for k in range(sources):
        back_grads_ref[k] = grad_in[k * capacity : (k + 1) * capacity]


def expert_pass(rows_list, grads_list, gate_slots, w_in, w_out, held_outs, position, first, count):
    sources = len(rows_list)
    local_experts, width, _ = w_in.shape
    slots = rows_list[0].shape[0]
    capacity = slots // local_experts
    held = sources * capacity
    block_spec = pl.BlockSpec((capacity, width), lambda e: (e + first, 0))
    back_spec = pl.BlockSpec((sources, capacity, width), lambda e: (0, e + first, 0))
    column_spec = pl.BlockSpec((None, held, 1), lambda e: (e + first, 0, 0))

    def kept_spec(columns):
        return pl.BlockSpec((None, held, columns), lambda e: (e + first, position[0], 0))

    def kept_shape(columns):
        return jax.ShapeDtypeStruct((local_experts, position[1] * held, columns), jnp.bfloat16)

    kept_widths = (width, width, FF, 2 * FF)
    first_held = 3 * sources + 2
    given = [(i, part) for i, part in enumerate(held_outs) if part is not None]
    return pl.pallas_call(
        functools.partial(expert_kernel, sources),
        grid=(count,),
        in_specs=[block_spec] * (2 * sources)
        + [pl.BlockSpec((capacity, 1), lambda e: (e + first, 0))] * sources
        + [
            pl.BlockSpec((None, width, 2 * FF), lambda e: (e + first, 0, 0)),
            pl.BlockSpec((None, FF, width), lambda e: (e + first, 0, 0)),
        ]
        + [pl.BlockSpec(memory_space=pl.ANY)] * len(given),
        out_specs=[back_spec, back_spec, column_spec] + [kept_spec(c) for c in kept_widths],
        out_shape=[
            jax.ShapeDtypeStruct((sources, slots, width), jnp.bfloat16),
            jax.ShapeDtypeStruct((sources, slots, width), jnp.bfloat16),
            jax.ShapeDtypeStruct((local_experts, held, 1), jnp.float32),
        ]
        + [kept_shape(c) for c in kept_widths],
        input_output_aliases={first_held + at: i for at, (i, _) in enumerate(given)},
        compiler_params=pltpu.CompilerParams(vmem_limit_bytes=60 * 1024 * 1024),
        cost_estimate=SMALL_COST,
        name="expert_pass",
    )(*rows_list, *grads_list, *gate_slots, w_in, w_out, *[part for _, part in given])


def block_call(kernel, operands, out_shape, name, scratch=(), prefetch=None):
    def spec(array, lead=(), rows=None):
        rest = array.shape[len(lead) :]
        at = lead + (0,) * len(rest)
        if rows is not None:
            count, block = rows if isinstance(rows, tuple) else (rows, 0)
            rest = (count,) + rest[1:]
            at = lead + (block,) + (0,) * (len(rest) - 1)
        return pl.BlockSpec((None,) * len(lead) + rest, lambda *_: at)

    scalars = [] if prefetch is None else [prefetch]
    return pl.pallas_call(
        kernel,
        grid_spec=pltpu.PrefetchScalarGridSpec(
            num_scalar_prefetch=len(scalars),
            grid=(1,),
            in_specs=[spec(*operand) for operand in operands],
            out_specs=[spec(shape) for shape in out_shape],
            scratch_shapes=list(scratch),
        ),
        out_shape=out_shape,
        compiler_params=pltpu.CompilerParams(vmem_limit_bytes=60 * 1024 * 1024),
        cost_estimate=SMALL_COST,
        name=name,
    )(*scalars, *[operand[0] for operand in operands])


def pick_kernel(shares, gated, first_ref, place_ref, *refs):
    at = 0
    outs = refs[sum(count for _, count in shares) + (len(shares) if gated else 0) :]
    for number, (k, count) in enumerate(shares):
        total, row = None, 0
        for block_ref in refs[at : at + count]:
            held = block_ref.shape[0]
            part = dot32(place_ref[k, :, row : row + held], block_ref[...])
            total = part if total is None else total + part
            row += held
        outs[number][...] = total.astype(jnp.bfloat16)
        at += count
        if gated:
            slot_gates(first_ref[0], place_ref[k], refs[at], outs[len(shares) + number])
            at += 1


def slot_gates(first_expert, place, pack_ref, out_ref):
    slots, rows = place.shape
    pack = pack_ref[...].astype(jnp.float32)
    halves = EXPERTS // EXTRA
    line = lax.broadcasted_iota(jnp.int32, (EXTRA, rows), 0)
    local_experts = slots * 4 // rows
    capacity = rows // 4
    for e in range(local_experts):
        gate = jnp.zeros((1, rows), jnp.float32)
        for half in range(halves):
            hit = line + half * EXTRA == first_expert + e
            for piece in range(PIECES):
                at = (piece * halves + half) * rows
                gate += jnp.sum(
                    jnp.where(hit, pack[:, at : at + rows], 0.0), axis=0, keepdims=True
                )
        span = slice(e * capacity, (e + 1) * capacity)
        out_ref[span, :] = jnp.sum(
            place[span].astype(jnp.float32) * gate, axis=-1, keepdims=True
        )


def pick_rows(first_expert, place, ring, distances, gated):
    _, slots, rows = place.shape
    half = rows // 2
    operands, shares = [], []
    for k in distances:
        spans = [(0, rows)]
        if k == ring.peers // 2 and ring.half < rows:
            spans = [(0, half), (half, half)]
        shares.append((k, len(spans)))
        for at, count in spans + ([(rows, EXTRA)] if gated else []):
            array, at = ring.rows(k, at, count)
            operands.append((array, (), (count, at // count)))
    width = operands[0][0].shape[-1]
    out_shape = [jax.ShapeDtypeStruct((slots, width), jnp.bfloat16) for _ in distances]
    if gated:
        out_shape += [jax.ShapeDtypeStruct((slots, 1), jnp.float32) for _ in distances]
    return block_call(
        functools.partial(pick_kernel, shares, gated),
        [(place,)] + operands,
        out_shape,
        "pick_rows",
        prefetch=first_expert,
    )


def spread_kernel(middle, spans, held, first_ref, place_ref, rows_ref, grads_ref, gate_ref, *refs):
    out_ref, *far_refs = refs[held:]
    place = place_ref[...]
    rows = place.shape[1]
    out_ref[:rows, :] = dot_tn(place, grads_ref[...]).astype(jnp.bfloat16)
    out_ref[rows + EXTRA :, :] = dot_tn(place, rows_ref[...]).astype(jnp.bfloat16)
    capacity = gate_ref.shape[1]
    expert = lax.broadcasted_iota(jnp.int32, (EXPERTS, rows), 0) - first_ref[0]
    gates = jnp.zeros((EXPERTS, rows), jnp.float32)
    for e in range(gate_ref.shape[0]):
        hit = place[e * capacity : (e + 1) * capacity].astype(jnp.float32)
        line = jnp.sum(hit * gate_ref[e], axis=0, keepdims=True)
        gates = jnp.where(expert == e, line, gates)
    pack_pieces(gates, out_ref, rows)

    @pl.when(pl.program_id(0) == middle)
    def _():
        for far_ref, (row, count) in zip(far_refs, spans):
            far_ref[...] = out_ref[row : row + count, :]


def spread_rows(first_expert, place, rows_back, grads_back, gate_slots, group, spans, held):
    sources, slots, rows = place.shape
    width = rows_back.shape[-1]
    local_experts = gate_slots.shape[0]
    base = group * GROUP
    by_source = pl.BlockSpec((None, slots, width), lambda k, f: (k, 0, 0))
    held = [] if held is None else [held]
    out_shape = [jax.ShapeDtypeStruct((sources, 2 * rows + EXTRA, width), jnp.bfloat16)]
    out_shape += [jax.ShapeDtypeStruct((count, width), jnp.bfloat16) for _, count in spans]
    out_specs = [pl.BlockSpec((None, 2 * rows + EXTRA, width), lambda k, f: (base + k, 0, 0))]
    out_specs += [pl.BlockSpec((count, width), lambda k, f: (0, 0)) for _, count in spans]
    return pl.pallas_call(
        functools.partial(spread_kernel, sources // 2 - base, spans, len(held)),
        grid_spec=pltpu.PrefetchScalarGridSpec(
            num_scalar_prefetch=1,
            grid=(GROUP,),
            in_specs=[
                pl.BlockSpec((None, slots, rows), lambda k, f: (base + k, 0, 0)),
                by_source,
                by_source,
                pl.BlockSpec((local_experts, slots // local_experts, 1), lambda k, f: (0, k, 0)),
            ]
            + [pl.BlockSpec(memory_space=pl.ANY)] * len(held),
            out_specs=out_specs,
        ),
        out_shape=out_shape,
        input_output_aliases={5 + i: i for i in range(len(held))},
        compiler_params=pltpu.CompilerParams(vmem_limit_bytes=60 * 1024 * 1024),
        cost_estimate=SMALL_COST,
        name="spread_rows",
    )(first_expert, place, rows_back, grads_back, gate_slots, *held)


def weight_grad_kernel(left_ref, right_ref, *refs):
    refs[-1][...] = dot_tn(left_ref[...], right_ref[...]).astype(jnp.bfloat16)


def weight_grads(left, right, first, count, held_out):
    experts, held, height = left.shape
    columns = right.shape[-1]
    tile = min(height, 768)
    given = [] if held_out is None else [held_out]
    return pl.pallas_call(
        weight_grad_kernel,
        grid=(count, height // tile),
        in_specs=[
            pl.BlockSpec((None, held, tile), lambda e, i: (e + first, 0, i)),
            pl.BlockSpec((None, held, columns), lambda e, i: (e + first, 0, 0)),
        ]
        + [pl.BlockSpec(memory_space=pl.ANY)] * len(given),
        out_specs=pl.BlockSpec((None, tile, columns), lambda e, i: (e + first, i, 0)),
        out_shape=jax.ShapeDtypeStruct((experts, height, columns), jnp.bfloat16),
        input_output_aliases={2: 0} if given else {},
        compiler_params=pltpu.CompilerParams(vmem_limit_bytes=60 * 1024 * 1024),
        cost_estimate=SMALL_COST,
        name="weight_grads",
    )(left, right, *given)


def attention_forward(starts, tokens, seg_col, seg_row, routes, cos, sin, weights):
    count, rows, width = tokens.shape

    def by_micro(*shape):
        return pl.BlockSpec((None,) + shape, lambda m, s: (m,) + (0,) * len(shape))

    def shared(part):
        return pl.BlockSpec(part.shape, lambda m, s: (0, 0))

    kv_width = 2 * KEY_VALUE_HEADS * HEAD_SIZE
    shapes = [
        ((rows, width), jnp.bfloat16),
        ((rows, QUERY_HEADS * HEAD_SIZE), jnp.bfloat16),
        ((rows, kv_width), jnp.bfloat16),
        ((rows, QUERY_HEADS * HEAD_SIZE), jnp.bfloat16),
        ((rows, 128), jnp.float32),
        ((EXTRA, PIECES * EXPERTS // EXTRA * rows), jnp.bfloat16),
    ]
    return pl.pallas_call(
        attention_kernel,
        grid_spec=pltpu.PrefetchScalarGridSpec(
            num_scalar_prefetch=1,
            grid=(count,),
            in_specs=[
                by_micro(rows, width),
                by_micro(rows, 1),
                by_micro(1, rows),
                by_micro(rows, TOPK),
                shared(cos),
                shared(sin),
            ]
            + [shared(part) for part in weights],
            out_specs=[by_micro(*shape) for shape, _ in shapes]
            + [pl.BlockSpec((8, width), lambda m, s: (0, 0))],
        ),
        out_shape=[jax.ShapeDtypeStruct((count,) + shape, kind) for shape, kind in shapes]
        + [jax.ShapeDtypeStruct((8, width), jnp.float32)],
        compiler_params=pltpu.CompilerParams(vmem_limit_bytes=60 * 1024 * 1024),
        cost_estimate=SMALL_COST,
        name="attention_forward",
    )(starts, tokens, seg_col, seg_row, routes, cos, sin, *weights)


def join_kernel(starts_ref, *refs):
    for at, block_ref in enumerate(refs[:-1]):

        @pl.when(pl.program_id(0) == at)
        def _():
            refs[-1][...] = block_ref[...]


def join_blocks(starts, blocks):
    if len(blocks) == 1:
        return blocks[0]
    span, columns = blocks[0].shape
    return pl.pallas_call(
        join_kernel,
        grid_spec=pltpu.PrefetchScalarGridSpec(
            num_scalar_prefetch=1,
            grid=(len(blocks),),
            in_specs=[pl.BlockSpec((span, columns), lambda i, s: (0, 0)) for _ in blocks],
            out_specs=pl.BlockSpec((span, columns), lambda i, s: (s[i] // span, 0)),
        ),
        out_shape=jax.ShapeDtypeStruct((len(blocks) * span, columns), blocks[0].dtype),
        compiler_params=pltpu.CompilerParams(vmem_limit_bytes=60 * 1024 * 1024),
        cost_estimate=SMALL_COST,
        name="join_blocks",
    )(starts, *blocks)


def attention_grad_kernel(core_ref, xn1, mixed, *refs):
    count = xn1.shape[0]
    proj, attn, sums = [refs[i * count : (i + 1) * count] for i in range(3)]
    mine_ref, other_ref = refs[-2:]
    split = proj[0].shape[1]
    span = mine_ref.shape[0]
    grad = sum(dot_tn(xn1[m], proj[m][...]) for m in range(count))
    router = grad[:, split - 128 :]
    lane = lax.broadcasted_iota(jnp.int32, router.shape, 1)
    router = router + pltpu.roll(router, 128 - EXPERTS, 1)
    gain = sum(part[...] for part in sums)
    lines = [jnp.zeros((EXPERTS, gain.shape[1]), jnp.float32), gain]
    lines.append(jnp.zeros((128 - EXPERTS - gain.shape[0], gain.shape[1]), jnp.float32))
    router = jnp.where(lane < EXPERTS, router, jnp.concatenate(lines, axis=0).T)
    first = core_ref[0] == 0

    def put(columns, value):
        value = value.astype(jnp.bfloat16)
        low, high = value[:span], value[span:]
        mine_ref[:, columns] = jnp.where(first, low, high)
        other_ref[:, columns] = jnp.where(first, high, low)

    put(slice(0, split - 128), grad[:, : split - 128])
    put(slice(split - 128, split), router)
    put(slice(split, None), sum(dot_tn(mixed[m], attn[m][...]) for m in range(count)))


def attention_grads(core, xn1, mixed, proj, attn, gain_sums, parts):
    count, rows, width = xn1.shape
    span = width // parts
    lines = parts // 2
    columns = proj[0].shape[1] + attn[0].shape[1]
    by_line = pl.BlockSpec((count, rows, 2 * span), lambda i, c: (0, 0, i))

    def shared(part):
        return pl.BlockSpec(part.shape, lambda i, c: (0, 0))

    out_spec = pl.BlockSpec((None, span, columns), lambda i, c: (i, 0, 0))
    out_shape = jax.ShapeDtypeStruct((lines, span, columns), jnp.bfloat16)
    return pl.pallas_call(
        attention_grad_kernel,
        grid_spec=pltpu.PrefetchScalarGridSpec(
            num_scalar_prefetch=1,
            grid=(lines,),
            in_specs=[by_line, by_line]
            + [shared(p) for p in proj]
            + [shared(p) for p in attn]
            + [pl.BlockSpec((p.shape[0], 2 * span), lambda i, c: (0, i)) for p in gain_sums],
            out_specs=[out_spec, out_spec],
        ),
        out_shape=[out_shape, out_shape],
        compiler_params=pltpu.CompilerParams(vmem_limit_bytes=60 * 1024 * 1024),
        cost_estimate=SMALL_COST,
        name="attention_grads",
    )(core, xn1, mixed, *proj, *attn, *gain_sums)


def gather_blocks(part, dp_at, dp_count):
    span = part.shape[0]
    if span % 128 or dp_count != 4:
        whole = lax.all_gather(part, "dp", axis=0, tiled=True)
        return [whole], jnp.zeros((1,), jnp.int32)
    line = [(d, (d + 2) % 4) for d in range(4)]
    core = [(d, d ^ 1) for d in range(4)]
    across = lax.ppermute(part, "dp", line)
    beside = lax.ppermute(part, "dp", core)
    both = lax.ppermute(across, "dp", core)
    far = lax.rem(dp_at + 2, 4)
    owners = jnp.stack([dp_at, dp_at + 1 - 2 * lax.rem(dp_at, 2), far, far + 1 - 2 * lax.rem(far, 2)])
    return [part, beside, across, both], owners * span


def per_device(
    tokens,
    segments,
    routes,
    norm_one,
    norm_two,
    w_query,
    key_value_weight,
    w_out_attn,
    w_router,
    w_in,
    w_out,
    cotangent,
):
    micro_count, rows, width = tokens.shape
    micros = range(micro_count)
    peers = lax.axis_size("expert")
    dp_count = lax.axis_size("dp")
    local_experts = w_in.shape[0]
    experts = local_experts * peers
    capacity = rows // 4
    first_expert = lax.axis_index("expert") * local_experts
    q_width = w_query.shape[1]
    kv_width = key_value_weight.shape[1]
    proj_width = q_width + kv_width
    cosine_table, sine_values = rope_tables(rows, HEAD_SIZE)
    cos = jnp.concatenate([cosine_table, cosine_table], axis=1)
    sin = jnp.concatenate([-sine_values, sine_values], axis=1)
    order = ring_order(peers)
    spot = [order.index(dev) for dev in range(peers)]
    my_spot = jnp.array(spot, jnp.int32)[lax.axis_index("expert")]

    router_pad = jnp.zeros((w_router.shape[0], 126 - 2 * experts), jnp.bfloat16)
    first_weight = jnp.concatenate(
        [
            w_query,
            key_value_weight,
            w_router,
            w_router,
            norm_one[:, None],
            norm_two[:, None],
            router_pad,
        ],
        axis=1,
    )
    dp_at = lax.axis_index("dp").astype(jnp.int32)
    first_weights, starts = gather_blocks(first_weight, dp_at, dp_count)
    out_weights, _ = gather_blocks(w_out_attn, dp_at, dp_count)

    routes_rows = jnp.swapaxes(routes, 1, 2).reshape(-1, rows).astype(jnp.bfloat16)
    routes_rows = jnp.pad(
        routes_rows, ((0, EXTRA - routes_rows.shape[0]), (0, width - rows))
    )
    cot_rings = [
        RingGather(jnp.concatenate([cotangent[0], routes_rows], axis=0), peers, rows // 2),
        RingGather(cotangent[1], peers, rows // 2),
    ]
    steps = peers // 2
    for _ in range(steps - 2):
        for ring in cot_rings:
            ring.step()
    first_at = first_expert.astype(jnp.int32).reshape(1)
    seg_col, seg_row = segments[:, :, None], segments[:, None, :]
    xn1, query, keyval, mixed, gates, gates_pack, gains = attention_forward(
        starts, tokens, seg_col, seg_row, routes, cos, sin, first_weights
    )
    for ring in cot_rings:
        ring.step(mixed)
    first_whole = join_blocks(starts, [after(first_weights[0], gates)] + first_weights[1:])
    out_whole = join_blocks(starts, [after(out_weights[0], first_whole)] + out_weights[1:])
    hidden, xn2 = [], []
    for m in micros:
        out = block_call(
            hidden_kernel,
            [(mixed, (m,)), (tokens, (m,)), (gains,), (gates_pack, (m,))]
            + [(part,) for part in out_weights],
            [
                jax.ShapeDtypeStruct((rows, width), jnp.float32),
                jax.ShapeDtypeStruct((rows + EXTRA, width), jnp.bfloat16),
            ],
            "hidden_rows",
            prefetch=starts,
        )
        hidden.append(out[0])
        xn2.append(out[1])
    cot_rings[0].step(xn2[1])
    cot_rings[1].step(xn2[1], out_whole)
    routes_all = cot_rings[0].stack_rows(rows, micro_count * TOPK)[:, :, :rows]
    routes_all = routes_all.reshape(peers, micro_count, TOPK, rows)
    places = [
        slot_hits(routes_all[:, m], first_expert, local_experts, capacity)
        .astype(jnp.bfloat16)
        .reshape(peers, -1, rows)
        for m in micros
    ]
    every = list(range(peers))
    late = [steps - 1, steps, steps + 1]
    early = [k for k in every if k not in late]
    row_rings = [RingGather(xn2[m], peers, rows // 2) for m in micros]
    row_rings[0].step(*cot_rings[0].got, *cot_rings[1].got)
    groups = peers // GROUP

    class Experts:
        kept = [None] * 4

        def __init__(self, m, calls):
            self.m = m
            self.calls = calls
            self.per_call = local_experts // calls
            self.outs = [[None] * 3 for _ in range(groups)]
            self.found = {}

        def pick_grads(self):
            place = places[self.m]
            self.grads = pick_rows(first_at, place, cot_rings[self.m], every, False)
            return self.grads[0]

        def pick(self, distances):
            out = pick_rows(first_at, places[self.m], row_rings[self.m], distances, True)
            self.found.update(zip(distances, zip(out, out[len(distances) :])))
            self.rows = [self.found[k][0] for k in every if k in self.found]
            self.gate_slots = [self.found[k][1] for k in every if k in self.found]
            return out[0]

        def call(self, number, *earlier):
            for g in range(groups):
                span = slice(g * GROUP, (g + 1) * GROUP)
                here = self.rows[span]
                here[0] = after(here[0], *earlier) if earlier else here[0]
                done = expert_pass(
                    here,
                    self.grads[span],
                    self.gate_slots[span],
                    w_in,
                    w_out,
                    self.outs[g] + Experts.kept,
                    (self.m * groups + g, micro_count * groups),
                    number * self.per_call,
                    self.per_call,
                )
                self.outs[g], Experts.kept = list(done[:3]), list(done[3:])
            return done[2]

        def spread(self, spans, *earlier):
            place = places[self.m]
            place = after(place, *earlier) if earlier else place
            self.sums = None
            for g in range(groups):
                out = spread_rows(first_at, place, *self.outs[g], g, spans, self.sums)
                self.sums = out[0]
                if g == groups // 2:
                    far = out[1:]
            return far

    calls = 2
    first, second = Experts(0, calls), Experts(1, calls)
    ring, ring_next = row_rings
    while len(ring.from_left) < steps - 1:
        ring.step(*places)
    ring.step(first.pick_grads())
    ring.step(first.pick(early))
    first.pick(late)
    ring_next.step(*ring.got)
    token = first.call(0)
    for number in range(1, calls):
        got = ring_next.got
        ring_next.step(token)
        token = first.call(number, *got)
    block = rows + EXTRA
    got = ring_next.got
    while len(ring_next.from_left) < steps:
        ring_next.step(token)
    far = first.spread([(0, block), (block, rows)], *got)
    got = ring_next.got
    while ring_next.far is None:
        ring_next.step()
    ring_first = RingScatter(lambda k: first.sums[k], far, peers)
    ring_first.step(*got)
    second.pick_grads()
    second.pick(early)
    second.pick(late)
    token = second.call(0)
    for number in range(1, calls):
        ring_first.step(token)
        token = second.call(number, *ring_first.sent)
    half = rows // 2
    spans = [(0, half), (half, block - half), (block, half), (block + half, half)]
    far = second.spread(spans)
    ring_grads = RingScatter(lambda k: second.sums[k, :block], far[:2], peers)
    ring_results = RingScatter(lambda k: second.sums[k, block:], far[2:], peers)
    ring_grads.step()
    picked, grad_result, activated, grad_pre = Experts.kept
    place_at = jnp.stack([lax.rem(dp_at, 2), dp_at // 2])
    ring_grads.step()
    w_out_sum = weight_grads(
        after(activated, *ring_grads.sent, *ring_first.got), grad_result, 0, local_experts, None
    )
    def backward(m, pieces, *earlier):
        own, left, right = pieces
        return block_call(
            backward_kernel,
            [
                (after(own, *earlier), (0,), block),
                (left, (), block),
                (right, (), block),
                (cotangent, (m,)),
                (hidden[m],),
                (tokens, (m,)),
                (query, (m,)),
                (keyval, (m,)),
                (seg_col, (m,)),
                (seg_row, (m,)),
                (gates, (m,)),
                (gains,),
                (cos,),
                (sin,),
                (first_whole,),
                (out_whole,),
            ],
            [
                jax.ShapeDtypeStruct((rows, width), jnp.bfloat16),
                jax.ShapeDtypeStruct((rows, proj_width + 128), jnp.bfloat16),
                jax.ShapeDtypeStruct((rows, width), jnp.bfloat16),
                jax.ShapeDtypeStruct((8, width), jnp.float32),
            ],
            "attention_backward",
            [pltpu.VMEM((rows, q_width), jnp.bfloat16)],
        )

    half = max(1, local_experts // 2)
    got = second_got = ring_grads.got
    ring_grads.step(w_out_sum)
    picked = after(picked, w_out_sum, *got, *ring_grads.sent)
    while ring_first.at > 1:
        ring_first.step(w_out_sum)
    picked = after(picked, *ring_first.sent)
    w_in_sum = weight_grads(picked, grad_pre, 0, half, None)
    while ring_grads.at > 0:
        got = ring_grads.got
        ring_grads.step(w_in_sum)
    last = ring_first.got
    while ring_first.at > 0:
        ring_first.step(*ring_grads.sent)
    picked = after(picked, w_in_sum, *got, *ring_grads.sent, *ring_first.sent)
    w_in_sum = weight_grads(picked, grad_pre, half, local_experts - half, w_in_sum)
    got = last
    ring_results.step(*got)
    grad_w_out = lax.psum_scatter(
        after(w_out_sum, *second_got), "dp", scatter_dimension=1, tiled=True
    )
    grad_w_in = lax.psum_scatter(
        after(w_in_sum, *ring_grads.got), "dp", scatter_dimension=1, tiled=True
    )
    back_second = backward(1, (second.sums, ring_grads.left, ring_grads.right), w_in_sum)
    ring_results.step(back_second[3], *got)
    back_first = backward(
        0, (first.sums, ring_first.left, ring_first.right), *ring_results.sent
    )
    ring_results.step(back_first[3])
    grad_tokens, grad_proj, grad_attn, gain_sums = zip(back_first, back_second)
    mine, other = attention_grads(
        place_at, after(xn1, *ring_results.sent), mixed, grad_proj, grad_attn, gain_sums, dp_count
    )
    grads, grad_w_in, grad_w_out = reduce_packed(
        mine, other, my_spot, peers, dp_count, grad_w_in, grad_w_out, ring_results, (q_width, kv_width)
    )
    grad_query, grad_keyval, grad_small, grad_attn_out = grads
    wide = jnp.float32
    outputs = []
    for m, (own, ring, at) in enumerate(
        ((first.sums, ring_first, block), (second.sums, ring_results, 0))
    ):
        total = hidden[m] + own[0, block:].astype(wide)
        total = total + ring.left[at:].astype(wide) + ring.right[at:].astype(wide)
        outputs.append(total.astype(jnp.bfloat16))
    return (
        jnp.stack(outputs),
        jnp.stack(grad_tokens),
        grad_small[:, experts],
        grad_small[:, experts + 1],
        grad_query,
        grad_keyval,
        grad_attn_out,
        grad_small[:, :experts],
        grad_w_in,
        grad_w_out,
    )


def last_kernel(spot_ref, *refs):
    outs = refs[-4:]
    blocks = refs[:-4]
    peers = len(blocks) - 1
    piece = blocks[0].shape[0]
    for k, block_ref in enumerate(blocks):
        distance = k if k <= peers // 2 else k - 1
        spot = lax.rem(spot_ref[0] - distance + peers, peers)
        held = block_ref.shape[0]
        row = spot * piece + (held if k == peers // 2 + 1 else 0)
        at = 0
        for out_ref in outs:
            columns = out_ref.shape[1]
            out_ref[pl.ds(pl.multiple_of(row, 8), held), :] = block_ref[
                :, at : at + columns
            ].astype(jnp.float32)
            at += columns


def reduce_packed(mine, other, my_spot, peers, dp_count, grad_w_in, grad_w_out, ring_results, widths):
    lines, span, columns = mine.shape
    swap = [(d, d ^ 1) for d in range(dp_count)]
    while ring_results.at > 0:
        ring_results.step()
    total = add_rows(mine, lax.ppermute(other, "dp", swap))
    piece = span // peers
    total = total.reshape(lines, peers, piece, columns)

    def part(k):
        at = lax.rem(my_spot - k + peers, peers)
        return lax.dynamic_slice_in_dim(total, at, 1, axis=1).reshape(lines * piece, columns)

    half = lines * piece // 2
    farthest = part(peers // 2)
    ring = RingScatter(part, (farthest[:half], farthest[half:]), peers)
    ring.step()
    while ring.at > 0:
        ring.step()
    own, left, right = [held.astype(jnp.float32) for held in (part(0), ring.left, ring.right)]
    mine = (own + left + right).astype(jnp.bfloat16).reshape(lines, piece, columns)
    mine = after(mine, grad_w_in, grad_w_out)
    line = lax.axis_index("dp") // 2

    def for_line(at):
        return lax.dynamic_index_in_dim(mine, lax.rem(at, lines), 0, keepdims=False)

    share = for_line(line).astype(jnp.float32)
    for k in range(1, lines):
        pairs = [(d, (d + 2 * k) % dp_count) for d in range(dp_count)]
        share = share + lax.ppermute(for_line(line + k), "dp", pairs)
    gather = RingGather(share.astype(jnp.bfloat16), peers, piece // 2)
    gather.step()
    grad_w_out = grad_w_out.astype(jnp.float32)
    gather.step(grad_w_out)
    grad_w_in = grad_w_in.astype(jnp.float32)
    gather.step(grad_w_in, *ring_results.got)
    while gather.far is None:
        gather.step()
    blocks = gather.from_left + list(gather.far) + gather.from_right[:0:-1]
    columns = (widths[0], widths[1], 128, columns - sum(widths) - 128)
    if piece % 16 == 0:
        grads = block_call(
            last_kernel,
            [(block,) for block in blocks],
            [jax.ShapeDtypeStruct((span, count), jnp.float32) for count in columns],
            "last_rows",
            prefetch=my_spot.astype(jnp.int32).reshape(1),
        )
    else:
        far = jnp.concatenate(gather.far, axis=0)
        by_distance = jnp.stack(gather.from_left + [far] + gather.from_right[:0:-1])
        distance = lax.rem(my_spot - jnp.arange(peers, dtype=jnp.int32) + peers, peers)
        by_spot = jnp.take(by_distance, distance, axis=0).reshape(span, -1).astype(jnp.float32)
        edges = [sum(columns[:i]) for i in range(5)]
        grads = [by_spot[:, edges[i] : edges[i + 1]] for i in range(4)]
    return grads, grad_w_in, grad_w_out


def solution(mesh):
    return jax.shard_map(
        per_device,
        mesh=mesh,
        in_specs=(
            P(None, ("dp", "expert"), None),
            P(None, ("dp", "expert")),
            P(None, ("dp", "expert"), None),
            P("dp"),
            P("dp"),
            P("dp", None),
            P("dp", None),
            P("dp", None),
            P("dp", None),
            P("expert", None, None),
            P("expert", None, None),
            P(None, ("dp", "expert"), None),
        ),
        out_specs=(
            P(None, ("dp", "expert"), None),
            P(None, ("dp", "expert"), None),
            P("dp"),
            P("dp"),
            P("dp", None),
            P("dp", None),
            P("dp", None),
            P("dp", None),
            P("expert", "dp", None),
            P("expert", "dp", None),
        ),
        check_vma=False,
    )
```

profile of v0, /device:TPU:0, one launch (start us, length us, event | category | flops | bytes accessed | tf_op | source)
XLA Modules:
  0.0 782.7 jit_solution(5655353523218062740)
XLA Ops:
  22.1 15.9 %collective-permute-done.14.refs_1_ = bf16[256,1536]{1,0:T(8,128)(2,1)} collective-permute-done((bf16[256,1536]{1,0:T(8,128)(2,1)}, bf16[256,1536]{1,0:T(8,128)(2,1)}, u32[]{:S(2)}, u32[]{:S(2)}) %collective-permute-start.14) | collective-permute-done | bytes 786464 | tf_op jit(solution)/shard_map/ppermute | solution.py:289
  40.1 13.3 %collective-permute-done.1.refs_2_ = bf16[384,2176]{1,0:T(8,128)(2,1)} collective-permute-done((bf16[384,2176]{1,0:T(8,128)(2,1)S(1)}, bf16[384,2176]{1,0:T(8,128)(2,1)}, u32[]{:S(2)}, u32[]{:S(2)}) %collective-permute-start.1) | collective-permute-done | bytes 1671200 | tf_op jit(solution)/shard_map/ppermute | solution.py:764
  56.8 21.1 %collective-permute-done.4.refs_2_ = bf16[384,1536]{1,0:T(8,128)(2,1)} collective-permute-done((bf16[384,1536]{1,0:T(8,128)(2,1)S(1)}, bf16[384,1536]{1,0:T(8,128)(2,1)}, u32[]{:S(2)}, u32[]{:S(2)}) %collective-permute-start.4) | collective-permute-done | bytes 1179680 | tf_op jit(solution)/shard_map/ppermute | solution.py:764
  86.1 14.2 %attention_forward.1 = (bf16[2,256,1536]{2,1,0:T(8,128)(2,1)}, bf16[2,256,1536]{2,1,0:T(8,128)(2,1)}, bf16[2,256,512]{2,1,0:T(8,128)(2,1)}, bf16[2,256,1536]{2,1...) custom-call(s32[4]{0:T(128)} %add_multiply_fusion.starts_ref, ...), custom_call_target="tpu_custom_call" | custom-call | flops 1000000 | bytes 1000000 | tf_op jit(solution)/shard_map/attention_forward/pallas_call | solution.py:648
  100.3 15.7 %collective-permute-done.17.refs_7_ = bf16[256,1536]{1,0:T(8,128)(2,1)} collective-permute-done((bf16[256,1536]{1,0:T(8,128)(2,1)}, bf16[256,1536]{1,0:T(8,128)(2,1)}, u32[]{:S(2)}, u32[]{:S(2)}) %collective-permute-start.17) | collective-permute-done | bytes 786464 | tf_op jit(solution)/shard_map/ppermute | solution.py:289
  121.6 6.8 join_blocks.2.refs_0_
  129.4 6.8 hidden_rows.3
  177.6 10.6 %collective-permute-done.22.refs_2_.refs_3_ = bf16[272,1536]{1,0:T(8,128)(2,1)S(1)} collective-permute-done((bf16[272,1536]{1,0:T(8,128)(2,1)S(1)}, bf16[272,1536]{1,0:T(8,128)(2,1)S(1)}, u32[]{:S(2)}, u32[]{:S(2)}) %collective-permute-start.22) | collective-permute-done | bytes 835616 | tf_op jit(solution)/shard_map/ppermute | solution.py:289
  198.3 8.9 %collective-permute-done.24.refs_4_.refs_5_ = bf16[272,1536]{1,0:T(8,128)(2,1)} collective-permute-done((bf16[272,1536]{1,0:T(8,128)(2,1)S(1)}, bf16[272,1536]{1,0:T(8,128)(2,1)}, u32[]{:S(2)}, u32[]{:S(2)}) %collective-permute-start.24) | collective-permute-done | bytes 835616 | tf_op jit(solution)/shard_map/ppermute | solution.py:289
  217.4 11.8 %collective-permute-done.27.refs_5_.refs_6_ = bf16[272,1536]{1,0:T(8,128)(2,1)S(1)} collective-permute-done((bf16[272,1536]{1,0:T(8,128)(2,1)}, bf16[272,1536]{1,0:T(8,128)(2,1)S(1)}, u32[]{:S(2)}, u32[]{:S(2)}) %collective-permute-start.27) | collective-permute-done | bytes 835616 | tf_op jit(solution)/shard_map/ppermute | solution.py:289
  231.3 10.3 %collective-permute-done.28.refs_2_ = bf16[128,1536]{1,0:T(8,128)(2,1)S(1)} collective-permute-done((bf16[128,1536]{1,0:T(8,128)(2,1)S(1)}, bf16[128,1536]{1,0:T(8,128)(2,1)S(1)}, u32[]{:S(2)}, u32[]{:S(2)}) %collective-permute-start.28) | collective-permute-done | bytes 393248 | tf_op jit(solution)/shard_map/ppermute | solution.py:289
  248.5 24.3 %expert_pass.4 = (bf16[8,256,1536]{2,1,0:T(8,128)(2,1)}, bf16[8,256,1536]{2,1,0:T(8,128)(2,1)}, f32[4,512,1]{2,1,0:T(8,128)}, bf16[4,1024,1536]{2,1,0:T(8,128)(2...) custom-call(bf16[256,1536]{1,0:T(8,128)(2,1)} %get-tuple-element.287.refs_0_, ...), custom_call_target="tpu_custom_call" | custom-call | flops 1000000 | bytes 1000000 | tf_op jit(solution)/shard_map/expert_pass/pallas_call | solution.py:435
  275.1 24.3 %expert_pass.5 = (bf16[8,256,1536]{2,1,0:T(8,128)(2,1)}, bf16[8,256,1536]{2,1,0:T(8,128)(2,1)}, f32[4,512,1]{2,1,0:T(8,128)}, bf16[4,1024,1536]{2,1,0:T(8,128)(2...) custom-call(bf16[256,1536]{1,0:T(8,128)(2,1)} %get-tuple-element.287, ...), custom_call_target="tpu_custom_call", output_to_operand_aliasing={{0}: (26, {}), {1}: (27, {}), {2}: (28, {}), {3}: (29, {}),... | custom-call | flops 1000000 | bytes 1000000 | tf_op jit(solution)/shard_map/expert_pass/pallas_call | solution.py:435
  307.8 14.1 %spread_rows.2 = (bf16[8,528,1536]{2,1,0:T(8,128)(2,1)}, bf16[272,1536]{1,0:T(8,128)(2,1)}, bf16[256,1536]{1,0:T(8,128)(2,1)}) custom-call(s32[1]{0:T(128)} %bitcast.5.first_ref, bf16[8,256,256]{2,1,0:T(8,128)(2,1)} %get-tuple-element.286.place_ref, bf16[8,256,1536]{2,1,0:T(8,128)(2,1)} %get-tuple-element.294.rows_ref, ...), custom_call_target="tpu_custom_call" | custom-call | flops 1000000 | bytes 1000000 | tf_op jit(solution)/shard_map/spread_rows/pallas_call | solution.py:582
  333.9 9.5 %collective-permute-done.38.refs_2_ = bf16[128,1536]{1,0:T(8,128)(2,1)S(1)} collective-permute-done((bf16[128,1536]{1,0:T(8,128)(2,1)S(1)}, bf16[128,1536]{1,0:T(8,128)(2,1)S(1)}, u32[]{:S(2)}, u32[]{:S(2)}) %collective-permute-start.38) | collective-permute-done | bytes 393248 | tf_op jit(solution)/shard_map/ppermute | solution.py:289
  349.2 24.3 %expert_pass.6 = (bf16[8,256,1536]{2,1,0:T(8,128)(2,1)}, bf16[8,256,1536]{2,1,0:T(8,128)(2,1)}, f32[4,512,1]{2,1,0:T(8,128)}, bf16[4,1024,1536]{2,1,0:T(8,128)(2...) custom-call(bf16[256,1536]{1,0:T(8,128)(2,1)} %get-tuple-element.341, ...), custom_call_target="tpu_custom_call", output_to_operand_aliasing={{3}: (26, {}), {4}: (27, {}), {5}: (28, {}), {6}: (29, {})} | custom-call | flops 1000000 | bytes 1000000 | tf_op jit(solution)/shard_map/expert_pass/pallas_call | solution.py:435
  381.2 24.3 %expert_pass.7 = (bf16[8,256,1536]{2,1,0:T(8,128)(2,1)}, bf16[8,256,1536]{2,1,0:T(8,128)(2,1)}, f32[4,512,1]{2,1,0:T(8,128)}, bf16[4,1024,1536]{2,1,0:T(8,128)(2...) custom-call(bf16[256,1536]{1,0:T(8,128)(2,1)} %get-tuple-element.341, ...), custom_call_target="tpu_custom_call", output_to_operand_aliasing={{0}: (26, {}), {1}: (27, {}), {2}: (28, {}), {3}: (29, {}),... | custom-call | flops 1000000 | bytes 1000000 | tf_op jit(solution)/shard_map/expert_pass/pallas_call | solution.py:435
  405.5 14.1 %spread_rows.3 = (bf16[8,528,1536]{2,1,0:T(8,128)(2,1)}, bf16[128,1536]{1,0:T(8,128)(2,1)}, bf16[144,1536]{1,0:T(8,128)(2,1)}, bf16[128,1536]{1,0:T(8,128)(2,1)}, bf16[128,1536]{1,0:T(8,128)(2,1)}) custom-call(s32[1]{0:T(128)} %bitcast.5.first_ref, bf16[8,256,256]{2,1,0:T(8,128)(2,1)} %get-tuple-element.508.place_ref, ...), custom_call_target="tpu_custom_call" | custom-call | flops 1000000 | bytes 1000000 | tf_op jit(solution)/shard_map/spread_rows/pallas_call | solution.py:582
  424.9 8.8 %collective-permute-done.42 = bf16[128,1536]{1,0:T(8,128)(2,1)S(1)} collective-permute-done((bf16[128,1536]{1,0:T(8,128)(2,1)S(1)}, bf16[128,1536]{1,0:T(8,128)(2,1)S(1)}, u32[]{:S(2)}, u32[]{:S(2)}) %collective-permute-start.42) | collective-permute-done | bytes 393248 | tf_op jit(solution)/shard_map/ppermute | solution.py:289
  440.0 15.1 %weight_grads.3 = bf16[4,768,1536]{2,1,0:T(8,128)(2,1)} custom-call(bf16[4,1024,768]{2,1,0:T(8,128)(2,1)} %get-tuple-element.359.left_ref, bf16[4,1024,1536]{2,1,0:T(8,128)(2,1)} %get-tuple-element.360.right_ref), custom_call_target="tpu_custom_call" | custom-call | flops 1000000 | bytes 1000000 | tf_op jit(solution)/shard_map/weight_grads/pallas_call | solution.py:613
  473.5 15.4 %weight_grads.4.refs_0_ = bf16[4,1536,1536]{2,1,0:T(8,128)(2,1)} custom-call(bf16[4,1024,1536]{2,1,0:T(8,128)(2,1)} %get-tuple-element.388.left_ref, bf16[4,1024,1536]{2,1,0:T(8,128)(2,1)} %get-tuple-element.372.right_ref), custom_call_target="tpu_custom_call" | custom-call | flops 1000000 | bytes 1000000 | tf_op jit(solution)/shard_map/weight_grads/pallas_call | solution.py:613
  488.8 23.5 %collective-permute-done.48 = bf16[272,1536]{1,0:T(8,128)(2,1)} collective-permute-done((bf16[272,1536]{1,0:T(8,128)(2,1)}, bf16[272,1536]{1,0:T(8,128)(2,1)}, u32[]{:S(2)}, u32[]{:S(2)}) %collective-permute-start.48) | collective-permute-done | bytes 835616 | tf_op jit(solution)/shard_map/ppermute | solution.py:289
  522.6 14.9 %weight_grads.5 = bf16[4,1536,1536]{2,1,0:T(8,128)(2,1)} custom-call(bf16[4,1024,1536]{2,1,0:T(8,128)(2,1)} %get-tuple-element.388.left_ref, bf16[4,1024,1536]{2,1,0:T(8,128)(2,1)} %get-tuple-element.372.right_ref, bf16[4,1536,1536]{2,1,0:T(8,128)(2,1)} %weight_grads.4.refs_0_), custom_call_target="tpu_custom_call", output_to_operand_aliasing={{}: (2, {})} | custom-call | flops 1000000 | bytes 1000000 | tf_op jit(solution)/shard_map/weight_grads/pallas_call | solution.py:613
  542.6 20.3 %attention_backward.2 = (bf16[256,1536]{1,0:T(8,128)(2,1)}, bf16[256,2176]{1,0:T(8,128)(2,1)}, bf16[256,1536]{1,0:T(8,128)(2,1)}, f32[8,1536]{1,0:T(8,128)}) custom-call(bf16[8,528,1536]{2,1,0:T(8,128)(2,1)} %get-tuple-element.389.own_ref, bf16[272,1536]{1,0:T(8,128)(2,1)} %collective-permute-done.54.left_ref, ...), custom_call_target="tpu_custom_call" | custom-call | flops 1000000 | bytes 1000000 | tf_op jit(solution)/shard_map/attention_backward/pallas_call | solution.py:470
  576.1 18.3 %attention_backward.3 = (bf16[256,1536]{1,0:T(8,128)(2,1)}, bf16[256,2176]{1,0:T(8,128)(2,1)}, bf16[256,1536]{1,0:T(8,128)(2,1)}, f32[8,1536]{1,0:T(8,128)}) custom-call(bf16[8,528,1536]{2,1,0:T(8,128)(2,1)} %get-tuple-element.397.own_ref, bf16[528,1536]{1,0:T(8,128)(2,1)} %copy-done.11, bf16[528,1536]{1,0:T(8,128)(2,1)} %copy-done.12, ...), custom_call_target="tpu_custom_call" | custom-call | flops 1000000 | bytes 1000000 | tf_op jit(solution)/shard_map/attention_backward/pallas_call | solution.py:470
  596.6 13.0 %attention_grads.1 = (bf16[2,384,3712]{2,1,0:T(8,128)(2,1)}, bf16[2,384,3712]{2,1,0:T(8,128)(2,1)}) custom-call(s32[2]{0:T(128)} %pad_add_fusion.core_ref, bf16[2,256,1536]{2,1,0:T(8,128)(2,1)} %get-tuple-element.408.xn1, bf16[2,256,1536]{2,1,0:T(8,128)(2,1)} %get-tuple-element.224.mixed_ref.mixed, bf16[256,2176]{1,0:T(8,128)(2,1)} %get-tuple-element.409.refs_0_, ...), custom_call_target="tpu_custom_call" | custom-call | flops 1000000 | bytes 1000000 | tf_op jit(solution)/shard_map/attention_grads/pallas_call | solution.py:739
  612.2 7.1 collective-permute-done.62
  627.2 8.5 %collective-permute-done.63 = bf16[48,3712]{1,0:T(8,128)(2,1)S(1)} collective-permute-done((bf16[48,3712]{1,0:T(8,128)(2,1)S(1)}, bf16[48,3712]{1,0:T(8,128)(2,1)S(1)}, u32[]{:S(2)}, u32[]{:S(2)}) %collective-permute-start.63) | collective-permute-done | bytes 356384 | tf_op jit(solution)/shard_map/ppermute | solution.py:289
  645.7 9.7 %collective-permute-done.66 = bf16[96,3712]{1,0:T(8,128)(2,1)} collective-permute-done((bf16[96,3712]{1,0:T(8,128)(2,1)}, bf16[96,3712]{1,0:T(8,128)(2,1)}, u32[]{:S(2)}, u32[]{:S(2)}) %collective-permute-start.66) | collective-permute-done | bytes 712736 | tf_op jit(solution)/shard_map/ppermute | solution.py:289
  663.7 14.2 %collective-permute-done.68 = bf16[96,3712]{1,0:T(8,128)(2,1)S(1)} collective-permute-done((bf16[96,3712]{1,0:T(8,128)(2,1)S(1)}, bf16[96,3712]{1,0:T(8,128)(2,1)S(1)}, u32[]{:S(2)}, u32[]{:S(2)}) %collective-permute-start.68) | collective-permute-done | bytes 712736 | tf_op jit(solution)/shard_map/ppermute | solution.py:289
  681.8 13.3 %collective-permute-done.69 = bf16[96,3712]{1,0:T(8,128)(2,1)} collective-permute-done((bf16[96,3712]{1,0:T(8,128)(2,1)}, bf16[96,3712]{1,0:T(8,128)(2,1)}, u32[]{:S(2)}, u32[]{:S(2)}) %collective-permute-start.69) | collective-permute-done | bytes 712736 | tf_op jit(solution)/shard_map/ppermute | solution.py:289
  708.0 10.6 %collective-permute-done.58 = bf16[256,1536]{1,0:T(8,128)(2,1)S(1)} collective-permute-done((bf16[256,1536]{1,0:T(8,128)(2,1)S(1)}, bf16[256,1536]{1,0:T(8,128)(2,1)S(1)}, u32[]{:S(2)}, u32[]{:S(2)}) %collective-permute-start.58) | collective-permute-done | bytes 786464 | tf_op jit(solution)/shard_map/ppermute | solution.py:289
  (351 shorter events, 299.4 us)
Async XLA Ops:
  7.2 690.1 %reduce-scatter.5.cloned.1.call-start = ((), (), s32[]{:S(2)}) async-start(), calls=%async_computation.3 | async-start | bytes 11796480 | tf_op jit(solution)/shard_map/reduce_scatter | solution.py:1019
  13.0 40.5 %collective-permute-start.1 = (bf16[384,2176]{1,0:T(8,128)(2,1)S(1)}, bf16[384,2176]{1,0:T(8,128)(2,1)}, u32[]{:S(2)}, u32[]{:S(2)}) collective-permute-start(bf16[384,2176]{1,0:T(8,128)(2,1)S(1)} %concatenate.38.refs_0_), channel_id=1, source_target_pairs={{0,16},{8,24},{16,0},{24,8},{1,17},{9,25},{17,1},{25,9},{2,18},{10... | collective-permute-start | bytes 5013512 | tf_op jit(solution)/shard_map/ppermute | solution.py:764
  20.5 34.0 %collective-permute-start.6 = (bf16[272,1536]{1,0:T(8,128)(2,1)S(1)}, bf16[272,1536]{1,0:T(8,128)(2,1)}, u32[]{:S(2)}, u32[]{:S(2)}) collective-permute-start(bf16[272,1536]{1,0:T(8,128)(2,1)S(1)} %pad_maximum_fusion.4.refs_0_), channel_id=1, source_target_pairs={{0,2},{2,4},{4,6},{6,7},{7,5},{5,3},{3,1},{1,0},{8,10},{10,12},{12... | collective-permute-start | bytes 2506760 | tf_op jit(solution)/shard_map/ppermute | solution.py:289
  22.1 57.8 %collective-permute-start = (bf16[384,2176]{1,0:T(8,128)(2,1)S(1)}, bf16[384,2176]{1,0:T(8,128)(2,1)}, u32[]{:S(2)}, u32[]{:S(2)}) collective-permute-start(bf16[384,2176]{1,0:T(8,128)(2,1)S(1)} %concatenate.38.refs_0_), channel_id=1, source_target_pairs={{0,8},{8,0},{16,24},{24,16},{1,9},{9,1},{17,25},{25,17},{2,10},{10... | collective-permute-start | bytes 5013512 | tf_op jit(solution)/shard_map/ppermute | solution.py:765
  38.0 39.9 %collective-permute-start.4 = (bf16[384,1536]{1,0:T(8,128)(2,1)S(1)}, bf16[384,1536]{1,0:T(8,128)(2,1)}, u32[]{:S(2)}, u32[]{:S(2)}) collective-permute-start(bf16[384,1536]{1,0:T(8,128)(2,1)S(1)} %copy-done.3), channel_id=1, source_target_pairs={{0,16},{8,24},{16,0},{24,8},{1,17},{9,25},{17,1},{25,9},{2,18},{10... | collective-permute-start | bytes 3538952 | tf_op jit(solution)/shard_map/ppermute | solution.py:764
  53.4 29.7 %collective-permute-start.2 = (bf16[384,2176]{1,0:T(8,128)(2,1)}, bf16[384,2176]{1,0:T(8,128)(2,1)}, u32[]{:S(2)}, u32[]{:S(2)}) collective-permute-start(bf16[384,2176]{1,0:T(8,128)(2,1)} %collective-permute-done.1.refs_2_), channel_id=1, source_target_pairs={{0,8},{8,0},{16,24},{24,16},{1,9},{9,1},{17,25},{25,17},{2,10},{10... | collective-permute-start | bytes 5013512 | tf_op jit(solution)/shard_map/ppermute | solution.py:766
  56.8 61.8 %collective-permute-start.3 = (bf16[384,1536]{1,0:T(8,128)(2,1)S(1)}, bf16[384,1536]{1,0:T(8,128)(2,1)}, u32[]{:S(2)}, u32[]{:S(2)}) collective-permute-start(bf16[384,1536]{1,0:T(8,128)(2,1)S(1)} %copy-done.3), channel_id=1, source_target_pairs={{0,8},{8,0},{16,24},{24,16},{1,9},{9,1},{17,25},{25,17},{2,10},{10... | collective-permute-start | bytes 3538952 | tf_op jit(solution)/shard_map/ppermute | solution.py:765
  77.9 39.7 %collective-permute-start.8 = (bf16[272,1536]{1,0:T(8,128)(2,1)}, bf16[272,1536]{1,0:T(8,128)(2,1)}, u32[]{:S(2)}, u32[]{:S(2)}) collective-permute-start(bf16[272,1536]{1,0:T(8,128)(2,1)} %collective-permute-done.6.refs_1_), channel_id=1, source_target_pairs={{0,2},{2,4},{4,6},{6,7},{7,5},{5,3},{3,1},{1,0},{8,10},{10,12},{12... | collective-permute-start | bytes 2506760 | tf_op jit(solution)/shard_map/ppermute | solution.py:289
  79.7 38.4 %collective-permute-start.9 = (bf16[272,1536]{1,0:T(8,128)(2,1)}, bf16[272,1536]{1,0:T(8,128)(2,1)}, u32[]{:S(2)}, u32[]{:S(2)}) collective-permute-start(bf16[272,1536]{1,0:T(8,128)(2,1)} %collective-permute-done.7.refs_8_), channel_id=1, source_target_pairs={{0,1},{2,0},{4,2},{6,4},{7,6},{5,7},{3,5},{1,3},{8,9},{10,8},{12,1... | collective-permute-start | bytes 2506760 | tf_op jit(solution)/shard_map/ppermute | solution.py:289
  79.9 36.1 %collective-permute-start.17 = (bf16[256,1536]{1,0:T(8,128)(2,1)}, bf16[256,1536]{1,0:T(8,128)(2,1)}, u32[]{:S(2)}, u32[]{:S(2)}) collective-permute-start(bf16[256,1536]{1,0:T(8,128)(2,1)} %collective-permute-done.15.refs_8_), channel_id=1, source_target_pairs={{0,1},{2,0},{4,2},{6,4},{7,6},{5,7},{3,5},{1,3},{8,9},{10,8},{12,1... | collective-permute-start | bytes 2359304 | tf_op jit(solution)/shard_map/ppermute | solution.py:289
  83.1 45.3 %collective-permute-start.5 = (bf16[384,1536]{1,0:T(8,128)(2,1)}, bf16[384,1536]{1,0:T(8,128)(2,1)S(1)}, u32[]{:S(2)}, u32[]{:S(2)}) collective-permute-start(bf16[384,1536]{1,0:T(8,128)(2,1)} %collective-permute-done.4.refs_2_), channel_id=1, source_target_pairs={{0,8},{8,0},{16,24},{24,16},{1,9},{9,1},{17,25},{25,17},{2,10},{10... | collective-permute-start | bytes 3538952 | tf_op jit(solution)/shard_map/ppermute | solution.py:766
  116.0 32.5 %collective-permute-start.18 = (bf16[256,1536]{1,0:T(8,128)(2,1)}, bf16[256,1536]{1,0:T(8,128)(2,1)}, u32[]{:S(2)}, u32[]{:S(2)}) collective-permute-start(bf16[256,1536]{1,0:T(8,128)(2,1)} %collective-permute-done.16.refs_2_), channel_id=1, source_target_pairs={{0,2},{2,4},{4,6},{6,7},{7,5},{5,3},{3,1},{1,0},{8,10},{10,12},{12... | collective-permute-start | bytes 2359304 | tf_op jit(solution)/shard_map/ppermute | solution.py:289
  117.6 32.1 %collective-permute-start.19 = (bf16[256,1536]{1,0:T(8,128)(2,1)}, bf16[256,1536]{1,0:T(8,128)(2,1)}, u32[]{:S(2)}, u32[]{:S(2)}) collective-permute-start(bf16[256,1536]{1,0:T(8,128)(2,1)} %collective-permute-done.17.refs_7_), channel_id=1, source_target_pairs={{0,1},{2,0},{4,2},{6,4},{7,6},{5,7},{3,5},{1,3},{8,9},{10,8},{12,1... | collective-permute-start | bytes 2359304 | tf_op jit(solution)/shard_map/ppermute | solution.py:289
  118.1 35.9 %collective-permute-start.11 = (bf16[272,1536]{1,0:T(8,128)(2,1)}, bf16[272,1536]{1,0:T(8,128)(2,1)}, u32[]{:S(2)}, u32[]{:S(2)}) collective-permute-start(bf16[272,1536]{1,0:T(8,128)(2,1)} %collective-permute-done.9.refs_7_), channel_id=1, source_target_pairs={{0,1},{2,0},{4,2},{6,4},{7,6},{5,7},{3,5},{1,3},{8,9},{10,8},{12,1... | collective-permute-start | bytes 2506760 | tf_op jit(solution)/shard_map/ppermute | solution.py:289
  118.6 36.4 %collective-permute-start.10 = (bf16[272,1536]{1,0:T(8,128)(2,1)}, bf16[272,1536]{1,0:T(8,128)(2,1)S(1)}, u32[]{:S(2)}, u32[]{:S(2)}) collective-permute-start(bf16[272,1536]{1,0:T(8,128)(2,1)} %collective-permute-done.8.refs_2_), channel_id=1, source_target_pairs={{0,2},{2,4},{4,6},{6,7},{7,5},{5,3},{3,1},{1,0},{8,10},{10,12},{12... | collective-permute-start | bytes 2506760 | tf_op jit(solution)/shard_map/ppermute | solution.py:289
  242.4 30.5 %collective-permute-start.30 = (bf16[272,1536]{1,0:T(8,128)(2,1)S(1)}, bf16[272,1536]{1,0:T(8,128)(2,1)S(1)}, u32[]{:S(2)}, u32[]{:S(2)}) collective-permute-start(bf16[272,1536]{1,0:T(8,128)(2,1)S(1)} %copy-done.13), channel_id=1, source_target_pairs={{0,2},{2,4},{4,6},{6,7},{7,5},{5,3},{3,1},{1,0},{8,10},{10,12},{12... | collective-permute-start | bytes 2506760 | tf_op jit(solution)/shard_map/ppermute | solution.py:289
  244.1 28.7 %collective-permute-start.31 = (bf16[272,1536]{1,0:T(8,128)(2,1)S(1)}, bf16[272,1536]{1,0:T(8,128)(2,1)}, u32[]{:S(2)}, u32[]{:S(2)}) collective-permute-start(bf16[272,1536]{1,0:T(8,128)(2,1)S(1)} %copy-done.13), channel_id=1, source_target_pairs={{0,1},{2,0},{4,2},{6,4},{7,6},{5,7},{3,5},{1,3},{8,9},{10,8},{12,1... | collective-permute-start | bytes 2506760 | tf_op jit(solution)/shard_map/ppermute | solution.py:289
  299.5 27.3 %collective-permute-start.35 = (bf16[272,1536]{1,0:T(8,128)(2,1)}, bf16[272,1536]{1,0:T(8,128)(2,1)S(1)}, u32[]{:S(2)}, u32[]{:S(2)}) collective-permute-start(bf16[272,1536]{1,0:T(8,128)(2,1)} %collective-permute-done.33.refs_6_.refs_7_), channel_id=1, source_target_pairs={{0,1},{2,0},{4,2},{6,4},{7,6},{5,7},{3,5},{1,3},{8,9},{10,8},{12,1... | collective-permute-start | bytes 2506760 | tf_op jit(solution)/shard_map/ppermute | solution.py:289
  299.6 27.2 %collective-permute-start.34 = (bf16[272,1536]{1,0:T(8,128)(2,1)S(1)}, bf16[272,1536]{1,0:T(8,128)(2,1)S(1)}, u32[]{:S(2)}, u32[]{:S(2)}) collective-permute-start(bf16[272,1536]{1,0:T(8,128)(2,1)S(1)} %collective-permute-done.32.refs_4_.refs_5_), channel_id=1, source_target_pairs={{0,2},{2,4},{4,6},{6,7},{7,5},{5,3},{3,1},{1,0},{8,10},{10,12},{12... | collective-permute-start | bytes 2506760 | tf_op jit(solution)/shard_map/ppermute | solution.py:289
  326.9 46.7 %collective-permute-start.36 = (bf16[272,1536]{1,0:T(8,128)(2,1)}, bf16[272,1536]{1,0:T(8,128)(2,1)S(1)}, u32[]{:S(2)}, u32[]{:S(2)}) collective-permute-start(bf16[272,1536]{1,0:T(8,128)(2,1)} %get-tuple-element.304), channel_id=1, source_target_pairs={{0,1},{2,0},{4,2},{6,4},{7,6},{5,7},{3,5},{1,3},{8,9},{10,8},{12,1... | collective-permute-start | bytes 2506760 | tf_op jit(solution)/shard_map/ppermute | solution.py:289
  327.0 46.5 %collective-permute-start.37 = (bf16[256,1536]{1,0:T(8,128)(2,1)}, bf16[256,1536]{1,0:T(8,128)(2,1)}, u32[]{:S(2)}, u32[]{:S(2)}) collective-permute-start(bf16[256,1536]{1,0:T(8,128)(2,1)} %get-tuple-element.305), channel_id=1, source_target_pairs={{0,2},{2,4},{4,6},{6,7},{7,5},{5,3},{3,1},{1,0},{8,10},{10,12},{12... | collective-permute-start | bytes 2359304 | tf_op jit(solution)/shard_map/ppermute | solution.py:289
  379.0 61.0 %collective-permute-start.40 = (bf16[528,1536]{1,0:T(8,128)(2,1)}, bf16[528,1536]{1,0:T(8,128)(2,1)S(1)}, u32[]{:S(2)}, u32[]{:S(2)}) collective-permute-start(bf16[528,1536]{1,0:T(8,128)(2,1)} %pad_maximum_fusion), channel_id=1, source_target_pairs={{0,1},{2,0},{4,2},{6,4},{7,6},{5,7},{3,5},{1,3},{8,9},{10,8},{12,1... | collective-permute-start | bytes 4866056 | tf_op jit(solution)/shard_map/ppermute | solution.py:289
  379.2 60.7 %collective-permute-start.41 = (bf16[528,1536]{1,0:T(8,128)(2,1)}, bf16[528,1536]{1,0:T(8,128)(2,1)S(1)}, u32[]{:S(2)}, u32[]{:S(2)}) collective-permute-start(bf16[528,1536]{1,0:T(8,128)(2,1)} %pad_maximum_fusion.1), channel_id=1, source_target_pairs={{0,2},{2,4},{4,6},{6,7},{7,5},{5,3},{3,1},{1,0},{8,10},{10,12},{12... | collective-permute-start | bytes 4866056 | tf_op jit(solution)/shard_map/ppermute | solution.py:289
  460.3 237.0 %reduce-scatter.3.cloned.1.call-start = ((), (), s32[]{:S(2)}) async-start(), calls=%async_computation.2 | async-start | bytes 23592960 | tf_op jit(solution)/shard_map/reduce_scatter | solution.py:1022
  464.8 53.3 %collective-permute-start.44 = (bf16[528,1536]{1,0:T(8,128)(2,1)}, bf16[528,1536]{1,0:T(8,128)(2,1)S(1)}, u32[]{:S(2)}, u32[]{:S(2)}) collective-permute-start(bf16[528,1536]{1,0:T(8,128)(2,1)} %get-tuple-element.363), channel_id=1, source_target_pairs={{0,1},{2,0},{4,2},{6,4},{7,6},{5,7},{3,5},{1,3},{8,9},{10,8},{12,1... | collective-permute-start | bytes 4866056 | tf_op jit(solution)/shard_map/ppermute | solution.py:289
  464.9 53.2 %collective-permute-start.45 = (bf16[528,1536]{1,0:T(8,128)(2,1)}, bf16[528,1536]{1,0:T(8,128)(2,1)S(1)}, u32[]{:S(2)}, u32[]{:S(2)}) collective-permute-start(bf16[528,1536]{1,0:T(8,128)(2,1)} %get-tuple-element.364), channel_id=1, source_target_pairs={{0,2},{2,4},{4,6},{6,7},{7,5},{5,3},{3,1},{1,0},{8,10},{10,12},{12... | collective-permute-start | bytes 4866056 | tf_op jit(solution)/shard_map/ppermute | solution.py:289
  471.1 41.3 %collective-permute-start.48 = (bf16[272,1536]{1,0:T(8,128)(2,1)}, bf16[272,1536]{1,0:T(8,128)(2,1)}, u32[]{:S(2)}, u32[]{:S(2)}) collective-permute-start(bf16[272,1536]{1,0:T(8,128)(2,1)} %get-tuple-element.367), channel_id=1, source_target_pairs={{0,1},{2,0},{4,2},{6,4},{7,6},{5,7},{3,5},{1,3},{8,9},{10,8},{12,1... | collective-permute-start | bytes 2506760 | tf_op jit(solution)/shard_map/ppermute | solution.py:289
  471.1 41.6 %collective-permute-start.49 = (bf16[272,1536]{1,0:T(8,128)(2,1)S(1)}, bf16[272,1536]{1,0:T(8,128)(2,1)}, u32[]{:S(2)}, u32[]{:S(2)}) collective-permute-start(bf16[272,1536]{1,0:T(8,128)(2,1)S(1)} %get-tuple-element.368), channel_id=1, source_target_pairs={{0,2},{2,4},{4,6},{6,7},{7,5},{5,3},{3,1},{1,0},{8,10},{10,12},{12... | collective-permute-start | bytes 2506760 | tf_op jit(solution)/shard_map/ppermute | solution.py:289
  540.6 33.1 %collective-permute-start.50 = (bf16[528,1536]{1,0:T(8,128)(2,1)}, bf16[528,1536]{1,0:T(8,128)(2,1)S(1)}, u32[]{:S(2)}, u32[]{:S(2)}) collective-permute-start(bf16[528,1536]{1,0:T(8,128)(2,1)} %get-tuple-element.379), channel_id=1, source_target_pairs={{0,1},{2,0},{4,2},{6,4},{7,6},{5,7},{3,5},{1,3},{8,9},{10,8},{12,1... | collective-permute-start | bytes 4866056 | tf_op jit(solution)/shard_map/ppermute | solution.py:289
  541.6 33.3 %collective-permute-start.51 = (bf16[528,1536]{1,0:T(8,128)(2,1)}, bf16[528,1536]{1,0:T(8,128)(2,1)S(1)}, u32[]{:S(2)}, u32[]{:S(2)}) collective-permute-start(bf16[528,1536]{1,0:T(8,128)(2,1)} %get-tuple-element.380), channel_id=1, source_target_pairs={{0,2},{2,4},{4,6},{6,7},{7,5},{5,3},{3,1},{1,0},{8,10},{10,12},{12... | collective-permute-start | bytes 4866056 | tf_op jit(solution)/shard_map/ppermute | solution.py:289
  566.7 27.7 %collective-permute-start.56 = (bf16[256,1536]{1,0:T(8,128)(2,1)}, bf16[256,1536]{1,0:T(8,128)(2,1)}, u32[]{:S(2)}, u32[]{:S(2)}) collective-permute-start(bf16[256,1536]{1,0:T(8,128)(2,1)} %pad_maximum_fusion.7), channel_id=1, source_target_pairs={{0,1},{2,0},{4,2},{6,4},{7,6},{5,7},{3,5},{1,3},{8,9},{10,8},{12,1... | collective-permute-start | bytes 2359304 | tf_op jit(solution)/shard_map/ppermute | solution.py:289
  567.1 27.3 %collective-permute-start.57 = (bf16[256,1536]{1,0:T(8,128)(2,1)}, bf16[256,1536]{1,0:T(8,128)(2,1)}, u32[]{:S(2)}, u32[]{:S(2)}) collective-permute-start(bf16[256,1536]{1,0:T(8,128)(2,1)} %pad_maximum_fusion.8), channel_id=1, source_target_pairs={{0,2},{2,4},{4,6},{6,7},{7,5},{5,3},{3,1},{1,0},{8,10},{10,12},{12... | collective-permute-start | bytes 2359304 | tf_op jit(solution)/shard_map/ppermute | solution.py:289
  (99 other events, 1356.0 us)
Sparse Core Ops, SparseCore 0:
  460.4 77.5 reduce-scatter.4
  540.6 139.4 reduce-scatter.2
where the time goes:
time: 793 us; the launch traced here: 783 us
  Pallas kernels  298 us (38%)
  waiting for transfers between devices  282 us (36%)
  starting transfers between devices  82.5 us (10%)
  other arithmetic  66.4 us (8%)
  local copies, waits for them, and re-layouts  33.3 us (4%)
  between operations  20.3 us (3%)
    ppermute x72, waiting for transfers between devices, ring_step(): return lax.ppermute(part, 'expert', pairs)  236 us
    pallas_call x4, Pallas kernels, expert_pass(): pl.pallas_call(functools.partial(expert_kernel, sources), grid=(count,),...  97.3 us
    pallas_call x11, Pallas kernels, block_call(): pl.pallas_call(kernel, grid_spec=pltpu.PrefetchScalarGridSpec(num_scalar_...  87.6 us
    ppermute x72, starting transfers between devices, ring_step(): return lax.ppermute(part, 'expert', pairs)  78.3 us
    pallas_call x3, Pallas kernels, weight_grads(): pl.pallas_call(weight_grad_kernel, grid=(count, height // tile), in_specs...  45.4 us
    convert_element_type x17, other arithmetic, add_rows(): (left.astype(jnp.float32) + right.astype(jnp.float32)).astype(jnp.bfloat16)  36.2 us
    ppermute x2, waiting for transfers between devices, gather_blocks(): across = lax.ppermute(part, 'dp', line)  34.4 us
    pallas_call x2, Pallas kernels, spread_rows(): pl.pallas_call(functools.partial(spread_kernel, sources // 2 - base, span...  28.2 us
  transfers between devices with their start and end apart: 82, of which 48 were waited for; matrix products, arithmetic and copies ran while one was open for 10% of the time, Pallas kernels for 37%

commit v1 on v0

--- a/solution.py
+++ b/solution.py
@@ -758,15 +758,19 @@
     span = part.shape[0]
     if span % 128 or dp_count != 4:
         whole = lax.all_gather(part, "dp", axis=0, tiled=True)
-        return [whole], jnp.zeros((1,), jnp.int32)
+        return lambda *earlier: [whole], jnp.zeros((1,), jnp.int32)
     line = [(d, (d + 2) % 4) for d in range(4)]
     core = [(d, d ^ 1) for d in range(4)]
     across = lax.ppermute(part, "dp", line)
     beside = lax.ppermute(part, "dp", core)
-    both = lax.ppermute(across, "dp", core)
     far = lax.rem(dp_at + 2, 4)
     owners = jnp.stack([dp_at, dp_at + 1 - 2 * lax.rem(dp_at, 2), far, far + 1 - 2 * lax.rem(far, 2)])
-    return [part, beside, across, both], owners * span
+
+    def blocks(*earlier):
+        moved = after(across, *earlier) if earlier else across
+        return [part, beside, moved, lax.ppermute(moved, "dp", core)]
+
+    return blocks, owners * span
 
 
 def per_device(
@@ -827,9 +831,11 @@
         RingGather(cotangent[1], peers, rows // 2),
     ]
     steps = peers // 2
-    for _ in range(steps - 2):
+    for at in range(steps - 2):
         for ring in cot_rings:
             ring.step()
+        if at == 0:
+            first_weights = first_weights(*cot_rings[0].got, *cot_rings[1].got)
     first_at = first_expert.astype(jnp.int32).reshape(1)
     seg_col, seg_row = segments[:, :, None], segments[:, None, :]
     xn1, query, keyval, mixed, gates, gates_pack, gains = attention_forward(
@@ -837,8 +843,7 @@
     )
     for ring in cot_rings:
         ring.step(mixed)
-    first_whole = join_blocks(starts, [after(first_weights[0], gates)] + first_weights[1:])
-    out_whole = join_blocks(starts, [after(out_weights[0], first_whole)] + out_weights[1:])
+    out_weights = out_weights(mixed)
     hidden, xn2 = [], []
     for m in micros:
         out = block_call(
@@ -854,8 +859,10 @@
         )
         hidden.append(out[0])
         xn2.append(out[1])
-    cot_rings[0].step(xn2[1])
-    cot_rings[1].step(xn2[1], out_whole)
+    for ring in cot_rings:
+        ring.step()
+    first_whole = join_blocks(starts, [after(first_weights[0], xn2[1])] + first_weights[1:])
+    out_whole = join_blocks(starts, [after(out_weights[0], first_whole)] + out_weights[1:])
     routes_all = cot_rings[0].stack_rows(rows, micro_count * TOPK)[:, :, :rows]
     routes_all = routes_all.reshape(peers, micro_count, TOPK, rows)
     places = [
@@ -927,9 +934,10 @@
     first, second = Experts(0, calls), Experts(1, calls)
     ring, ring_next = row_rings
     while len(ring.from_left) < steps - 1:
-        ring.step(*places)
+        ring.step(*places, out_whole)
     ring.step(first.pick_grads())
     ring.step(first.pick(early))
+    places[0] = after(places[0], second.pick_grads())
     first.pick(late)
     ring_next.step(*ring.got)
     token = first.call(0)
@@ -947,7 +955,6 @@
         ring_next.step()
     ring_first = RingScatter(lambda k: first.sums[k], far, peers)
     ring_first.step(*got)
-    second.pick_grads()
     second.pick(early)
     second.pick(late)
     token = second.call(0)
@@ -960,11 +967,14 @@
     ring_grads = RingScatter(lambda k: second.sums[k, :block], far[:2], peers)
     ring_results = RingScatter(lambda k: second.sums[k, block:], far[2:], peers)
     ring_grads.step()
+    got = ring_first.got
+    while ring_first.at > 1:
+        ring_first.step(second.sums)
     picked, grad_result, activated, grad_pre = Experts.kept
     place_at = jnp.stack([lax.rem(dp_at, 2), dp_at // 2])
     ring_grads.step()
     w_out_sum = weight_grads(
-        after(activated, *ring_grads.sent, *ring_first.got), grad_result, 0, local_experts, None
+        after(activated, *ring_grads.sent, *ring_first.sent), grad_result, 0, local_experts, None
     )
     def backward(m, pieces, *earlier):
         own, left, right = pieces
@@ -1002,9 +1012,6 @@
     got = second_got = ring_grads.got
     ring_grads.step(w_out_sum)
     picked = after(picked, w_out_sum, *got, *ring_grads.sent)
-    while ring_first.at > 1:
-        ring_first.step(w_out_sum)
-    picked = after(picked, *ring_first.sent)
     w_in_sum = weight_grads(picked, grad_pre, 0, half, None)
     while ring_grads.at > 0:
         got = ring_grads.got
@@ -1080,9 +1087,10 @@
 def reduce_packed(mine, other, my_spot, peers, dp_count, grad_w_in, grad_w_out, ring_results, widths):
     lines, span, columns = mine.shape
     swap = [(d, d ^ 1) for d in range(dp_count)]
-    while ring_results.at > 0:
+    while ring_results.at > 1:
         ring_results.step()
     total = add_rows(mine, lax.ppermute(other, "dp", swap))
+    total = after(total, *ring_results.got)
     piece = span // peers
     total = total.reshape(lines, peers, piece, columns)
 
@@ -1094,11 +1102,13 @@
     farthest = part(peers // 2)
     ring = RingScatter(part, (farthest[:half], farthest[half:]), peers)
     ring.step()
+    ring_results.step()
+    ring.step(*ring_results.sent)
     while ring.at > 0:
         ring.step()
     own, left, right = [held.astype(jnp.float32) for held in (part(0), ring.left, ring.right)]
     mine = (own + left + right).astype(jnp.bfloat16).reshape(lines, piece, columns)
-    mine = after(mine, grad_w_in, grad_w_out)
+    mine = after(mine, grad_w_in, grad_w_out, *ring_results.got)
     line = lax.axis_index("dp") // 2
 
     def for_line(at):

time: 793 us -> 789 us (level)
    ppermute x2, waiting for transfers between devices: 34.4 us -> 5.06 us  [gather_blocks(): across = lax.ppermute(part, 'dp', line)]
    ppermute x72, waiting for transfers between devices: 236 us -> 260 us  [ring_step(): return lax.ppermute(part, 'expert', pairs)]
  transfers between devices with their start and end apart: 82 -> 82, of which waited for: 48 -> 43; matrix products, arithmetic and copies ran while one was open for 10% -> 10% of each run, Pallas kernels for 37% -> 38%
where the time goes in v1:
time: 789 us; the launch traced here: 779 us
  Pallas kernels  299 us (38%)
  waiting for transfers between devices  277 us (35%)
  starting transfers between devices  81.3 us (10%)
  other arithmetic  66.7 us (8%)
  local copies, waits for them, and re-layouts  34.7 us (4%)
  between operations  20.4 us (3%)
    ppermute x72, waiting for transfers between devices, ring_step(): return lax.ppermute(part, 'expert', pairs)  260 us
    pallas_call x4, Pallas kernels, expert_pass(): pl.pallas_call(functools.partial(expert_kernel, sources), grid=(count,),...  97.3 us
    pallas_call x11, Pallas kernels, block_call(): pl.pallas_call(kernel, grid_spec=pltpu.PrefetchScalarGridSpec(num_scalar_...  87.5 us
    ppermute x72, starting transfers between devices, ring_step(): return lax.ppermute(part, 'expert', pairs)  77.3 us
    pallas_call x3, Pallas kernels, weight_grads(): pl.pallas_call(weight_grad_kernel, grid=(count, height // tile), in_specs...  46.1 us
    convert_element_type x17, other arithmetic, add_rows(): (left.astype(jnp.float32) + right.astype(jnp.float32)).astype(jnp.bfloat16)  36.5 us
    pallas_call x2, Pallas kernels, spread_rows(): pl.pallas_call(functools.partial(spread_kernel, sources // 2 - base, span...  28.1 us
  transfers between devices with their start and end apart: 82, of which 43 were waited for; matrix products, arithmetic and copies ran while one was open for 10% of the time, Pallas kernels for 38%

profile of v1, /device:TPU:0, one launch (start us, length us, event | category | flops | bytes accessed | tf_op | source)
XLA Modules:
  0.0 779.2 jit_solution(1476086777963748385)
XLA Ops:
  20.3 33.0 %collective-permute-done.4.refs_1_ = bf16[256,1536]{1,0:T(8,128)(2,1)} collective-permute-done((bf16[256,1536]{1,0:T(8,128)(2,1)S(1)}, bf16[256,1536]{1,0:T(8,128)(2,1)}, u32[]{:S(2)}, u32[]{:S(2)}) %collective-permute-start.4) | collective-permute-done | bytes 786464 | tf_op jit(solution)/shard_map/ppermute | solution.py:289
  64.0 14.2 %attention_forward.1 = (bf16[2,256,1536]{2,1,0:T(8,128)(2,1)}, bf16[2,256,1536]{2,1,0:T(8,128)(2,1)}, bf16[2,256,512]{2,1,0:T(8,128)(2,1)}, bf16[2,256,1536]{2,1...) custom-call(s32[4]{0:T(128)} %add_multiply_fusion.starts_ref, ...), custom_call_target="tpu_custom_call" | custom-call | flops 1000000 | bytes 1000000 | tf_op jit(solution)/shard_map/attention_forward/pallas_call | solution.py:648
  84.8 8.6 %collective-permute-done.10.refs_2_ = bf16[272,1536]{1,0:T(8,128)(2,1)} collective-permute-done((bf16[272,1536]{1,0:T(8,128)(2,1)}, bf16[272,1536]{1,0:T(8,128)(2,1)}, u32[]{:S(2)}, u32[]{:S(2)}) %collective-permute-start.10) | collective-permute-done | bytes 835616 | tf_op jit(solution)/shard_map/ppermute | solution.py:289
  95.6 14.1 %collective-permute-done.17.refs_3_ = bf16[256,1536]{1,0:T(8,128)(2,1)} collective-permute-done((bf16[256,1536]{1,0:T(8,128)(2,1)}, bf16[256,1536]{1,0:T(8,128)(2,1)}, u32[]{:S(2)}, u32[]{:S(2)}) %collective-permute-start.17) | collective-permute-done | bytes 786464 | tf_op jit(solution)/shard_map/ppermute | solution.py:289
  117.0 13.1 %collective-permute-done.13.refs_6_ = bf16[272,1536]{1,0:T(8,128)(2,1)S(1)} collective-permute-done((bf16[272,1536]{1,0:T(8,128)(2,1)}, bf16[272,1536]{1,0:T(8,128)(2,1)S(1)}, u32[]{:S(2)}, u32[]{:S(2)}) %collective-permute-start.13) | collective-permute-done | bytes 835616 | tf_op jit(solution)/shard_map/ppermute | solution.py:289
  142.2 6.9 join_blocks.2.refs_0_
  168.7 10.6 %collective-permute-done.22.refs_2_.refs_3_ = bf16[272,1536]{1,0:T(8,128)(2,1)S(1)} collective-permute-done((bf16[272,1536]{1,0:T(8,128)(2,1)S(1)}, bf16[272,1536]{1,0:T(8,128)(2,1)S(1)}, u32[]{:S(2)}, u32[]{:S(2)}) %collective-permute-start.22) | collective-permute-done | bytes 835616 | tf_op jit(solution)/shard_map/ppermute | solution.py:289
  189.2 8.3 %collective-permute-done.24.refs_4_.refs_5_ = bf16[272,1536]{1,0:T(8,128)(2,1)} collective-permute-done((bf16[272,1536]{1,0:T(8,128)(2,1)S(1)}, bf16[272,1536]{1,0:T(8,128)(2,1)}, u32[]{:S(2)}, u32[]{:S(2)}) %collective-permute-start.24) | collective-permute-done | bytes 835616 | tf_op jit(solution)/shard_map/ppermute | solution.py:289
  207.8 11.8 %collective-permute-done.27.refs_5_.refs_6_ = bf16[272,1536]{1,0:T(8,128)(2,1)S(1)} collective-permute-done((bf16[272,1536]{1,0:T(8,128)(2,1)}, bf16[272,1536]{1,0:T(8,128)(2,1)S(1)}, u32[]{:S(2)}, u32[]{:S(2)}) %collective-permute-start.27) | collective-permute-done | bytes 835616 | tf_op jit(solution)/shard_map/ppermute | solution.py:289
  221.8 10.5 %collective-permute-done.28.refs_2_ = bf16[128,1536]{1,0:T(8,128)(2,1)S(1)} collective-permute-done((bf16[128,1536]{1,0:T(8,128)(2,1)S(1)}, bf16[128,1536]{1,0:T(8,128)(2,1)S(1)}, u32[]{:S(2)}, u32[]{:S(2)}) %collective-permute-start.28) | collective-permute-done | bytes 393248 | tf_op jit(solution)/shard_map/ppermute | solution.py:289
  245.3 24.3 %expert_pass.4 = (bf16[8,256,1536]{2,1,0:T(8,128)(2,1)}, bf16[8,256,1536]{2,1,0:T(8,128)(2,1)}, f32[4,512,1]{2,1,0:T(8,128)}, bf16[4,1024,1536]{2,1,0:T(8,128)(2...) custom-call(bf16[256,1536]{1,0:T(8,128)(2,1)} %get-tuple-element.295.refs_0_, ...), custom_call_target="tpu_custom_call" | custom-call | flops 1000000 | bytes 1000000 | tf_op jit(solution)/shard_map/expert_pass/pallas_call | solution.py:435
  271.9 24.3 %expert_pass.5 = (bf16[8,256,1536]{2,1,0:T(8,128)(2,1)}, bf16[8,256,1536]{2,1,0:T(8,128)(2,1)}, f32[4,512,1]{2,1,0:T(8,128)}, bf16[4,1024,1536]{2,1,0:T(8,128)(2...) custom-call(bf16[256,1536]{1,0:T(8,128)(2,1)} %get-tuple-element.295, ...), custom_call_target="tpu_custom_call", output_to_operand_aliasing={{0}: (26, {}), {1}: (27, {}), {2}: (28, {}), {3}: (29, {}),... | custom-call | flops 1000000 | bytes 1000000 | tf_op jit(solution)/shard_map/expert_pass/pallas_call | solution.py:435
  298.3 14.0 %spread_rows.2 = (bf16[8,528,1536]{2,1,0:T(8,128)(2,1)}, bf16[272,1536]{1,0:T(8,128)(2,1)}, bf16[256,1536]{1,0:T(8,128)(2,1)}) custom-call(s32[1]{0:T(128)} %bitcast.8.first_ref, bf16[8,256,256]{2,1,0:T(8,128)(2,1)} %get-tuple-element.294.place_ref, bf16[8,256,1536]{2,1,0:T(8,128)(2,1)} %get-tuple-element.302.rows_ref, ...), custom_call_target="tpu_custom_call" | custom-call | flops 1000000 | bytes 1000000 | tf_op jit(solution)/shard_map/spread_rows/pallas_call | solution.py:582
  324.4 9.9 %collective-permute-done.38.refs_2_ = bf16[128,1536]{1,0:T(8,128)(2,1)S(1)} collective-permute-done((bf16[128,1536]{1,0:T(8,128)(2,1)S(1)}, bf16[128,1536]{1,0:T(8,128)(2,1)S(1)}, u32[]{:S(2)}, u32[]{:S(2)}) %collective-permute-start.38) | collective-permute-done | bytes 393248 | tf_op jit(solution)/shard_map/ppermute | solution.py:289
  341.2 24.3 %expert_pass.6 = (bf16[8,256,1536]{2,1,0:T(8,128)(2,1)}, bf16[8,256,1536]{2,1,0:T(8,128)(2,1)}, f32[4,512,1]{2,1,0:T(8,128)}, bf16[4,1024,1536]{2,1,0:T(8,128)(2...) custom-call(bf16[256,1536]{1,0:T(8,128)(2,1)} %get-tuple-element.348, ...), custom_call_target="tpu_custom_call", output_to_operand_aliasing={{3}: (26, {}), {4}: (27, {}), {5}: (28, {}), {6}: (29, {})} | custom-call | flops 1000000 | bytes 1000000 | tf_op jit(solution)/shard_map/expert_pass/pallas_call | solution.py:435
  373.2 24.3 %expert_pass.7 = (bf16[8,256,1536]{2,1,0:T(8,128)(2,1)}, bf16[8,256,1536]{2,1,0:T(8,128)(2,1)}, f32[4,512,1]{2,1,0:T(8,128)}, bf16[4,1024,1536]{2,1,0:T(8,128)(2...) custom-call(bf16[256,1536]{1,0:T(8,128)(2,1)} %get-tuple-element.348, ...), custom_call_target="tpu_custom_call", output_to_operand_aliasing={{0}: (26, {}), {1}: (27, {}), {2}: (28, {}), {3}: (29, {}),... | custom-call | flops 1000000 | bytes 1000000 | tf_op jit(solution)/shard_map/expert_pass/pallas_call | solution.py:435
  397.6 14.1 %spread_rows.3 = (bf16[8,528,1536]{2,1,0:T(8,128)(2,1)}, bf16[128,1536]{1,0:T(8,128)(2,1)}, bf16[144,1536]{1,0:T(8,128)(2,1)}, bf16[128,1536]{1,0:T(8,128)(2,1)}, bf16[128,1536]{1,0:T(8,128)(2,1)}) custom-call(s32[1]{0:T(128)} %bitcast.8.first_ref, bf16[8,256,256]{2,1,0:T(8,128)(2,1)} %get-tuple-element.518.place_ref, ...), custom_call_target="tpu_custom_call" | custom-call | flops 1000000 | bytes 1000000 | tf_op jit(solution)/shard_map/spread_rows/pallas_call | solution.py:582
  417.1 8.9 %collective-permute-done.44 = bf16[128,1536]{1,0:T(8,128)(2,1)S(1)} collective-permute-done((bf16[128,1536]{1,0:T(8,128)(2,1)S(1)}, bf16[128,1536]{1,0:T(8,128)(2,1)S(1)}, u32[]{:S(2)}, u32[]{:S(2)}) %collective-permute-start.44) | collective-permute-done | bytes 393248 | tf_op jit(solution)/shard_map/ppermute | solution.py:289
  436.9 15.1 %weight_grads.3 = bf16[4,768,1536]{2,1,0:T(8,128)(2,1)} custom-call(bf16[4,1024,768]{2,1,0:T(8,128)(2,1)} %get-tuple-element.370.left_ref, bf16[4,1024,1536]{2,1,0:T(8,128)(2,1)} %get-tuple-element.371.right_ref), custom_call_target="tpu_custom_call" | custom-call | flops 1000000 | bytes 1000000 | tf_op jit(solution)/shard_map/weight_grads/pallas_call | solution.py:613
  461.6 16.1 %weight_grads.4.refs_0_ = bf16[4,1536,1536]{2,1,0:T(8,128)(2,1)} custom-call(bf16[4,1024,1536]{2,1,0:T(8,128)(2,1)} %get-tuple-element.394.left_ref, bf16[4,1024,1536]{2,1,0:T(8,128)(2,1)} %get-tuple-element.378.right_ref), custom_call_target="tpu_custom_call" | custom-call | flops 1000000 | bytes 1000000 | tf_op jit(solution)/shard_map/weight_grads/pallas_call | solution.py:613
  477.7 23.5 %collective-permute-done.48 = bf16[272,1536]{1,0:T(8,128)(2,1)} collective-permute-done((bf16[272,1536]{1,0:T(8,128)(2,1)}, bf16[272,1536]{1,0:T(8,128)(2,1)}, u32[]{:S(2)}, u32[]{:S(2)}) %collective-permute-start.48) | collective-permute-done | bytes 835616 | tf_op jit(solution)/shard_map/ppermute | solution.py:289
  514.8 14.9 %weight_grads.5 = bf16[4,1536,1536]{2,1,0:T(8,128)(2,1)} custom-call(bf16[4,1024,1536]{2,1,0:T(8,128)(2,1)} %get-tuple-element.394.left_ref, bf16[4,1024,1536]{2,1,0:T(8,128)(2,1)} %get-tuple-element.378.right_ref, bf16[4,1536,1536]{2,1,0:T(8,128)(2,1)} %weight_grads.4.refs_0_), custom_call_target="tpu_custom_call", output_to_operand_aliasing={{}: (2, {})} | custom-call | flops 1000000 | bytes 1000000 | tf_op jit(solution)/shard_map/weight_grads/pallas_call | solution.py:613
  535.1 20.0 %attention_backward.2 = (bf16[256,1536]{1,0:T(8,128)(2,1)}, bf16[256,2176]{1,0:T(8,128)(2,1)}, bf16[256,1536]{1,0:T(8,128)(2,1)}, f32[8,1536]{1,0:T(8,128)}) custom-call(bf16[8,528,1536]{2,1,0:T(8,128)(2,1)} %get-tuple-element.395.own_ref, bf16[272,1536]{1,0:T(8,128)(2,1)} %collective-permute-done.54.left_ref, ...), custom_call_target="tpu_custom_call" | custom-call | flops 1000000 | bytes 1000000 | tf_op jit(solution)/shard_map/attention_backward/pallas_call | solution.py:470
  561.9 9.7 %collective-permute-done.50.left_ref = bf16[528,1536]{1,0:T(8,128)(2,1)S(1)} collective-permute-done((bf16[528,1536]{1,0:T(8,128)(2,1)}, bf16[528,1536]{1,0:T(8,128)(2,1)S(1)}, u32[]{:S(2)}, u32[]{:S(2)}) %collective-permute-start.50) | collective-permute-done | bytes 1622048 | tf_op jit(solution)/shard_map/ppermute | solution.py:289
  574.9 18.5 %attention_backward.3 = (bf16[256,1536]{1,0:T(8,128)(2,1)}, bf16[256,2176]{1,0:T(8,128)(2,1)}, bf16[256,1536]{1,0:T(8,128)(2,1)}, f32[8,1536]{1,0:T(8,128)}) custom-call(bf16[8,528,1536]{2,1,0:T(8,128)(2,1)} %get-tuple-element.404.own_ref, bf16[528,1536]{1,0:T(8,128)(2,1)} %copy-done.12, bf16[528,1536]{1,0:T(8,128)(2,1)} %copy-done.13, ...), custom_call_target="tpu_custom_call" | custom-call | flops 1000000 | bytes 1000000 | tf_op jit(solution)/shard_map/attention_backward/pallas_call | solution.py:470
  595.7 13.0 %attention_grads.1 = (bf16[2,384,3712]{2,1,0:T(8,128)(2,1)}, bf16[2,384,3712]{2,1,0:T(8,128)(2,1)}) custom-call(s32[2]{0:T(128)} %pad_add_fusion.core_ref, bf16[2,256,1536]{2,1,0:T(8,128)(2,1)} %get-tuple-element.415.xn1, bf16[2,256,1536]{2,1,0:T(8,128)(2,1)} %get-tuple-element.234.mixed_ref.mixed, bf16[256,2176]{1,0:T(8,128)(2,1)} %get-tuple-element.416.refs_0_, ...), custom_call_target="tpu_custom_call" | custom-call | flops 1000000 | bytes 1000000 | tf_op jit(solution)/shard_map/attention_grads/pallas_call | solution.py:739
  624.0 7.3 collective-permute-done.58
  652.6 9.0 %collective-permute-done.66 = bf16[96,3712]{1,0:T(8,128)(2,1)} collective-permute-done((bf16[96,3712]{1,0:T(8,128)(2,1)}, bf16[96,3712]{1,0:T(8,128)(2,1)}, u32[]{:S(2)}, u32[]{:S(2)}) %collective-permute-start.66) | collective-permute-done | bytes 712736 | tf_op jit(solution)/shard_map/ppermute | solution.py:289
  669.7 13.2 %collective-permute-done.68 = bf16[96,3712]{1,0:T(8,128)(2,1)S(1)} collective-permute-done((bf16[96,3712]{1,0:T(8,128)(2,1)S(1)}, bf16[96,3712]{1,0:T(8,128)(2,1)S(1)}, u32[]{:S(2)}, u32[]{:S(2)}) %collective-permute-start.68) | collective-permute-done | bytes 712736 | tf_op jit(solution)/shard_map/ppermute | solution.py:289
  688.8 15.2 %collective-permute-done.69 = bf16[96,3712]{1,0:T(8,128)(2,1)} collective-permute-done((bf16[96,3712]{1,0:T(8,128)(2,1)}, bf16[96,3712]{1,0:T(8,128)(2,1)}, u32[]{:S(2)}, u32[]{:S(2)}) %collective-permute-start.69) | collective-permute-done | bytes 712736 | tf_op jit(solution)/shard_map/ppermute | solution.py:289
  706.4 9.8 %collective-permute-done.60 = bf16[256,1536]{1,0:T(8,128)(2,1)S(1)} collective-permute-done((bf16[256,1536]{1,0:T(8,128)(2,1)S(1)}, bf16[256,1536]{1,0:T(8,128)(2,1)S(1)}, u32[]{:S(2)}, u32[]{:S(2)}) %collective-permute-start.60) | collective-permute-done | bytes 786464 | tf_op jit(solution)/shard_map/ppermute | solution.py:289
  717.4 7.2 collective-permute-done.71
  (365 shorter events, 291.1 us)
Async XLA Ops:
  7.2 709.9 %reduce-scatter.5.cloned.1.call-start = ((), (), s32[]{:S(2)}) async-start(), calls=%async_computation.3 | async-start | bytes 11796480 | tf_op jit(solution)/shard_map/reduce_scatter | solution.py:1026
  12.9 41.7 %collective-permute-start.1 = (bf16[384,2176]{1,0:T(8,128)(2,1)S(1)}, bf16[384,2176]{1,0:T(8,128)(2,1)}, u32[]{:S(2)}, u32[]{:S(2)}) collective-permute-start(bf16[384,2176]{1,0:T(8,128)(2,1)S(1)} %concatenate.38.refs_0_), channel_id=1, source_target_pairs={{0,16},{8,24},{16,0},{24,8},{1,17},{9,25},{17,1},{25,9},{2,18},{10... | collective-permute-start | bytes 5013512 | tf_op jit(solution)/shard_map/ppermute | solution.py:764
  16.2 38.4 %collective-permute-start.2 = (bf16[272,1536]{1,0:T(8,128)(2,1)S(1)}, bf16[272,1536]{1,0:T(8,128)(2,1)S(1)}, u32[]{:S(2)}, u32[]{:S(2)}) collective-permute-start(bf16[272,1536]{1,0:T(8,128)(2,1)S(1)} %pad_maximum_fusion.4.refs_0_), channel_id=1, source_target_pairs={{0,2},{2,4},{4,6},{6,7},{7,5},{5,3},{3,1},{1,0},{8,10},{10,12},{12... | collective-permute-start | bytes 2506760 | tf_op jit(solution)/shard_map/ppermute | solution.py:289
  17.9 36.7 %collective-permute-start.3 = (bf16[272,1536]{1,0:T(8,128)(2,1)S(1)}, bf16[272,1536]{1,0:T(8,128)(2,1)S(1)}, u32[]{:S(2)}, u32[]{:S(2)}) collective-permute-start(bf16[272,1536]{1,0:T(8,128)(2,1)S(1)} %pad_maximum_fusion.4.refs_0_), channel_id=1, source_target_pairs={{0,1},{2,0},{4,2},{6,4},{7,6},{5,7},{3,5},{1,3},{8,9},{10,8},{12,1... | collective-permute-start | bytes 2506760 | tf_op jit(solution)/shard_map/ppermute | solution.py:289
  18.3 35.0 %collective-permute-start.4 = (bf16[256,1536]{1,0:T(8,128)(2,1)S(1)}, bf16[256,1536]{1,0:T(8,128)(2,1)}, u32[]{:S(2)}, u32[]{:S(2)}) collective-permute-start(bf16[256,1536]{1,0:T(8,128)(2,1)S(1)} %get-tuple-element.232.refs_0_), channel_id=1, source_target_pairs={{0,2},{2,4},{4,6},{6,7},{7,5},{5,3},{3,1},{1,0},{8,10},{10,12},{12... | collective-permute-start | bytes 2359304 | tf_op jit(solution)/shard_map/ppermute | solution.py:289
  19.9 34.7 %collective-permute-start.5 = (bf16[256,1536]{1,0:T(8,128)(2,1)S(1)}, bf16[256,1536]{1,0:T(8,128)(2,1)}, u32[]{:S(2)}, u32[]{:S(2)}) collective-permute-start(bf16[256,1536]{1,0:T(8,128)(2,1)S(1)} %get-tuple-element.232.refs_0_), channel_id=1, source_target_pairs={{0,1},{2,0},{4,2},{6,4},{7,6},{5,7},{3,5},{1,3},{8,9},{10,8},{12,1... | collective-permute-start | bytes 2359304 | tf_op jit(solution)/shard_map/ppermute | solution.py:289
  58.7 34.6 %collective-permute-start.10 = (bf16[272,1536]{1,0:T(8,128)(2,1)}, bf16[272,1536]{1,0:T(8,128)(2,1)}, u32[]{:S(2)}, u32[]{:S(2)}) collective-permute-start(bf16[272,1536]{1,0:T(8,128)(2,1)} %copy-done.32), channel_id=1, source_target_pairs={{0,2},{2,4},{4,6},{6,7},{7,5},{5,3},{3,1},{1,0},{8,10},{10,12},{12... | collective-permute-start | bytes 2506760 | tf_op jit(solution)/shard_map/ppermute | solution.py:289
  60.3 33.9 %collective-permute-start.11 = (bf16[272,1536]{1,0:T(8,128)(2,1)}, bf16[272,1536]{1,0:T(8,128)(2,1)}, u32[]{:S(2)}, u32[]{:S(2)}) collective-permute-start(bf16[272,1536]{1,0:T(8,128)(2,1)} %copy-done.33), channel_id=1, source_target_pairs={{0,1},{2,0},{4,2},{6,4},{7,6},{5,7},{3,5},{1,3},{8,9},{10,8},{12,1... | collective-permute-start | bytes 2506760 | tf_op jit(solution)/shard_map/ppermute | solution.py:289
  78.3 31.4 %collective-permute-start.17 = (bf16[256,1536]{1,0:T(8,128)(2,1)}, bf16[256,1536]{1,0:T(8,128)(2,1)}, u32[]{:S(2)}, u32[]{:S(2)}) collective-permute-start(bf16[256,1536]{1,0:T(8,128)(2,1)} %collective-permute-done.15.refs_2_), channel_id=1, source_target_pairs={{0,2},{2,4},{4,6},{6,7},{7,5},{5,3},{3,1},{1,0},{8,10},{10,12},{12... | collective-permute-start | bytes 2359304 | tf_op jit(solution)/shard_map/ppermute | solution.py:289
  79.6 53.2 %collective-permute-start.7 = (bf16[384,1536]{1,0:T(8,128)(2,1)}, bf16[384,1536]{1,0:T(8,128)(2,1)S(1)}, u32[]{:S(2)}, u32[]{:S(2)}) collective-permute-start(bf16[384,1536]{1,0:T(8,128)(2,1)} %refs_0_.4), channel_id=1, source_target_pairs={{0,8},{8,0},{16,24},{24,16},{1,9},{9,1},{17,25},{25,17},{2,10},{10... | collective-permute-start | bytes 3538952 | tf_op jit(solution)/shard_map/ppermute | solution.py:765
  84.8 49.6 %collective-permute-start.9 = (bf16[384,1536]{1,0:T(8,128)(2,1)S(1)}, bf16[384,1536]{1,0:T(8,128)(2,1)S(1)}, u32[]{:S(2)}, u32[]{:S(2)}) collective-permute-start(bf16[384,1536]{1,0:T(8,128)(2,1)S(1)} %collective-permute-done.8.refs_2_), channel_id=1, source_target_pairs={{0,8},{8,0},{16,24},{24,16},{1,9},{9,1},{17,25},{25,17},{2,10},{10... | collective-permute-start | bytes 3538952 | tf_op jit(solution)/shard_map/ppermute | solution.py:771
  94.2 35.9 %collective-permute-start.13 = (bf16[272,1536]{1,0:T(8,128)(2,1)}, bf16[272,1536]{1,0:T(8,128)(2,1)S(1)}, u32[]{:S(2)}, u32[]{:S(2)}) collective-permute-start(bf16[272,1536]{1,0:T(8,128)(2,1)} %collective-permute-done.11.refs_7_), channel_id=1, source_target_pairs={{0,1},{2,0},{4,2},{6,4},{7,6},{5,7},{3,5},{1,3},{8,9},{10,8},{12,1... | collective-permute-start | bytes 2506760 | tf_op jit(solution)/shard_map/ppermute | solution.py:289
  115.4 46.2 %collective-permute-start.19 = (bf16[128,1536]{1,0:T(8,128)(2,1)}, bf16[128,1536]{1,0:T(8,128)(2,1)}, u32[]{:S(2)}, u32[]{:S(2)}) collective-permute-start(bf16[128,1536]{1,0:T(8,128)(2,1)} %slice.318), channel_id=1, source_target_pairs={{0,2},{2,4},{4,6},{6,7},{7,5},{5,3},{3,1},{1,0},{8,10},{10,12},{12... | collective-permute-start | bytes 1179656 | tf_op jit(solution)/shard_map/ppermute | solution.py:289
  130.1 31.5 %collective-permute-start.20 = (bf16[128,1536]{1,0:T(8,128)(2,1)}, bf16[128,1536]{1,0:T(8,128)(2,1)}, u32[]{:S(2)}, u32[]{:S(2)}) collective-permute-start(bf16[128,1536]{1,0:T(8,128)(2,1)} %slice.319), channel_id=1, source_target_pairs={{0,1},{2,0},{4,2},{6,4},{7,6},{5,7},{3,5},{1,3},{8,9},{10,8},{12,1... | collective-permute-start | bytes 1179656 | tf_op jit(solution)/shard_map/ppermute | solution.py:289
  132.3 29.3 %collective-permute-start.14 = (bf16[144,1536]{1,0:T(8,128)(2,1)S(1)}, bf16[144,1536]{1,0:T(8,128)(2,1)S(1)}, u32[]{:S(2)}, u32[]{:S(2)}) collective-permute-start(bf16[144,1536]{1,0:T(8,128)(2,1)S(1)} %slice.310), channel_id=1, source_target_pairs={{0,1},{2,0},{4,2},{6,4},{7,6},{5,7},{3,5},{1,3},{8,9},{10,8},{12,1... | collective-permute-start | bytes 1327112 | tf_op jit(solution)/shard_map/ppermute | solution.py:289
  233.1 36.5 %collective-permute-start.30 = (bf16[272,1536]{1,0:T(8,128)(2,1)S(1)}, bf16[272,1536]{1,0:T(8,128)(2,1)S(1)}, u32[]{:S(2)}, u32[]{:S(2)}) collective-permute-start(bf16[272,1536]{1,0:T(8,128)(2,1)S(1)} %copy-done.14), channel_id=1, source_target_pairs={{0,2},{2,4},{4,6},{6,7},{7,5},{5,3},{3,1},{1,0},{8,10},{10,12},{12... | collective-permute-start | bytes 2506760 | tf_op jit(solution)/shard_map/ppermute | solution.py:289
  234.6 35.0 %collective-permute-start.31 = (bf16[272,1536]{1,0:T(8,128)(2,1)S(1)}, bf16[272,1536]{1,0:T(8,128)(2,1)}, u32[]{:S(2)}, u32[]{:S(2)}) collective-permute-start(bf16[272,1536]{1,0:T(8,128)(2,1)S(1)} %copy-done.14), channel_id=1, source_target_pairs={{0,1},{2,0},{4,2},{6,4},{7,6},{5,7},{3,5},{1,3},{8,9},{10,8},{12,1... | collective-permute-start | bytes 2506760 | tf_op jit(solution)/shard_map/ppermute | solution.py:289
  317.3 48.2 %collective-permute-start.36 = (bf16[272,1536]{1,0:T(8,128)(2,1)}, bf16[272,1536]{1,0:T(8,128)(2,1)S(1)}, u32[]{:S(2)}, u32[]{:S(2)}) collective-permute-start(bf16[272,1536]{1,0:T(8,128)(2,1)} %get-tuple-element.312), channel_id=1, source_target_pairs={{0,1},{2,0},{4,2},{6,4},{7,6},{5,7},{3,5},{1,3},{8,9},{10,8},{12,1... | collective-permute-start | bytes 2506760 | tf_op jit(solution)/shard_map/ppermute | solution.py:289
  317.6 48.0 %collective-permute-start.37 = (bf16[256,1536]{1,0:T(8,128)(2,1)}, bf16[256,1536]{1,0:T(8,128)(2,1)}, u32[]{:S(2)}, u32[]{:S(2)}) collective-permute-start(bf16[256,1536]{1,0:T(8,128)(2,1)} %get-tuple-element.313), channel_id=1, source_target_pairs={{0,2},{2,4},{4,6},{6,7},{7,5},{5,3},{3,1},{1,0},{8,10},{10,12},{12... | collective-permute-start | bytes 2359304 | tf_op jit(solution)/shard_map/ppermute | solution.py:289
  371.0 61.4 %collective-permute-start.40 = (bf16[528,1536]{1,0:T(8,128)(2,1)}, bf16[528,1536]{1,0:T(8,128)(2,1)S(1)}, u32[]{:S(2)}, u32[]{:S(2)}) collective-permute-start(bf16[528,1536]{1,0:T(8,128)(2,1)} %pad_maximum_fusion), channel_id=1, source_target_pairs={{0,1},{2,0},{4,2},{6,4},{7,6},{5,7},{3,5},{1,3},{8,9},{10,8},{12,1... | collective-permute-start | bytes 4866056 | tf_op jit(solution)/shard_map/ppermute | solution.py:289
  371.2 61.2 %collective-permute-start.41 = (bf16[528,1536]{1,0:T(8,128)(2,1)}, bf16[528,1536]{1,0:T(8,128)(2,1)S(1)}, u32[]{:S(2)}, u32[]{:S(2)}) collective-permute-start(bf16[528,1536]{1,0:T(8,128)(2,1)} %pad_maximum_fusion.1), channel_id=1, source_target_pairs={{0,2},{2,4},{4,6},{6,7},{7,5},{5,3},{3,1},{1,0},{8,10},{10,12},{12... | collective-permute-start | bytes 4866056 | tf_op jit(solution)/shard_map/ppermute | solution.py:289
  452.0 265.0 %reduce-scatter.3.cloned.1.call-start = ((), (), s32[]{:S(2)}) async-start(), calls=%async_computation.2 | async-start | bytes 23592960 | tf_op jit(solution)/shard_map/reduce_scatter | solution.py:1029
  453.4 55.9 %collective-permute-start.42 = (bf16[528,1536]{1,0:T(8,128)(2,1)S(1)}, bf16[528,1536]{1,0:T(8,128)(2,1)}, u32[]{:S(2)}, u32[]{:S(2)}) collective-permute-start(bf16[528,1536]{1,0:T(8,128)(2,1)S(1)} %copy-done.28), channel_id=1, source_target_pairs={{0,1},{2,0},{4,2},{6,4},{7,6},{5,7},{3,5},{1,3},{8,9},{10,8},{12,1... | collective-permute-start | bytes 4866056 | tf_op jit(solution)/shard_map/ppermute | solution.py:289
  455.4 54.0 %collective-permute-start.43 = (bf16[528,1536]{1,0:T(8,128)(2,1)S(1)}, bf16[528,1536]{1,0:T(8,128)(2,1)}, u32[]{:S(2)}, u32[]{:S(2)}) collective-permute-start(bf16[528,1536]{1,0:T(8,128)(2,1)S(1)} %copy-done.27), channel_id=1, source_target_pairs={{0,2},{2,4},{4,6},{6,7},{7,5},{5,3},{3,1},{1,0},{8,10},{10,12},{12... | collective-permute-start | bytes 4866056 | tf_op jit(solution)/shard_map/ppermute | solution.py:289
  459.2 42.0 %collective-permute-start.48 = (bf16[272,1536]{1,0:T(8,128)(2,1)}, bf16[272,1536]{1,0:T(8,128)(2,1)}, u32[]{:S(2)}, u32[]{:S(2)}) collective-permute-start(bf16[272,1536]{1,0:T(8,128)(2,1)} %get-tuple-element.374), channel_id=1, source_target_pairs={{0,1},{2,0},{4,2},{6,4},{7,6},{5,7},{3,5},{1,3},{8,9},{10,8},{12,1... | collective-permute-start | bytes 2506760 | tf_op jit(solution)/shard_map/ppermute | solution.py:289
  460.9 42.8 %collective-permute-start.49 = (bf16[272,1536]{1,0:T(8,128)(2,1)}, bf16[272,1536]{1,0:T(8,128)(2,1)}, u32[]{:S(2)}, u32[]{:S(2)}) collective-permute-start(bf16[272,1536]{1,0:T(8,128)(2,1)} %get-tuple-element.375), channel_id=1, source_target_pairs={{0,2},{2,4},{4,6},{6,7},{7,5},{5,3},{3,1},{1,0},{8,10},{10,12},{12... | collective-permute-start | bytes 2506760 | tf_op jit(solution)/shard_map/ppermute | solution.py:289
  533.1 38.6 %collective-permute-start.50 = (bf16[528,1536]{1,0:T(8,128)(2,1)}, bf16[528,1536]{1,0:T(8,128)(2,1)S(1)}, u32[]{:S(2)}, u32[]{:S(2)}) collective-permute-start(bf16[528,1536]{1,0:T(8,128)(2,1)} %get-tuple-element.385), channel_id=1, source_target_pairs={{0,1},{2,0},{4,2},{6,4},{7,6},{5,7},{3,5},{1,3},{8,9},{10,8},{12,1... | collective-permute-start | bytes 4866056 | tf_op jit(solution)/shard_map/ppermute | solution.py:289
  535.1 38.6 %collective-permute-start.51 = (bf16[528,1536]{1,0:T(8,128)(2,1)}, bf16[528,1536]{1,0:T(8,128)(2,1)S(1)}, u32[]{:S(2)}, u32[]{:S(2)}) collective-permute-start(bf16[528,1536]{1,0:T(8,128)(2,1)} %get-tuple-element.386), channel_id=1, source_target_pairs={{0,2},{2,4},{4,6},{6,7},{7,5},{5,3},{3,1},{1,0},{8,10},{10,12},{12... | collective-permute-start | bytes 4866056 | tf_op jit(solution)/shard_map/ppermute | solution.py:289
  558.8 34.6 %collective-permute-start.56 = (bf16[256,1536]{1,0:T(8,128)(2,1)}, bf16[256,1536]{1,0:T(8,128)(2,1)}, u32[]{:S(2)}, u32[]{:S(2)}) collective-permute-start(bf16[256,1536]{1,0:T(8,128)(2,1)} %pad_maximum_fusion.7), channel_id=1, source_target_pairs={{0,1},{2,0},{4,2},{6,4},{7,6},{5,7},{3,5},{1,3},{8,9},{10,8},{12,1... | collective-permute-start | bytes 2359304 | tf_op jit(solution)/shard_map/ppermute | solution.py:289
  561.1 32.3 %collective-permute-start.57 = (bf16[256,1536]{1,0:T(8,128)(2,1)}, bf16[256,1536]{1,0:T(8,128)(2,1)}, u32[]{:S(2)}, u32[]{:S(2)}) collective-permute-start(bf16[256,1536]{1,0:T(8,128)(2,1)} %pad_maximum_fusion.8), channel_id=1, source_target_pairs={{0,2},{2,4},{4,6},{6,7},{7,5},{5,3},{3,1},{1,0},{8,10},{10,12},{12... | collective-permute-start | bytes 2359304 | tf_op jit(solution)/shard_map/ppermute | solution.py:289
  686.8 29.4 %collective-permute-start.60 = (bf16[256,1536]{1,0:T(8,128)(2,1)S(1)}, bf16[256,1536]{1,0:T(8,128)(2,1)S(1)}, u32[]{:S(2)}, u32[]{:S(2)}) collective-permute-start(bf16[256,1536]{1,0:T(8,128)(2,1)S(1)} %get-tuple-element.410), channel_id=1, source_target_pairs={{0,1},{2,0},{4,2},{6,4},{7,6},{5,7},{3,5},{1,3},{8,9},{10,8},{12,1... | collective-permute-start | bytes 2359304 | tf_op jit(solution)/shard_map/ppermute | solution.py:289
  687.8 29.2 %collective-permute-start.61 = (bf16[256,1536]{1,0:T(8,128)(2,1)S(1)}, bf16[256,1536]{1,0:T(8,128)(2,1)}, u32[]{:S(2)}, u32[]{:S(2)}) collective-permute-start(bf16[256,1536]{1,0:T(8,128)(2,1)S(1)} %get-tuple-element.411), channel_id=1, source_target_pairs={{0,2},{2,4},{4,6},{6,7},{7,5},{5,3},{3,1},{1,0},{8,10},{10,12},{12... | collective-permute-start | bytes 2359304 | tf_op jit(solution)/shard_map/ppermute | solution.py:289
  (106 other events, 1416.7 us)
Sparse Core Ops, SparseCore 0:
  452.2 78.6 reduce-scatter.4
  533.4 139.4 reduce-scatter.2

commit v2 on v1

--- a/solution.py
+++ b/solution.py
@@ -601,30 +601,27 @@
     )(first_expert, place, rows_back, grads_back, gate_slots, *held)
 
 
-def weight_grad_kernel(left_ref, right_ref, *refs):
-    refs[-1][...] = dot_tn(left_ref[...], right_ref[...]).astype(jnp.bfloat16)
-
-
-def weight_grads(left, right, first, count, held_out):
-    experts, held, height = left.shape
+def weight_grad_kernel(left_ref, right_ref, out_ref):
+    out_ref[...] = dot_tn(left_ref[...], right_ref[...]).astype(jnp.bfloat16)
+
+
+def weight_grads(left, right, first, count):
+    _, held, height = left.shape
     columns = right.shape[-1]
     tile = min(height, 768)
-    given = [] if held_out is None else [held_out]
     return pl.pallas_call(
         weight_grad_kernel,
         grid=(count, height // tile),
         in_specs=[
             pl.BlockSpec((None, held, tile), lambda e, i: (e + first, 0, i)),
             pl.BlockSpec((None, held, columns), lambda e, i: (e + first, 0, 0)),
-        ]
-        + [pl.BlockSpec(memory_space=pl.ANY)] * len(given),
-        out_specs=pl.BlockSpec((None, tile, columns), lambda e, i: (e + first, i, 0)),
-        out_shape=jax.ShapeDtypeStruct((experts, height, columns), jnp.bfloat16),
-        input_output_aliases={2: 0} if given else {},
+        ],
+        out_specs=pl.BlockSpec((None, tile, columns), lambda e, i: (e, i, 0)),
+        out_shape=jax.ShapeDtypeStruct((count, height, columns), jnp.bfloat16),
         compiler_params=pltpu.CompilerParams(vmem_limit_bytes=60 * 1024 * 1024),
         cost_estimate=SMALL_COST,
         name="weight_grads",
-    )(left, right, *given)
+    )(left, right)
 
 
 def attention_forward(starts, tokens, seg_col, seg_row, routes, cos, sin, weights):
@@ -848,7 +845,7 @@
     for m in micros:
         out = block_call(
             hidden_kernel,
-            [(mixed, (m,)), (tokens, (m,)), (gains,), (gates_pack, (m,))]
+            [(after(mixed, *xn2), (m,)), (tokens, (m,)), (gains,), (gates_pack, (m,))]
             + [(part,) for part in out_weights],
             [
                 jax.ShapeDtypeStruct((rows, width), jnp.float32),
@@ -861,7 +858,8 @@
         xn2.append(out[1])
     for ring in cot_rings:
         ring.step()
-    first_whole = join_blocks(starts, [after(first_weights[0], xn2[1])] + first_weights[1:])
+    got = cot_rings[0].got + cot_rings[1].got
+    first_whole = join_blocks(starts, [after(first_weights[0], *got)] + first_weights[1:])
     out_whole = join_blocks(starts, [after(out_weights[0], first_whole)] + out_weights[1:])
     routes_all = cot_rings[0].stack_rows(rows, micro_count * TOPK)[:, :, :rows]
     routes_all = routes_all.reshape(peers, micro_count, TOPK, rows)
@@ -875,7 +873,7 @@
     late = [steps - 1, steps, steps + 1]
     early = [k for k in every if k not in late]
     row_rings = [RingGather(xn2[m], peers, rows // 2) for m in micros]
-    row_rings[0].step(*cot_rings[0].got, *cot_rings[1].got)
+    row_rings[0].step()
     groups = peers // GROUP
 
     class Experts:
@@ -974,7 +972,7 @@
     place_at = jnp.stack([lax.rem(dp_at, 2), dp_at // 2])
     ring_grads.step()
     w_out_sum = weight_grads(
-        after(activated, *ring_grads.sent, *ring_first.sent), grad_result, 0, local_experts, None
+        after(activated, *ring_grads.sent, *ring_first.sent), grad_result, 0, local_experts
     )
     def backward(m, pieces, *earlier):
         own, left, right = pieces
@@ -1012,29 +1010,31 @@
     got = second_got = ring_grads.got
     ring_grads.step(w_out_sum)
     picked = after(picked, w_out_sum, *got, *ring_grads.sent)
-    w_in_sum = weight_grads(picked, grad_pre, 0, half, None)
-    while ring_grads.at > 0:
-        got = ring_grads.got
+    w_in_sum = weight_grads(picked, grad_pre, 0, half)
+    while ring_grads.at > 1:
         ring_grads.step(w_in_sum)
-    last = ring_first.got
+    got = ring_first.got + ring_grads.got
     while ring_first.at > 0:
-        ring_first.step(*ring_grads.sent)
-    picked = after(picked, w_in_sum, *got, *ring_grads.sent, *ring_first.sent)
-    w_in_sum = weight_grads(picked, grad_pre, half, local_experts - half, w_in_sum)
-    got = last
-    ring_results.step(*got)
-    grad_w_out = lax.psum_scatter(
-        after(w_out_sum, *second_got), "dp", scatter_dimension=1, tiled=True
-    )
-    grad_w_in = lax.psum_scatter(
-        after(w_in_sum, *ring_grads.got), "dp", scatter_dimension=1, tiled=True
-    )
-    back_second = backward(1, (second.sums, ring_grads.left, ring_grads.right), w_in_sum)
-    ring_results.step(back_second[3], *got)
+        ring_first.step(w_in_sum)
+
+    def scatter(part, *earlier):
+        return lax.psum_scatter(after(part, *earlier), "dp", scatter_dimension=1, tiled=True)
+
+    grad_w_out = scatter(w_out_sum, *second_got)
+    grad_w_in = [scatter(w_in_sum, *got)]
+    picked = after(picked, w_in_sum, *got, *ring_first.sent)
+    w_in_sum = weight_grads(picked, grad_pre, half, local_experts - half)
+    grad_w_in.append(scatter(w_in_sum, *ring_first.got))
+    ring_grads.step(w_in_sum)
+    ring_results.step(w_in_sum)
     back_first = backward(
-        0, (first.sums, ring_first.left, ring_first.right), *ring_results.sent
+        0, (first.sums, ring_first.left, ring_first.right), *ring_grads.sent
     )
     ring_results.step(back_first[3])
+    back_second = backward(
+        1, (second.sums, ring_grads.left, ring_grads.right), back_first[3]
+    )
+    ring_results.step(back_second[3])
     grad_tokens, grad_proj, grad_attn, gain_sums = zip(back_first, back_second)
     mine, other = attention_grads(
         place_at, after(xn1, *ring_results.sent), mixed, grad_proj, grad_attn, gain_sums, dp_count
@@ -1108,7 +1108,7 @@
         ring.step()
     own, left, right = [held.astype(jnp.float32) for held in (part(0), ring.left, ring.right)]
     mine = (own + left + right).astype(jnp.bfloat16).reshape(lines, piece, columns)
-    mine = after(mine, grad_w_in, grad_w_out, *ring_results.got)
+    mine = after(mine, *grad_w_in, grad_w_out, *ring_results.got)
     line = lax.axis_index("dp") // 2
 
     def for_line(at):
@@ -1122,7 +1122,7 @@
     gather.step()
     grad_w_out = grad_w_out.astype(jnp.float32)
     gather.step(grad_w_out)
-    grad_w_in = grad_w_in.astype(jnp.float32)
+    grad_w_in = jnp.concatenate([part.astype(jnp.float32) for part in grad_w_in], axis=0)
     gather.step(grad_w_in, *ring_results.got)
     while gather.far is None:
         gather.step()

time: 789 us -> 771 us (0.977)
  waiting for transfers between devices: 277 us -> 265 us
  transfers between devices with their start and end apart: 82 -> 83, of which waited for: 43 -> 41; matrix products, arithmetic and copies ran while one was open for 10% -> 10% of each run, Pallas kernels for 38% -> 38%
where the time goes in v2:
time: 771 us; the launch traced here: 761 us
  Pallas kernels  298 us (39%)
  waiting for transfers between devices  265 us (34%)
  starting transfers between devices  81.5 us (11%)
  other arithmetic  62.5 us (8%)
  local copies, waits for them, and re-layouts  33.9 us (4%)
  between operations  20.1 us (3%)
    ppermute x72, waiting for transfers between devices, ring_step(): return lax.ppermute(part, 'expert', pairs)  253 us
    pallas_call x4, Pallas kernels, expert_pass(): pl.pallas_call(functools.partial(expert_kernel, sources), grid=(count,),...  97.4 us
    pallas_call x11, Pallas kernels, block_call(): pl.pallas_call(kernel, grid_spec=pltpu.PrefetchScalarGridSpec(num_scalar_...  86.5 us
    ppermute x72, starting transfers between devices, ring_step(): return lax.ppermute(part, 'expert', pairs)  77.2 us
    pallas_call x3, Pallas kernels, weight_grads(): pl.pallas_call(weight_grad_kernel, grid=(count, height // tile), in_specs...  46 us
    convert_element_type x17, other arithmetic, add_rows(): (left.astype(jnp.float32) + right.astype(jnp.float32)).astype(jnp.bfloat16)  35.2 us
    pallas_call x2, Pallas kernels, spread_rows(): pl.pallas_call(functools.partial(spread_kernel, sources // 2 - base, span...  28.2 us
  transfers between devices with their start and end apart: 83, of which 41 were waited for; matrix products, arithmetic and copies ran while one was open for 10% of the time, Pallas kernels for 38%

profile of v2, /device:TPU:0, one launch (start us, length us, event | category | flops | bytes accessed | tf_op | source)
XLA Modules:
  0.0 761.1 jit_solution(14310672261622439161)
XLA Ops:
  20.3 33.0 %collective-permute-done.4.refs_1_ = bf16[256,1536]{1,0:T(8,128)(2,1)} collective-permute-done((bf16[256,1536]{1,0:T(8,128)(2,1)S(1)}, bf16[256,1536]{1,0:T(8,128)(2,1)}, u32[]{:S(2)}, u32[]{:S(2)}) %collective-permute-start.4) | collective-permute-done | bytes 786464 | tf_op jit(solution)/shard_map/ppermute | solution.py:289
  64.0 14.2 %attention_forward.1 = (bf16[2,256,1536]{2,1,0:T(8,128)(2,1)}, bf16[2,256,1536]{2,1,0:T(8,128)(2,1)}, bf16[2,256,512]{2,1,0:T(8,128)(2,1)}, bf16[2,256,1536]{2,1...) custom-call(s32[4]{0:T(128)} %add_multiply_fusion.starts_ref, ...), custom_call_target="tpu_custom_call" | custom-call | flops 1000000 | bytes 1000000 | tf_op jit(solution)/shard_map/attention_forward/pallas_call | solution.py:645
  79.7 13.6 %collective-permute-done.10.refs_2_ = bf16[272,1536]{1,0:T(8,128)(2,1)} collective-permute-done((bf16[272,1536]{1,0:T(8,128)(2,1)}, bf16[272,1536]{1,0:T(8,128)(2,1)}, u32[]{:S(2)}, u32[]{:S(2)}) %collective-permute-start.10) | collective-permute-done | bytes 835616 | tf_op jit(solution)/shard_map/ppermute | solution.py:289
  96.2 14.0 %collective-permute-done.17.refs_3_ = bf16[256,1536]{1,0:T(8,128)(2,1)} collective-permute-done((bf16[256,1536]{1,0:T(8,128)(2,1)}, bf16[256,1536]{1,0:T(8,128)(2,1)}, u32[]{:S(2)}, u32[]{:S(2)}) %collective-permute-start.17) | collective-permute-done | bytes 786464 | tf_op jit(solution)/shard_map/ppermute | solution.py:289
  116.5 13.6 %collective-permute-done.13.refs_6_ = bf16[272,1536]{1,0:T(8,128)(2,1)S(1)} collective-permute-done((bf16[272,1536]{1,0:T(8,128)(2,1)}, bf16[272,1536]{1,0:T(8,128)(2,1)S(1)}, u32[]{:S(2)}, u32[]{:S(2)}) %collective-permute-start.13) | collective-permute-done | bytes 835616 | tf_op jit(solution)/shard_map/ppermute | solution.py:289
  134.4 6.7 hidden_rows.2
  151.7 7.0 join_blocks.2.refs_0_
  175.8 9.0 %collective-permute-done.24.refs_4_.refs_5_ = bf16[272,1536]{1,0:T(8,128)(2,1)S(1)} collective-permute-done((bf16[272,1536]{1,0:T(8,128)(2,1)S(1)}, bf16[272,1536]{1,0:T(8,128)(2,1)S(1)}, u32[]{:S(2)}, u32[]{:S(2)}) %collective-permute-start.24) | collective-permute-done | bytes 835616 | tf_op jit(solution)/shard_map/ppermute | solution.py:289
  194.7 11.8 %collective-permute-done.27.refs_5_.refs_6_ = bf16[272,1536]{1,0:T(8,128)(2,1)S(1)} collective-permute-done((bf16[272,1536]{1,0:T(8,128)(2,1)}, bf16[272,1536]{1,0:T(8,128)(2,1)S(1)}, u32[]{:S(2)}, u32[]{:S(2)}) %collective-permute-start.27) | collective-permute-done | bytes 835616 | tf_op jit(solution)/shard_map/ppermute | solution.py:289
  208.7 6.8 hidden_rows.3
  230.5 24.3 %expert_pass.4 = (bf16[8,256,1536]{2,1,0:T(8,128)(2,1)}, bf16[8,256,1536]{2,1,0:T(8,128)(2,1)}, f32[4,512,1]{2,1,0:T(8,128)}, bf16[4,1024,1536]{2,1,0:T(8,128)(2...) custom-call(bf16[256,1536]{1,0:T(8,128)(2,1)} %get-tuple-element.298.refs_0_, ...), custom_call_target="tpu_custom_call" | custom-call | flops 1000000 | bytes 1000000 | tf_op jit(solution)/shard_map/expert_pass/pallas_call | solution.py:435
  257.1 24.4 %expert_pass.5 = (bf16[8,256,1536]{2,1,0:T(8,128)(2,1)}, bf16[8,256,1536]{2,1,0:T(8,128)(2,1)}, f32[4,512,1]{2,1,0:T(8,128)}, bf16[4,1024,1536]{2,1,0:T(8,128)(2...) custom-call(bf16[256,1536]{1,0:T(8,128)(2,1)} %get-tuple-element.298, ...), custom_call_target="tpu_custom_call", output_to_operand_aliasing={{0}: (26, {}), {1}: (27, {}), {2}: (28, {}), {3}: (29, {}),... | custom-call | flops 1000000 | bytes 1000000 | tf_op jit(solution)/shard_map/expert_pass/pallas_call | solution.py:435
  283.7 14.1 %spread_rows.2 = (bf16[8,528,1536]{2,1,0:T(8,128)(2,1)}, bf16[272,1536]{1,0:T(8,128)(2,1)}, bf16[256,1536]{1,0:T(8,128)(2,1)}) custom-call(s32[1]{0:T(128)} %bitcast.8.first_ref, bf16[8,256,256]{2,1,0:T(8,128)(2,1)} %get-tuple-element.297.place_ref, bf16[8,256,1536]{2,1,0:T(8,128)(2,1)} %get-tuple-element.305.rows_ref, ...), custom_call_target="tpu_custom_call" | custom-call | flops 1000000 | bytes 1000000 | tf_op jit(solution)/shard_map/spread_rows/pallas_call | solution.py:582
  309.8 11.6 %collective-permute-done.38.refs_2_ = bf16[128,1536]{1,0:T(8,128)(2,1)S(1)} collective-permute-done((bf16[128,1536]{1,0:T(8,128)(2,1)S(1)}, bf16[128,1536]{1,0:T(8,128)(2,1)S(1)}, u32[]{:S(2)}, u32[]{:S(2)}) %collective-permute-start.38) | collective-permute-done | bytes 393248 | tf_op jit(solution)/shard_map/ppermute | solution.py:289
  326.9 24.3 %expert_pass.6 = (bf16[8,256,1536]{2,1,0:T(8,128)(2,1)}, bf16[8,256,1536]{2,1,0:T(8,128)(2,1)}, f32[4,512,1]{2,1,0:T(8,128)}, bf16[4,1024,1536]{2,1,0:T(8,128)(2...) custom-call(bf16[256,1536]{1,0:T(8,128)(2,1)} %get-tuple-element.351, ...), custom_call_target="tpu_custom_call", output_to_operand_aliasing={{3}: (26, {}), {4}: (27, {}), {5}: (28, {}), {6}: (29, {})} | custom-call | flops 1000000 | bytes 1000000 | tf_op jit(solution)/shard_map/expert_pass/pallas_call | solution.py:435
  358.9 24.3 %expert_pass.7 = (bf16[8,256,1536]{2,1,0:T(8,128)(2,1)}, bf16[8,256,1536]{2,1,0:T(8,128)(2,1)}, f32[4,512,1]{2,1,0:T(8,128)}, bf16[4,1024,1536]{2,1,0:T(8,128)(2...) custom-call(bf16[256,1536]{1,0:T(8,128)(2,1)} %get-tuple-element.351, ...), custom_call_target="tpu_custom_call", output_to_operand_aliasing={{0}: (26, {}), {1}: (27, {}), {2}: (28, {}), {3}: (29, {}),... | custom-call | flops 1000000 | bytes 1000000 | tf_op jit(solution)/shard_map/expert_pass/pallas_call | solution.py:435
  383.2 14.1 %spread_rows.3 = (bf16[8,528,1536]{2,1,0:T(8,128)(2,1)}, bf16[128,1536]{1,0:T(8,128)(2,1)}, bf16[144,1536]{1,0:T(8,128)(2,1)}, bf16[128,1536]{1,0:T(8,128)(2,1)}, bf16[128,1536]{1,0:T(8,128)(2,1)}) custom-call(s32[1]{0:T(128)} %bitcast.8.first_ref, bf16[8,256,256]{2,1,0:T(8,128)(2,1)} %get-tuple-element.522.place_ref, ...), custom_call_target="tpu_custom_call" | custom-call | flops 1000000 | bytes 1000000 | tf_op jit(solution)/shard_map/spread_rows/pallas_call | solution.py:582
  402.8 8.9 %collective-permute-done.44 = bf16[128,1536]{1,0:T(8,128)(2,1)S(1)} collective-permute-done((bf16[128,1536]{1,0:T(8,128)(2,1)S(1)}, bf16[128,1536]{1,0:T(8,128)(2,1)S(1)}, u32[]{:S(2)}, u32[]{:S(2)}) %collective-permute-start.44) | collective-permute-done | bytes 393248 | tf_op jit(solution)/shard_map/ppermute | solution.py:289
  424.4 15.1 %weight_grads.3 = bf16[4,768,1536]{2,1,0:T(8,128)(2,1)} custom-call(bf16[4,1024,768]{2,1,0:T(8,128)(2,1)} %get-tuple-element.374.left_ref, bf16[4,1024,1536]{2,1,0:T(8,128)(2,1)} %get-tuple-element.375.right_ref), custom_call_target="tpu_custom_call" | custom-call | flops 1000000 | bytes 1000000 | tf_op jit(solution)/shard_map/weight_grads/pallas_call | solution.py:612
  449.3 16.1 %weight_grads.4 = bf16[2,1536,1536]{2,1,0:T(8,128)(2,1)} custom-call(bf16[4,1024,1536]{2,1,0:T(8,128)(2,1)} %get-tuple-element.389.left_ref, bf16[4,1024,1536]{2,1,0:T(8,128)(2,1)} %get-tuple-element.381.right_ref), custom_call_target="tpu_custom_call" | custom-call | flops 1000000 | bytes 1000000 | tf_op jit(solution)/shard_map/weight_grads/pallas_call | solution.py:612
  465.4 21.6 %collective-permute-done.50 = bf16[272,1536]{1,0:T(8,128)(2,1)} collective-permute-done((bf16[272,1536]{1,0:T(8,128)(2,1)}, bf16[272,1536]{1,0:T(8,128)(2,1)}, u32[]{:S(2)}, u32[]{:S(2)}) %collective-permute-start.50) | collective-permute-done | bytes 835616 | tf_op jit(solution)/shard_map/ppermute | solution.py:289
  496.1 14.9 %weight_grads.5 = bf16[2,1536,1536]{2,1,0:T(8,128)(2,1)} custom-call(bf16[4,1024,1536]{2,1,0:T(8,128)(2,1)} %get-tuple-element.389.left_ref, bf16[4,1024,1536]{2,1,0:T(8,128)(2,1)} %get-tuple-element.381.right_ref), custom_call_target="tpu_custom_call" | custom-call | flops 1000000 | bytes 1000000 | tf_op jit(solution)/shard_map/weight_grads/pallas_call | solution.py:612
  519.2 13.1 %collective-permute-done.48.left_ref = bf16[528,1536]{1,0:T(8,128)(2,1)S(1)} collective-permute-done((bf16[528,1536]{1,0:T(8,128)(2,1)}, bf16[528,1536]{1,0:T(8,128)(2,1)S(1)}, u32[]{:S(2)}, u32[]{:S(2)}) %collective-permute-start.48) | collective-permute-done | bytes 1622048 | tf_op jit(solution)/shard_map/ppermute | solution.py:289
  534.2 18.8 %attention_backward.2 = (bf16[256,1536]{1,0:T(8,128)(2,1)}, bf16[256,2176]{1,0:T(8,128)(2,1)}, bf16[256,1536]{1,0:T(8,128)(2,1)}, f32[8,1536]{1,0:T(8,128)}) custom-call(bf16[8,528,1536]{2,1,0:T(8,128)(2,1)} %get-tuple-element.398.own_ref, bf16[528,1536]{1,0:T(8,128)(2,1)} %copy-done.12, bf16[528,1536]{1,0:T(8,128)(2,1)} %collective-permute-done.49.right_ref, ...), custom_call_target="tpu_custom_call" | custom-call | flops 1000000 | bytes 1000000 | tf_op jit(solution)/shard_map/attention_backward/pallas_call | solution.py:470
  559.5 18.5 %attention_backward.3 = (bf16[256,1536]{1,0:T(8,128)(2,1)}, bf16[256,2176]{1,0:T(8,128)(2,1)}, bf16[256,1536]{1,0:T(8,128)(2,1)}, f32[8,1536]{1,0:T(8,128)}) custom-call(bf16[8,528,1536]{2,1,0:T(8,128)(2,1)} %get-tuple-element.407.own_ref, bf16[272,1536]{1,0:T(8,128)(2,1)} %collective-permute-done.56.left_ref, ...), custom_call_target="tpu_custom_call" | custom-call | flops 1000000 | bytes 1000000 | tf_op jit(solution)/shard_map/attention_backward/pallas_call | solution.py:470
  579.8 12.8 %attention_grads.1 = (bf16[2,384,3712]{2,1,0:T(8,128)(2,1)}, bf16[2,384,3712]{2,1,0:T(8,128)(2,1)}) custom-call(s32[2]{0:T(128)} %pad_add_fusion.core_ref, bf16[2,256,1536]{2,1,0:T(8,128)(2,1)} %get-tuple-element.418.xn1, bf16[2,256,1536]{2,1,0:T(8,128)(2,1)} %get-tuple-element.255.mixed_ref.mixed, bf16[256,2176]{1,0:T(8,128)(2,1)} %get-tuple-element.419.refs_0_, ...), custom_call_target="tpu_custom_call" | custom-call | flops 1000000 | bytes 1000000 | tf_op jit(solution)/shard_map/attention_grads/pallas_call | solution.py:736
  607.9 7.3 collective-permute-done.58
  635.8 8.4 %collective-permute-done.66 = bf16[96,3712]{1,0:T(8,128)(2,1)S(1)} collective-permute-done((bf16[96,3712]{1,0:T(8,128)(2,1)S(1)}, bf16[96,3712]{1,0:T(8,128)(2,1)S(1)}, u32[]{:S(2)}, u32[]{:S(2)}) %collective-permute-start.66) | collective-permute-done | bytes 712736 | tf_op jit(solution)/shard_map/ppermute | solution.py:289
  652.5 12.9 %collective-permute-done.68 = bf16[96,3712]{1,0:T(8,128)(2,1)S(1)} collective-permute-done((bf16[96,3712]{1,0:T(8,128)(2,1)S(1)}, bf16[96,3712]{1,0:T(8,128)(2,1)S(1)}, u32[]{:S(2)}, u32[]{:S(2)}) %collective-permute-start.68) | collective-permute-done | bytes 712736 | tf_op jit(solution)/shard_map/ppermute | solution.py:289
  671.3 14.8 %collective-permute-done.69 = bf16[96,3712]{1,0:T(8,128)(2,1)S(1)} collective-permute-done((bf16[96,3712]{1,0:T(8,128)(2,1)S(1)}, bf16[96,3712]{1,0:T(8,128)(2,1)S(1)}, u32[]{:S(2)}, u32[]{:S(2)}) %collective-permute-start.69) | collective-permute-done | bytes 712736 | tf_op jit(solution)/shard_map/ppermute | solution.py:289
  689.1 9.4 %collective-permute-done.60 = bf16[256,1536]{1,0:T(8,128)(2,1)} collective-permute-done((bf16[256,1536]{1,0:T(8,128)(2,1)}, bf16[256,1536]{1,0:T(8,128)(2,1)}, u32[]{:S(2)}, u32[]{:S(2)}) %collective-permute-start.60) | collective-permute-done | bytes 786464 | tf_op jit(solution)/shard_map/ppermute | solution.py:289
  699.0 6.9 collective-permute-done.71
  (363 shorter events, 274.5 us)
Async XLA Ops:
  7.2 691.2 %reduce-scatter.8.cloned.1.call-start = ((), (), s32[]{:S(2)}) async-start(), calls=%async_computation.5 | async-start | bytes 11796480 | tf_op jit(solution)/shard_map/reduce_scatter | solution.py:1021
  12.9 41.7 %collective-permute-start.1 = (bf16[384,2176]{1,0:T(8,128)(2,1)S(1)}, bf16[384,2176]{1,0:T(8,128)(2,1)}, u32[]{:S(2)}, u32[]{:S(2)}) collective-permute-start(bf16[384,2176]{1,0:T(8,128)(2,1)S(1)} %concatenate.44.refs_0_), channel_id=1, source_target_pairs={{0,16},{8,24},{16,0},{24,8},{1,17},{9,25},{17,1},{25,9},{2,18},{10... | collective-permute-start | bytes 5013512 | tf_op jit(solution)/shard_map/ppermute | solution.py:761
  16.2 38.4 %collective-permute-start.2 = (bf16[272,1536]{1,0:T(8,128)(2,1)S(1)}, bf16[272,1536]{1,0:T(8,128)(2,1)S(1)}, u32[]{:S(2)}, u32[]{:S(2)}) collective-permute-start(bf16[272,1536]{1,0:T(8,128)(2,1)S(1)} %pad_maximum_fusion.4.refs_0_), channel_id=1, source_target_pairs={{0,2},{2,4},{4,6},{6,7},{7,5},{5,3},{3,1},{1,0},{8,10},{10,12},{12... | collective-permute-start | bytes 2506760 | tf_op jit(solution)/shard_map/ppermute | solution.py:289
  17.9 36.7 %collective-permute-start.3 = (bf16[272,1536]{1,0:T(8,128)(2,1)S(1)}, bf16[272,1536]{1,0:T(8,128)(2,1)S(1)}, u32[]{:S(2)}, u32[]{:S(2)}) collective-permute-start(bf16[272,1536]{1,0:T(8,128)(2,1)S(1)} %pad_maximum_fusion.4.refs_0_), channel_id=1, source_target_pairs={{0,1},{2,0},{4,2},{6,4},{7,6},{5,7},{3,5},{1,3},{8,9},{10,8},{12,1... | collective-permute-start | bytes 2506760 | tf_op jit(solution)/shard_map/ppermute | solution.py:289
  18.3 35.0 %collective-permute-start.4 = (bf16[256,1536]{1,0:T(8,128)(2,1)S(1)}, bf16[256,1536]{1,0:T(8,128)(2,1)}, u32[]{:S(2)}, u32[]{:S(2)}) collective-permute-start(bf16[256,1536]{1,0:T(8,128)(2,1)S(1)} %get-tuple-element.234.refs_0_), channel_id=1, source_target_pairs={{0,2},{2,4},{4,6},{6,7},{7,5},{5,3},{3,1},{1,0},{8,10},{10,12},{12... | collective-permute-start | bytes 2359304 | tf_op jit(solution)/shard_map/ppermute | solution.py:289
  19.9 34.7 %collective-permute-start.5 = (bf16[256,1536]{1,0:T(8,128)(2,1)S(1)}, bf16[256,1536]{1,0:T(8,128)(2,1)}, u32[]{:S(2)}, u32[]{:S(2)}) collective-permute-start(bf16[256,1536]{1,0:T(8,128)(2,1)S(1)} %get-tuple-element.234.refs_0_), channel_id=1, source_target_pairs={{0,1},{2,0},{4,2},{6,4},{7,6},{5,7},{3,5},{1,3},{8,9},{10,8},{12,1... | collective-permute-start | bytes 2359304 | tf_op jit(solution)/shard_map/ppermute | solution.py:289
  56.8 38.8 %collective-permute-start.8 = (bf16[384,1536]{1,0:T(8,128)(2,1)}, bf16[384,1536]{1,0:T(8,128)(2,1)S(1)}, u32[]{:S(2)}, u32[]{:S(2)}) collective-permute-start(bf16[384,1536]{1,0:T(8,128)(2,1)} %refs_0_.4), channel_id=1, source_target_pairs={{0,16},{8,24},{16,0},{24,8},{1,17},{9,25},{17,1},{25,9},{2,18},{10... | collective-permute-start | bytes 3538952 | tf_op jit(solution)/shard_map/ppermute | solution.py:761
  58.7 34.6 %collective-permute-start.10 = (bf16[272,1536]{1,0:T(8,128)(2,1)}, bf16[272,1536]{1,0:T(8,128)(2,1)}, u32[]{:S(2)}, u32[]{:S(2)}) collective-permute-start(bf16[272,1536]{1,0:T(8,128)(2,1)} %copy-done.33), channel_id=1, source_target_pairs={{0,2},{2,4},{4,6},{6,7},{7,5},{5,3},{3,1},{1,0},{8,10},{10,12},{12... | collective-permute-start | bytes 2506760 | tf_op jit(solution)/shard_map/ppermute | solution.py:289
  60.3 33.9 %collective-permute-start.11 = (bf16[272,1536]{1,0:T(8,128)(2,1)}, bf16[272,1536]{1,0:T(8,128)(2,1)}, u32[]{:S(2)}, u32[]{:S(2)}) collective-permute-start(bf16[272,1536]{1,0:T(8,128)(2,1)} %copy-done.34), channel_id=1, source_target_pairs={{0,1},{2,0},{4,2},{6,4},{7,6},{5,7},{3,5},{1,3},{8,9},{10,8},{12,1... | collective-permute-start | bytes 2506760 | tf_op jit(solution)/shard_map/ppermute | solution.py:289
  78.3 31.9 %collective-permute-start.17 = (bf16[256,1536]{1,0:T(8,128)(2,1)}, bf16[256,1536]{1,0:T(8,128)(2,1)}, u32[]{:S(2)}, u32[]{:S(2)}) collective-permute-start(bf16[256,1536]{1,0:T(8,128)(2,1)} %collective-permute-done.15.refs_2_), channel_id=1, source_target_pairs={{0,2},{2,4},{4,6},{6,7},{7,5},{5,3},{3,1},{1,0},{8,10},{10,12},{12... | collective-permute-start | bytes 2359304 | tf_op jit(solution)/shard_map/ppermute | solution.py:289
  79.6 53.0 %collective-permute-start.7 = (bf16[384,1536]{1,0:T(8,128)(2,1)}, bf16[384,1536]{1,0:T(8,128)(2,1)S(1)}, u32[]{:S(2)}, u32[]{:S(2)}) collective-permute-start(bf16[384,1536]{1,0:T(8,128)(2,1)} %refs_0_.4), channel_id=1, source_target_pairs={{0,8},{8,0},{16,24},{24,16},{1,9},{9,1},{17,25},{25,17},{2,10},{10... | collective-permute-start | bytes 3538952 | tf_op jit(solution)/shard_map/ppermute | solution.py:762
  94.2 35.9 %collective-permute-start.13 = (bf16[272,1536]{1,0:T(8,128)(2,1)}, bf16[272,1536]{1,0:T(8,128)(2,1)S(1)}, u32[]{:S(2)}, u32[]{:S(2)}) collective-permute-start(bf16[272,1536]{1,0:T(8,128)(2,1)} %collective-permute-done.11.refs_7_), channel_id=1, source_target_pairs={{0,1},{2,0},{4,2},{6,4},{7,6},{5,7},{3,5},{1,3},{8,9},{10,8},{12,1... | collective-permute-start | bytes 2506760 | tf_op jit(solution)/shard_map/ppermute | solution.py:289
  95.6 34.8 %collective-permute-start.12 = (bf16[272,1536]{1,0:T(8,128)(2,1)}, bf16[272,1536]{1,0:T(8,128)(2,1)S(1)}, u32[]{:S(2)}, u32[]{:S(2)}) collective-permute-start(bf16[272,1536]{1,0:T(8,128)(2,1)} %collective-permute-done.10.refs_2_), channel_id=1, source_target_pairs={{0,2},{2,4},{4,6},{6,7},{7,5},{5,3},{3,1},{1,0},{8,10},{10,12},{12... | collective-permute-start | bytes 2506760 | tf_op jit(solution)/shard_map/ppermute | solution.py:289
  114.9 36.8 %collective-permute-start.19 = (bf16[128,1536]{1,0:T(8,128)(2,1)}, bf16[128,1536]{1,0:T(8,128)(2,1)}, u32[]{:S(2)}, u32[]{:S(2)}) collective-permute-start(bf16[128,1536]{1,0:T(8,128)(2,1)} %slice.318), channel_id=1, source_target_pairs={{0,2},{2,4},{4,6},{6,7},{7,5},{5,3},{3,1},{1,0},{8,10},{10,12},{12... | collective-permute-start | bytes 1179656 | tf_op jit(solution)/shard_map/ppermute | solution.py:289
  218.0 36.8 %collective-permute-start.30 = (bf16[272,1536]{1,0:T(8,128)(2,1)}, bf16[272,1536]{1,0:T(8,128)(2,1)S(1)}, u32[]{:S(2)}, u32[]{:S(2)}) collective-permute-start(bf16[272,1536]{1,0:T(8,128)(2,1)} %get-tuple-element.271.refs_0_.refs_1_), channel_id=1, source_target_pairs={{0,2},{2,4},{4,6},{6,7},{7,5},{5,3},{3,1},{1,0},{8,10},{10,12},{12... | collective-permute-start | bytes 2506760 | tf_op jit(solution)/shard_map/ppermute | solution.py:289
  220.4 34.5 %collective-permute-start.31 = (bf16[272,1536]{1,0:T(8,128)(2,1)}, bf16[272,1536]{1,0:T(8,128)(2,1)S(1)}, u32[]{:S(2)}, u32[]{:S(2)}) collective-permute-start(bf16[272,1536]{1,0:T(8,128)(2,1)} %get-tuple-element.271.refs_0_.refs_1_), channel_id=1, source_target_pairs={{0,1},{2,0},{4,2},{6,4},{7,6},{5,7},{3,5},{1,3},{8,9},{10,8},{12,1... | collective-permute-start | bytes 2506760 | tf_op jit(solution)/shard_map/ppermute | solution.py:289
  302.8 48.5 %collective-permute-start.36 = (bf16[272,1536]{1,0:T(8,128)(2,1)}, bf16[272,1536]{1,0:T(8,128)(2,1)S(1)}, u32[]{:S(2)}, u32[]{:S(2)}) collective-permute-start(bf16[272,1536]{1,0:T(8,128)(2,1)} %get-tuple-element.315), channel_id=1, source_target_pairs={{0,1},{2,0},{4,2},{6,4},{7,6},{5,7},{3,5},{1,3},{8,9},{10,8},{12,1... | collective-permute-start | bytes 2506760 | tf_op jit(solution)/shard_map/ppermute | solution.py:289
  304.5 46.7 %collective-permute-start.37 = (bf16[256,1536]{1,0:T(8,128)(2,1)}, bf16[256,1536]{1,0:T(8,128)(2,1)}, u32[]{:S(2)}, u32[]{:S(2)}) collective-permute-start(bf16[256,1536]{1,0:T(8,128)(2,1)} %get-tuple-element.316), channel_id=1, source_target_pairs={{0,2},{2,4},{4,6},{6,7},{7,5},{5,3},{3,1},{1,0},{8,10},{10,12},{12... | collective-permute-start | bytes 2359304 | tf_op jit(solution)/shard_map/ppermute | solution.py:289
  356.7 63.2 %collective-permute-start.40 = (bf16[528,1536]{1,0:T(8,128)(2,1)}, bf16[528,1536]{1,0:T(8,128)(2,1)S(1)}, u32[]{:S(2)}, u32[]{:S(2)}) collective-permute-start(bf16[528,1536]{1,0:T(8,128)(2,1)} %pad_maximum_fusion), channel_id=1, source_target_pairs={{0,1},{2,0},{4,2},{6,4},{7,6},{5,7},{3,5},{1,3},{8,9},{10,8},{12,1... | collective-permute-start | bytes 4866056 | tf_op jit(solution)/shard_map/ppermute | solution.py:289
  358.7 61.2 %collective-permute-start.41 = (bf16[528,1536]{1,0:T(8,128)(2,1)}, bf16[528,1536]{1,0:T(8,128)(2,1)S(1)}, u32[]{:S(2)}, u32[]{:S(2)}) collective-permute-start(bf16[528,1536]{1,0:T(8,128)(2,1)} %pad_maximum_fusion.1), channel_id=1, source_target_pairs={{0,2},{2,4},{4,6},{6,7},{7,5},{5,3},{3,1},{1,0},{8,10},{10,12},{12... | collective-permute-start | bytes 4866056 | tf_op jit(solution)/shard_map/ppermute | solution.py:289
  439.5 259.0 %reduce-scatter.4.cloned.1.call-start = ((), (), s32[]{:S(2)}) async-start(), calls=%async_computation.3 | async-start | bytes 11796480 | tf_op jit(solution)/shard_map/reduce_scatter | solution.py:1021
  440.8 47.2 %collective-permute-start.42 = (bf16[528,1536]{1,0:T(8,128)(2,1)S(1)}, bf16[528,1536]{1,0:T(8,128)(2,1)}, u32[]{:S(2)}, u32[]{:S(2)}) collective-permute-start(bf16[528,1536]{1,0:T(8,128)(2,1)S(1)} %copy-done.29), channel_id=1, source_target_pairs={{0,1},{2,0},{4,2},{6,4},{7,6},{5,7},{3,5},{1,3},{8,9},{10,8},{12,1... | collective-permute-start | bytes 4866056 | tf_op jit(solution)/shard_map/ppermute | solution.py:289
  442.2 45.8 %collective-permute-start.43 = (bf16[528,1536]{1,0:T(8,128)(2,1)S(1)}, bf16[528,1536]{1,0:T(8,128)(2,1)}, u32[]{:S(2)}, u32[]{:S(2)}) collective-permute-start(bf16[528,1536]{1,0:T(8,128)(2,1)S(1)} %copy-done.28), channel_id=1, source_target_pairs={{0,2},{2,4},{4,6},{6,7},{7,5},{5,3},{3,1},{1,0},{8,10},{10,12},{12... | collective-permute-start | bytes 4866056 | tf_op jit(solution)/shard_map/ppermute | solution.py:289
  446.9 40.0 %collective-permute-start.50 = (bf16[272,1536]{1,0:T(8,128)(2,1)}, bf16[272,1536]{1,0:T(8,128)(2,1)}, u32[]{:S(2)}, u32[]{:S(2)}) collective-permute-start(bf16[272,1536]{1,0:T(8,128)(2,1)} %get-tuple-element.378), channel_id=1, source_target_pairs={{0,1},{2,0},{4,2},{6,4},{7,6},{5,7},{3,5},{1,3},{8,9},{10,8},{12,1... | collective-permute-start | bytes 2506760 | tf_op jit(solution)/shard_map/ppermute | solution.py:289
  447.9 40.2 %collective-permute-start.51 = (bf16[272,1536]{1,0:T(8,128)(2,1)}, bf16[272,1536]{1,0:T(8,128)(2,1)}, u32[]{:S(2)}, u32[]{:S(2)}) collective-permute-start(bf16[272,1536]{1,0:T(8,128)(2,1)} %get-tuple-element.379), channel_id=1, source_target_pairs={{0,2},{2,4},{4,6},{6,7},{7,5},{5,3},{3,1},{1,0},{8,10},{10,12},{12... | collective-permute-start | bytes 2506760 | tf_op jit(solution)/shard_map/ppermute | solution.py:289
  488.1 210.3 %reduce-scatter.6.cloned.1.call-start = ((), (), s32[]{:S(2)}) async-start(), calls=%async_computation.4 | async-start | bytes 11796480 | tf_op jit(solution)/shard_map/reduce_scatter | solution.py:1021
  493.6 38.7 %collective-permute-start.48 = (bf16[528,1536]{1,0:T(8,128)(2,1)}, bf16[528,1536]{1,0:T(8,128)(2,1)S(1)}, u32[]{:S(2)}, u32[]{:S(2)}) collective-permute-start(bf16[528,1536]{1,0:T(8,128)(2,1)} %get-tuple-element.384), channel_id=1, source_target_pairs={{0,1},{2,0},{4,2},{6,4},{7,6},{5,7},{3,5},{1,3},{8,9},{10,8},{12,1... | collective-permute-start | bytes 4866056 | tf_op jit(solution)/shard_map/ppermute | solution.py:289
  496.1 38.1 %collective-permute-start.49 = (bf16[528,1536]{1,0:T(8,128)(2,1)}, bf16[528,1536]{1,0:T(8,128)(2,1)}, u32[]{:S(2)}, u32[]{:S(2)}) collective-permute-start(bf16[528,1536]{1,0:T(8,128)(2,1)} %get-tuple-element.385), channel_id=1, source_target_pairs={{0,2},{2,4},{4,6},{6,7},{7,5},{5,3},{3,1},{1,0},{8,10},{10,12},{12... | collective-permute-start | bytes 4866056 | tf_op jit(solution)/shard_map/ppermute | solution.py:289
  511.0 42.1 %collective-permute-start.52 = (bf16[128,1536]{1,0:T(8,128)(2,1)}, bf16[128,1536]{1,0:T(8,128)(2,1)S(1)}, u32[]{:S(2)}, u32[]{:S(2)}) collective-permute-start(bf16[128,1536]{1,0:T(8,128)(2,1)} %get-tuple-element.392), channel_id=1, source_target_pairs={{0,1},{2,0},{4,2},{6,4},{7,6},{5,7},{3,5},{1,3},{8,9},{10,8},{12,1... | collective-permute-start | bytes 1179656 | tf_op jit(solution)/shard_map/ppermute | solution.py:289
  513.9 39.1 %collective-permute-start.53 = (bf16[128,1536]{1,0:T(8,128)(2,1)}, bf16[128,1536]{1,0:T(8,128)(2,1)}, u32[]{:S(2)}, u32[]{:S(2)}) collective-permute-start(bf16[128,1536]{1,0:T(8,128)(2,1)} %get-tuple-element.393), channel_id=1, source_target_pairs={{0,2},{2,4},{4,6},{6,7},{7,5},{5,3},{3,1},{1,0},{8,10},{10,12},{12... | collective-permute-start | bytes 1179656 | tf_op jit(solution)/shard_map/ppermute | solution.py:289
  517.2 42.3 %collective-permute-start.56 = (bf16[272,1536]{1,0:T(8,128)(2,1)}, bf16[272,1536]{1,0:T(8,128)(2,1)}, u32[]{:S(2)}, u32[]{:S(2)}) collective-permute-start(bf16[272,1536]{1,0:T(8,128)(2,1)} %get-tuple-element.396), channel_id=1, source_target_pairs={{0,1},{2,0},{4,2},{6,4},{7,6},{5,7},{3,5},{1,3},{8,9},{10,8},{12,1... | collective-permute-start | bytes 2506760 | tf_op jit(solution)/shard_map/ppermute | solution.py:289
  669.3 29.1 %collective-permute-start.60 = (bf16[256,1536]{1,0:T(8,128)(2,1)}, bf16[256,1536]{1,0:T(8,128)(2,1)}, u32[]{:S(2)}, u32[]{:S(2)}) collective-permute-start(bf16[256,1536]{1,0:T(8,128)(2,1)} %get-tuple-element.413), channel_id=1, source_target_pairs={{0,1},{2,0},{4,2},{6,4},{7,6},{5,7},{3,5},{1,3},{8,9},{10,8},{12,1... | collective-permute-start | bytes 2359304 | tf_op jit(solution)/shard_map/ppermute | solution.py:289
  (105 other events, 1343.4 us)
Sparse Core Ops, SparseCore 0:
  439.6 77.8 reduce-scatter.7
  520.0 78.4 reduce-scatter.3
  601.7 78.4 reduce-scatter.5

commit v3 on v2

--- a/solution.py
+++ b/solution.py
@@ -838,8 +838,7 @@
     xn1, query, keyval, mixed, gates, gates_pack, gains = attention_forward(
         starts, tokens, seg_col, seg_row, routes, cos, sin, first_weights
     )
-    for ring in cot_rings:
-        ring.step(mixed)
+    cot_rings[0].step(mixed)
     out_weights = out_weights(mixed)
     hidden, xn2 = [], []
     for m in micros:
@@ -856,6 +855,7 @@
         )
         hidden.append(out[0])
         xn2.append(out[1])
+    cot_rings[1].step(xn2[0])
     for ring in cot_rings:
         ring.step()
     got = cot_rings[0].got + cot_rings[1].got
@@ -934,8 +934,7 @@
     while len(ring.from_left) < steps - 1:
         ring.step(*places, out_whole)
     ring.step(first.pick_grads())
-    ring.step(first.pick(early))
-    places[0] = after(places[0], second.pick_grads())
+    ring.step(first.pick(early), second.pick_grads())
     first.pick(late)
     ring_next.step(*ring.got)
     token = first.call(0)
@@ -1087,10 +1086,10 @@
 def reduce_packed(mine, other, my_spot, peers, dp_count, grad_w_in, grad_w_out, ring_results, widths):
     lines, span, columns = mine.shape
     swap = [(d, d ^ 1) for d in range(dp_count)]
-    while ring_results.at > 1:
-        ring_results.step()
+    other = after(other, *ring_results.got)
+    ring_results.step()
     total = add_rows(mine, lax.ppermute(other, "dp", swap))
-    total = after(total, *ring_results.got)
+    total = after(total, *ring_results.sent)
     piece = span // peers
     total = total.reshape(lines, peers, piece, columns)
 
@@ -1102,8 +1101,7 @@
     farthest = part(peers // 2)
     ring = RingScatter(part, (farthest[:half], farthest[half:]), peers)
     ring.step()
-    ring_results.step()
-    ring.step(*ring_results.sent)
+    ring.step(*ring_results.got)
     while ring.at > 0:
         ring.step()
     own, left, right = [held.astype(jnp.float32) for held in (part(0), ring.left, ring.right)]

time: 771 us -> 776 us (level)
    unnamed x118 -> x138, local copies, waits for them, and re-layouts: 12.4 us -> 17.5 us
where the time goes in v3:
time: 776 us; the launch traced here: 765 us
  Pallas kernels  297 us (38%)
  waiting for transfers between devices  262 us (34%)
  starting transfers between devices  81.6 us (11%)
  other arithmetic  63.2 us (8%)
  local copies, waits for them, and re-layouts  40.4 us (5%)
  between operations  20.2 us (3%)
    ppermute x72, waiting for transfers between devices, ring_step(): return lax.ppermute(part, 'expert', pairs)  248 us
    pallas_call x4, Pallas kernels, expert_pass(): pl.pallas_call(functools.partial(expert_kernel, sources), grid=(count,),...  97.3 us
    pallas_call x11, Pallas kernels, block_call(): pl.pallas_call(kernel, grid_spec=pltpu.PrefetchScalarGridSpec(num_scalar_...  86.2 us
    ppermute x72, starting transfers between devices, ring_step(): return lax.ppermute(part, 'expert', pairs)  77.2 us
    pallas_call x3, Pallas kernels, weight_grads(): pl.pallas_call(weight_grad_kernel, grid=(count, height // tile), in_specs...  46.2 us
    convert_element_type x17, other arithmetic, add_rows(): (left.astype(jnp.float32) + right.astype(jnp.float32)).astype(jnp.bfloat16)  36.3 us
    pallas_call x2, Pallas kernels, spread_rows(): pl.pallas_call(functools.partial(spread_kernel, sources // 2 - base, span...  28.1 us
    unnamed x138, local copies, waits for them, and re-layouts  17.5 us
  transfers between devices with their start and end apart: 83, of which 41 were waited for; matrix products, arithmetic and copies ran while one was open for 10% of the time, Pallas kernels for 38%

profile of v3, /device:TPU:0, one launch (start us, length us, event | category | flops | bytes accessed | tf_op | source)
XLA Modules:
  0.0 765.5 jit_solution(15329094984766506183)
XLA Ops:
  20.3 32.9 %collective-permute-done.4.refs_1_ = bf16[256,1536]{1,0:T(8,128)(2,1)S(1)} collective-permute-done((bf16[256,1536]{1,0:T(8,128)(2,1)S(1)}, bf16[256,1536]{1,0:T(8,128)(2,1)S(1)}, u32[]{:S(2)}, u32[]{:S(2)}) %collective-permute-start.4) | collective-permute-done | bytes 786464 | tf_op jit(solution)/shard_map/ppermute | solution.py:289
  61.5 14.2 %attention_forward.1 = (bf16[2,256,1536]{2,1,0:T(8,128)(2,1)}, bf16[2,256,1536]{2,1,0:T(8,128)(2,1)}, bf16[2,256,512]{2,1,0:T(8,128)(2,1)}, bf16[2,256,1536]{2,1...) custom-call(s32[4]{0:T(128)} %add_multiply_fusion.starts_ref, ...), custom_call_target="tpu_custom_call" | custom-call | flops 1000000 | bytes 1000000 | tf_op jit(solution)/shard_map/attention_forward/pallas_call | solution.py:645
  87.0 10.4 %collective-permute-done.13.refs_6_ = bf16[272,1536]{1,0:T(8,128)(2,1)} collective-permute-done((bf16[272,1536]{1,0:T(8,128)(2,1)}, bf16[272,1536]{1,0:T(8,128)(2,1)}, u32[]{:S(2)}, u32[]{:S(2)}) %collective-permute-start.13) | collective-permute-done | bytes 835616 | tf_op jit(solution)/shard_map/ppermute | solution.py:289
  100.3 16.6 %collective-permute-done.12.refs_3_ = bf16[272,1536]{1,0:T(8,128)(2,1)S(1)} collective-permute-done((bf16[272,1536]{1,0:T(8,128)(2,1)}, bf16[272,1536]{1,0:T(8,128)(2,1)S(1)}, u32[]{:S(2)}, u32[]{:S(2)}) %collective-permute-start.12) | collective-permute-done | bytes 835616 | tf_op jit(solution)/shard_map/ppermute | solution.py:289
  120.9 6.8 hidden_rows.2
  138.5 10.0 %collective-permute-done.20.refs_3_ = bf16[256,1536]{1,0:T(8,128)(2,1)S(1)} collective-permute-done((bf16[256,1536]{1,0:T(8,128)(2,1)}, bf16[256,1536]{1,0:T(8,128)(2,1)S(1)}, u32[]{:S(2)}, u32[]{:S(2)}) %collective-permute-start.20) | collective-permute-done | bytes 786464 | tf_op jit(solution)/shard_map/ppermute | solution.py:289
  154.5 18.4 %collective-permute-done.22.refs_4_ = bf16[128,1536]{1,0:T(8,128)(2,1)S(1)} collective-permute-done((bf16[128,1536]{1,0:T(8,128)(2,1)S(1)}, bf16[128,1536]{1,0:T(8,128)(2,1)S(1)}, u32[]{:S(2)}, u32[]{:S(2)}) %collective-permute-start.22) | collective-permute-done | bytes 393248 | tf_op jit(solution)/shard_map/ppermute | solution.py:289
  174.4 7.0 join_blocks.2.refs_0_
  189.2 6.2 pick_rows.6
  195.4 10.1 %collective-permute-done.24.refs_4_.refs_5_ = bf16[272,1536]{1,0:T(8,128)(2,1)S(1)} collective-permute-done((bf16[272,1536]{1,0:T(8,128)(2,1)S(1)}, bf16[272,1536]{1,0:T(8,128)(2,1)S(1)}, u32[]{:S(2)}, u32[]{:S(2)}) %collective-permute-start.24) | collective-permute-done | bytes 835616 | tf_op jit(solution)/shard_map/ppermute | solution.py:289
  209.4 6.1 pick_rows.8
  227.8 6.8 hidden_rows.3
  243.1 24.3 %expert_pass.4 = (bf16[8,256,1536]{2,1,0:T(8,128)(2,1)}, bf16[8,256,1536]{2,1,0:T(8,128)(2,1)}, f32[4,512,1]{2,1,0:T(8,128)}, bf16[4,1024,1536]{2,1,0:T(8,128)(2...) custom-call(bf16[256,1536]{1,0:T(8,128)(2,1)} %get-tuple-element.297.refs_0_, ...), custom_call_target="tpu_custom_call" | custom-call | flops 1000000 | bytes 1000000 | tf_op jit(solution)/shard_map/expert_pass/pallas_call | solution.py:435
  269.7 24.3 %expert_pass.5 = (bf16[8,256,1536]{2,1,0:T(8,128)(2,1)}, bf16[8,256,1536]{2,1,0:T(8,128)(2,1)}, f32[4,512,1]{2,1,0:T(8,128)}, bf16[4,1024,1536]{2,1,0:T(8,128)(2...) custom-call(bf16[256,1536]{1,0:T(8,128)(2,1)} %get-tuple-element.297, ...), custom_call_target="tpu_custom_call", output_to_operand_aliasing={{0}: (26, {}), {1}: (27, {}), {2}: (28, {}), {3}: (29, {}),... | custom-call | flops 1000000 | bytes 1000000 | tf_op jit(solution)/shard_map/expert_pass/pallas_call | solution.py:435
  297.0 14.0 %spread_rows.2 = (bf16[8,528,1536]{2,1,0:T(8,128)(2,1)}, bf16[272,1536]{1,0:T(8,128)(2,1)}, bf16[256,1536]{1,0:T(8,128)(2,1)}) custom-call(s32[1]{0:T(128)} %bitcast.8.first_ref, bf16[8,256,256]{2,1,0:T(8,128)(2,1)} %get-tuple-element.296.place_ref, bf16[8,256,1536]{2,1,0:T(8,128)(2,1)} %get-tuple-element.304.rows_ref, ...), custom_call_target="tpu_custom_call" | custom-call | flops 1000000 | bytes 1000000 | tf_op jit(solution)/shard_map/spread_rows/pallas_call | solution.py:582
  323.1 15.6 %collective-permute-done.38.refs_2_ = bf16[128,1536]{1,0:T(8,128)(2,1)S(1)} collective-permute-done((bf16[128,1536]{1,0:T(8,128)(2,1)S(1)}, bf16[128,1536]{1,0:T(8,128)(2,1)S(1)}, u32[]{:S(2)}, u32[]{:S(2)}) %collective-permute-start.38) | collective-permute-done | bytes 393248 | tf_op jit(solution)/shard_map/ppermute | solution.py:289
  344.4 24.4 %expert_pass.6 = (bf16[8,256,1536]{2,1,0:T(8,128)(2,1)}, bf16[8,256,1536]{2,1,0:T(8,128)(2,1)}, f32[4,512,1]{2,1,0:T(8,128)}, bf16[4,1024,1536]{2,1,0:T(8,128)(2...) custom-call(bf16[256,1536]{1,0:T(8,128)(2,1)} %get-tuple-element.350, ...), custom_call_target="tpu_custom_call", output_to_operand_aliasing={{3}: (26, {}), {4}: (27, {}), {5}: (28, {}), {6}: (29, {})} | custom-call | flops 1000000 | bytes 1000000 | tf_op jit(solution)/shard_map/expert_pass/pallas_call | solution.py:435
  376.4 24.3 %expert_pass.7 = (bf16[8,256,1536]{2,1,0:T(8,128)(2,1)}, bf16[8,256,1536]{2,1,0:T(8,128)(2,1)}, f32[4,512,1]{2,1,0:T(8,128)}, bf16[4,1024,1536]{2,1,0:T(8,128)(2...) custom-call(bf16[256,1536]{1,0:T(8,128)(2,1)} %get-tuple-element.350, ...), custom_call_target="tpu_custom_call", output_to_operand_aliasing={{0}: (26, {}), {1}: (27, {}), {2}: (28, {}), {3}: (29, {}),... | custom-call | flops 1000000 | bytes 1000000 | tf_op jit(solution)/shard_map/expert_pass/pallas_call | solution.py:435
  400.7 14.1 %spread_rows.3 = (bf16[8,528,1536]{2,1,0:T(8,128)(2,1)}, bf16[128,1536]{1,0:T(8,128)(2,1)}, bf16[144,1536]{1,0:T(8,128)(2,1)}, bf16[128,1536]{1,0:T(8,128)(2,1)}, bf16[128,1536]{1,0:T(8,128)(2,1)}) custom-call(s32[1]{0:T(128)} %bitcast.8.first_ref, bf16[8,256,256]{2,1,0:T(8,128)(2,1)} %get-tuple-element.522.place_ref, ...), custom_call_target="tpu_custom_call" | custom-call | flops 1000000 | bytes 1000000 | tf_op jit(solution)/shard_map/spread_rows/pallas_call | solution.py:582
  439.3 15.1 %weight_grads.3 = bf16[4,768,1536]{2,1,0:T(8,128)(2,1)} custom-call(bf16[4,1024,768]{2,1,0:T(8,128)(2,1)} %get-tuple-element.373.left_ref, bf16[4,1024,1536]{2,1,0:T(8,128)(2,1)} %get-tuple-element.374.right_ref), custom_call_target="tpu_custom_call" | custom-call | flops 1000000 | bytes 1000000 | tf_op jit(solution)/shard_map/weight_grads/pallas_call | solution.py:612
  464.4 16.1 %weight_grads.4 = bf16[2,1536,1536]{2,1,0:T(8,128)(2,1)} custom-call(bf16[4,1024,1536]{2,1,0:T(8,128)(2,1)} %get-tuple-element.388.left_ref, bf16[4,1024,1536]{2,1,0:T(8,128)(2,1)} %get-tuple-element.380.right_ref), custom_call_target="tpu_custom_call" | custom-call | flops 1000000 | bytes 1000000 | tf_op jit(solution)/shard_map/weight_grads/pallas_call | solution.py:612
  480.4 21.9 %collective-permute-done.50 = bf16[272,1536]{1,0:T(8,128)(2,1)} collective-permute-done((bf16[272,1536]{1,0:T(8,128)(2,1)}, bf16[272,1536]{1,0:T(8,128)(2,1)}, u32[]{:S(2)}, u32[]{:S(2)}) %collective-permute-start.50) | collective-permute-done | bytes 835616 | tf_op jit(solution)/shard_map/ppermute | solution.py:289
  512.6 15.1 %weight_grads.5 = bf16[2,1536,1536]{2,1,0:T(8,128)(2,1)} custom-call(bf16[4,1024,1536]{2,1,0:T(8,128)(2,1)} %get-tuple-element.388.left_ref, bf16[4,1024,1536]{2,1,0:T(8,128)(2,1)} %get-tuple-element.380.right_ref), custom_call_target="tpu_custom_call" | custom-call | flops 1000000 | bytes 1000000 | tf_op jit(solution)/shard_map/weight_grads/pallas_call | solution.py:612
  534.9 14.0 %collective-permute-done.48.left_ref = bf16[528,1536]{1,0:T(8,128)(2,1)S(1)} collective-permute-done((bf16[528,1536]{1,0:T(8,128)(2,1)}, bf16[528,1536]{1,0:T(8,128)(2,1)S(1)}, u32[]{:S(2)}, u32[]{:S(2)}) %collective-permute-start.48) | collective-permute-done | bytes 1622048 | tf_op jit(solution)/shard_map/ppermute | solution.py:289
  551.3 18.3 %attention_backward.2 = (bf16[256,1536]{1,0:T(8,128)(2,1)}, bf16[256,2176]{1,0:T(8,128)(2,1)}, bf16[256,1536]{1,0:T(8,128)(2,1)}, f32[8,1536]{1,0:T(8,128)}) custom-call(bf16[8,528,1536]{2,1,0:T(8,128)(2,1)} %get-tuple-element.397.own_ref, bf16[528,1536]{1,0:T(8,128)(2,1)} %copy-done.12, bf16[528,1536]{1,0:T(8,128)(2,1)} %collective-permute-done.49.right_ref, ...), custom_call_target="tpu_custom_call" | custom-call | flops 1000000 | bytes 1000000 | tf_op jit(solution)/shard_map/attention_backward/pallas_call | solution.py:470
  574.2 18.6 %attention_backward.3 = (bf16[256,1536]{1,0:T(8,128)(2,1)}, bf16[256,2176]{1,0:T(8,128)(2,1)}, bf16[256,1536]{1,0:T(8,128)(2,1)}, f32[8,1536]{1,0:T(8,128)}) custom-call(bf16[8,528,1536]{2,1,0:T(8,128)(2,1)} %get-tuple-element.406.own_ref, bf16[272,1536]{1,0:T(8,128)(2,1)} %collective-permute-done.56.left_ref, ...), custom_call_target="tpu_custom_call" | custom-call | flops 1000000 | bytes 1000000 | tf_op jit(solution)/shard_map/attention_backward/pallas_call | solution.py:470
  599.7 12.7 %attention_grads.1 = (bf16[2,384,3712]{2,1,0:T(8,128)(2,1)}, bf16[2,384,3712]{2,1,0:T(8,128)(2,1)}) custom-call(s32[2]{0:T(128)} %pad_add_fusion.core_ref, bf16[2,256,1536]{2,1,0:T(8,128)(2,1)} %get-tuple-element.417.xn1, bf16[2,256,1536]{2,1,0:T(8,128)(2,1)} %get-tuple-element.247.mixed_ref.mixed, bf16[256,2176]{1,0:T(8,128)(2,1)} %get-tuple-element.418.refs_0_, ...), custom_call_target="tpu_custom_call" | custom-call | flops 1000000 | bytes 1000000 | tf_op jit(solution)/shard_map/attention_grads/pallas_call | solution.py:736
  622.1 7.5 add_convert_fusion
  653.6 9.5 %collective-permute-done.66 = bf16[96,3712]{1,0:T(8,128)(2,1)S(1)} collective-permute-done((bf16[96,3712]{1,0:T(8,128)(2,1)S(1)}, bf16[96,3712]{1,0:T(8,128)(2,1)S(1)}, u32[]{:S(2)}, u32[]{:S(2)}) %collective-permute-start.66) | collective-permute-done | bytes 712736 | tf_op jit(solution)/shard_map/ppermute | solution.py:289
  671.7 14.2 %collective-permute-done.68 = bf16[96,3712]{1,0:T(8,128)(2,1)S(1)} collective-permute-done((bf16[96,3712]{1,0:T(8,128)(2,1)S(1)}, bf16[96,3712]{1,0:T(8,128)(2,1)S(1)}, u32[]{:S(2)}, u32[]{:S(2)}) %collective-permute-start.68) | collective-permute-done | bytes 712736 | tf_op jit(solution)/shard_map/ppermute | solution.py:289
  688.5 13.4 %collective-permute-done.69 = bf16[96,3712]{1,0:T(8,128)(2,1)S(1)} collective-permute-done((bf16[96,3712]{1,0:T(8,128)(2,1)S(1)}, bf16[96,3712]{1,0:T(8,128)(2,1)S(1)}, u32[]{:S(2)}, u32[]{:S(2)}) %collective-permute-start.69) | collective-permute-done | bytes 712736 | tf_op jit(solution)/shard_map/ppermute | solution.py:289
  705.4 6.8 collective-permute-done.71
  (383 shorter events, 275.7 us)
Async XLA Ops:
  7.2 697.5 %reduce-scatter.8.cloned.1.call-start = ((), (), s32[]{:S(2)}) async-start(), calls=%async_computation.5 | async-start | bytes 11796480 | tf_op jit(solution)/shard_map/reduce_scatter | solution.py:1020
  12.9 41.6 %collective-permute-start.1 = (bf16[384,2176]{1,0:T(8,128)(2,1)S(1)}, bf16[384,2176]{1,0:T(8,128)(2,1)}, u32[]{:S(2)}, u32[]{:S(2)}) collective-permute-start(bf16[384,2176]{1,0:T(8,128)(2,1)S(1)} %concatenate.44.refs_0_), channel_id=1, source_target_pairs={{0,16},{8,24},{16,0},{24,8},{1,17},{9,25},{17,1},{25,9},{2,18},{10... | collective-permute-start | bytes 5013512 | tf_op jit(solution)/shard_map/ppermute | solution.py:761
  16.2 38.3 %collective-permute-start.2 = (bf16[272,1536]{1,0:T(8,128)(2,1)S(1)}, bf16[272,1536]{1,0:T(8,128)(2,1)}, u32[]{:S(2)}, u32[]{:S(2)}) collective-permute-start(bf16[272,1536]{1,0:T(8,128)(2,1)S(1)} %pad_maximum_fusion.4.refs_0_), channel_id=1, source_target_pairs={{0,2},{2,4},{4,6},{6,7},{7,5},{5,3},{3,1},{1,0},{8,10},{10,12},{12... | collective-permute-start | bytes 2506760 | tf_op jit(solution)/shard_map/ppermute | solution.py:289
  17.9 36.6 %collective-permute-start.3 = (bf16[272,1536]{1,0:T(8,128)(2,1)S(1)}, bf16[272,1536]{1,0:T(8,128)(2,1)}, u32[]{:S(2)}, u32[]{:S(2)}) collective-permute-start(bf16[272,1536]{1,0:T(8,128)(2,1)S(1)} %pad_maximum_fusion.4.refs_0_), channel_id=1, source_target_pairs={{0,1},{2,0},{4,2},{6,4},{7,6},{5,7},{3,5},{1,3},{8,9},{10,8},{12,1... | collective-permute-start | bytes 2506760 | tf_op jit(solution)/shard_map/ppermute | solution.py:289
  18.3 34.9 %collective-permute-start.4 = (bf16[256,1536]{1,0:T(8,128)(2,1)S(1)}, bf16[256,1536]{1,0:T(8,128)(2,1)S(1)}, u32[]{:S(2)}, u32[]{:S(2)}) collective-permute-start(bf16[256,1536]{1,0:T(8,128)(2,1)S(1)} %get-tuple-element.234.refs_0_), channel_id=1, source_target_pairs={{0,2},{2,4},{4,6},{6,7},{7,5},{5,3},{3,1},{1,0},{8,10},{10,12},{12... | collective-permute-start | bytes 2359304 | tf_op jit(solution)/shard_map/ppermute | solution.py:289
  19.9 34.6 %collective-permute-start.5 = (bf16[256,1536]{1,0:T(8,128)(2,1)S(1)}, bf16[256,1536]{1,0:T(8,128)(2,1)S(1)}, u32[]{:S(2)}, u32[]{:S(2)}) collective-permute-start(bf16[256,1536]{1,0:T(8,128)(2,1)S(1)} %get-tuple-element.234.refs_0_), channel_id=1, source_target_pairs={{0,1},{2,0},{4,2},{6,4},{7,6},{5,7},{3,5},{1,3},{8,9},{10,8},{12,1... | collective-permute-start | bytes 2359304 | tf_op jit(solution)/shard_map/ppermute | solution.py:289
  56.7 28.0 %collective-permute-start.8 = (bf16[384,1536]{1,0:T(8,128)(2,1)}, bf16[384,1536]{1,0:T(8,128)(2,1)S(1)}, u32[]{:S(2)}, u32[]{:S(2)}) collective-permute-start(bf16[384,1536]{1,0:T(8,128)(2,1)} %refs_0_.4), channel_id=1, source_target_pairs={{0,16},{8,24},{16,0},{24,8},{1,17},{9,25},{17,1},{25,9},{2,18},{10... | collective-permute-start | bytes 3538952 | tf_op jit(solution)/shard_map/ppermute | solution.py:761
  77.6 40.6 %collective-permute-start.7 = (bf16[384,1536]{1,0:T(8,128)(2,1)}, bf16[384,1536]{1,0:T(8,128)(2,1)S(1)}, u32[]{:S(2)}, u32[]{:S(2)}) collective-permute-start(bf16[384,1536]{1,0:T(8,128)(2,1)} %refs_0_.4), channel_id=1, source_target_pairs={{0,8},{8,0},{16,24},{24,16},{1,9},{9,1},{17,25},{25,17},{2,10},{10... | collective-permute-start | bytes 3538952 | tf_op jit(solution)/shard_map/ppermute | solution.py:762
  78.9 48.8 %collective-permute-start.18 = (bf16[256,1536]{1,0:T(8,128)(2,1)}, bf16[256,1536]{1,0:T(8,128)(2,1)}, u32[]{:S(2)}, u32[]{:S(2)}) collective-permute-start(bf16[256,1536]{1,0:T(8,128)(2,1)} %copy-done.44), channel_id=1, source_target_pairs={{0,2},{2,4},{4,6},{6,7},{7,5},{5,3},{3,1},{1,0},{8,10},{10,12},{12... | collective-permute-start | bytes 2359304 | tf_op jit(solution)/shard_map/ppermute | solution.py:289
  84.6 35.3 %collective-permute-start.9 = (bf16[384,1536]{1,0:T(8,128)(2,1)S(1)}, bf16[384,1536]{1,0:T(8,128)(2,1)S(1)}, u32[]{:S(2)}, u32[]{:S(2)}) collective-permute-start(bf16[384,1536]{1,0:T(8,128)(2,1)S(1)} %collective-permute-done.8.refs_2_), channel_id=1, source_target_pairs={{0,8},{8,0},{16,24},{24,16},{1,9},{9,1},{17,25},{25,17},{2,10},{10... | collective-permute-start | bytes 3538952 | tf_op jit(solution)/shard_map/ppermute | solution.py:768
  84.6 32.3 %collective-permute-start.12 = (bf16[272,1536]{1,0:T(8,128)(2,1)}, bf16[272,1536]{1,0:T(8,128)(2,1)S(1)}, u32[]{:S(2)}, u32[]{:S(2)}) collective-permute-start(bf16[272,1536]{1,0:T(8,128)(2,1)} %collective-permute-done.10.refs_2_), channel_id=1, source_target_pairs={{0,2},{2,4},{4,6},{6,7},{7,5},{5,3},{3,1},{1,0},{8,10},{10,12},{12... | collective-permute-start | bytes 2506760 | tf_op jit(solution)/shard_map/ppermute | solution.py:289
  97.3 30.4 %collective-permute-start.19 = (bf16[256,1536]{1,0:T(8,128)(2,1)}, bf16[256,1536]{1,0:T(8,128)(2,1)}, u32[]{:S(2)}, u32[]{:S(2)}) collective-permute-start(bf16[256,1536]{1,0:T(8,128)(2,1)} %copy-done.45), channel_id=1, source_target_pairs={{0,1},{2,0},{4,2},{6,4},{7,6},{5,7},{3,5},{1,3},{8,9},{10,8},{12,1... | collective-permute-start | bytes 2359304 | tf_op jit(solution)/shard_map/ppermute | solution.py:289
  118.3 36.2 %collective-permute-start.17 = (bf16[128,1536]{1,0:T(8,128)(2,1)}, bf16[128,1536]{1,0:T(8,128)(2,1)}, u32[]{:S(2)}, u32[]{:S(2)}) collective-permute-start(bf16[128,1536]{1,0:T(8,128)(2,1)} %slice.309), channel_id=1, source_target_pairs={{0,2},{2,4},{4,6},{6,7},{7,5},{5,3},{3,1},{1,0},{8,10},{10,12},{12... | collective-permute-start | bytes 1179656 | tf_op jit(solution)/shard_map/ppermute | solution.py:289
  129.8 57.2 %collective-permute-start.15 = (bf16[272,1536]{1,0:T(8,128)(2,1)}, bf16[272,1536]{1,0:T(8,128)(2,1)S(1)}, u32[]{:S(2)}, u32[]{:S(2)}) collective-permute-start(bf16[272,1536]{1,0:T(8,128)(2,1)} %get-tuple-element.250.refs_0_.refs_1_), channel_id=1, source_target_pairs={{0,2},{2,4},{4,6},{6,7},{7,5},{5,3},{3,1},{1,0},{8,10},{10,12},{12... | collective-permute-start | bytes 2506760 | tf_op jit(solution)/shard_map/ppermute | solution.py:289
  131.4 55.6 %collective-permute-start.16 = (bf16[272,1536]{1,0:T(8,128)(2,1)}, bf16[272,1536]{1,0:T(8,128)(2,1)S(1)}, u32[]{:S(2)}, u32[]{:S(2)}) collective-permute-start(bf16[272,1536]{1,0:T(8,128)(2,1)} %get-tuple-element.250.refs_0_.refs_1_), channel_id=1, source_target_pairs={{0,1},{2,0},{4,2},{6,4},{7,6},{5,7},{3,5},{1,3},{8,9},{10,8},{12,1... | collective-permute-start | bytes 2506760 | tf_op jit(solution)/shard_map/ppermute | solution.py:289
  236.7 30.7 %collective-permute-start.30 = (bf16[272,1536]{1,0:T(8,128)(2,1)}, bf16[272,1536]{1,0:T(8,128)(2,1)S(1)}, u32[]{:S(2)}, u32[]{:S(2)}) collective-permute-start(bf16[272,1536]{1,0:T(8,128)(2,1)} %get-tuple-element.270.refs_0_.refs_1_), channel_id=1, source_target_pairs={{0,2},{2,4},{4,6},{6,7},{7,5},{5,3},{3,1},{1,0},{8,10},{10,12},{12... | collective-permute-start | bytes 2506760 | tf_op jit(solution)/shard_map/ppermute | solution.py:289
  237.3 30.1 %collective-permute-start.31 = (bf16[272,1536]{1,0:T(8,128)(2,1)}, bf16[272,1536]{1,0:T(8,128)(2,1)S(1)}, u32[]{:S(2)}, u32[]{:S(2)}) collective-permute-start(bf16[272,1536]{1,0:T(8,128)(2,1)} %get-tuple-element.270.refs_0_.refs_1_), channel_id=1, source_target_pairs={{0,1},{2,0},{4,2},{6,4},{7,6},{5,7},{3,5},{1,3},{8,9},{10,8},{12,1... | collective-permute-start | bytes 2506760 | tf_op jit(solution)/shard_map/ppermute | solution.py:289
  316.1 52.7 %collective-permute-start.36 = (bf16[272,1536]{1,0:T(8,128)(2,1)}, bf16[272,1536]{1,0:T(8,128)(2,1)S(1)}, u32[]{:S(2)}, u32[]{:S(2)}) collective-permute-start(bf16[272,1536]{1,0:T(8,128)(2,1)} %get-tuple-element.314), channel_id=1, source_target_pairs={{0,1},{2,0},{4,2},{6,4},{7,6},{5,7},{3,5},{1,3},{8,9},{10,8},{12,1... | collective-permute-start | bytes 2506760 | tf_op jit(solution)/shard_map/ppermute | solution.py:289
  317.6 51.1 %collective-permute-start.37 = (bf16[256,1536]{1,0:T(8,128)(2,1)}, bf16[256,1536]{1,0:T(8,128)(2,1)}, u32[]{:S(2)}, u32[]{:S(2)}) collective-permute-start(bf16[256,1536]{1,0:T(8,128)(2,1)} %get-tuple-element.315), channel_id=1, source_target_pairs={{0,2},{2,4},{4,6},{6,7},{7,5},{5,3},{3,1},{1,0},{8,10},{10,12},{12... | collective-permute-start | bytes 2359304 | tf_op jit(solution)/shard_map/ppermute | solution.py:289
  374.2 60.7 %collective-permute-start.40 = (bf16[528,1536]{1,0:T(8,128)(2,1)}, bf16[528,1536]{1,0:T(8,128)(2,1)S(1)}, u32[]{:S(2)}, u32[]{:S(2)}) collective-permute-start(bf16[528,1536]{1,0:T(8,128)(2,1)} %pad_maximum_fusion), channel_id=1, source_target_pairs={{0,1},{2,0},{4,2},{6,4},{7,6},{5,7},{3,5},{1,3},{8,9},{10,8},{12,1... | collective-permute-start | bytes 4866056 | tf_op jit(solution)/shard_map/ppermute | solution.py:289
  375.8 59.1 %collective-permute-start.41 = (bf16[528,1536]{1,0:T(8,128)(2,1)}, bf16[528,1536]{1,0:T(8,128)(2,1)S(1)}, u32[]{:S(2)}, u32[]{:S(2)}) collective-permute-start(bf16[528,1536]{1,0:T(8,128)(2,1)} %pad_maximum_fusion.1), channel_id=1, source_target_pairs={{0,2},{2,4},{4,6},{6,7},{7,5},{5,3},{3,1},{1,0},{8,10},{10,12},{12... | collective-permute-start | bytes 4866056 | tf_op jit(solution)/shard_map/ppermute | solution.py:289
  454.4 250.2 %reduce-scatter.4.cloned.1.call-start = ((), (), s32[]{:S(2)}) async-start(), calls=%async_computation.3 | async-start | bytes 11796480 | tf_op jit(solution)/shard_map/reduce_scatter | solution.py:1020
  455.8 48.0 %collective-permute-start.42 = (bf16[528,1536]{1,0:T(8,128)(2,1)S(1)}, bf16[528,1536]{1,0:T(8,128)(2,1)}, u32[]{:S(2)}, u32[]{:S(2)}) collective-permute-start(bf16[528,1536]{1,0:T(8,128)(2,1)S(1)} %copy-done.30), channel_id=1, source_target_pairs={{0,1},{2,0},{4,2},{6,4},{7,6},{5,7},{3,5},{1,3},{8,9},{10,8},{12,1... | collective-permute-start | bytes 4866056 | tf_op jit(solution)/shard_map/ppermute | solution.py:289
  457.8 46.1 %collective-permute-start.43 = (bf16[528,1536]{1,0:T(8,128)(2,1)S(1)}, bf16[528,1536]{1,0:T(8,128)(2,1)}, u32[]{:S(2)}, u32[]{:S(2)}) collective-permute-start(bf16[528,1536]{1,0:T(8,128)(2,1)S(1)} %copy-done.29), channel_id=1, source_target_pairs={{0,2},{2,4},{4,6},{6,7},{7,5},{5,3},{3,1},{1,0},{8,10},{10,12},{12... | collective-permute-start | bytes 4866056 | tf_op jit(solution)/shard_map/ppermute | solution.py:289
  461.9 40.4 %collective-permute-start.50 = (bf16[272,1536]{1,0:T(8,128)(2,1)}, bf16[272,1536]{1,0:T(8,128)(2,1)}, u32[]{:S(2)}, u32[]{:S(2)}) collective-permute-start(bf16[272,1536]{1,0:T(8,128)(2,1)} %get-tuple-element.377), channel_id=1, source_target_pairs={{0,1},{2,0},{4,2},{6,4},{7,6},{5,7},{3,5},{1,3},{8,9},{10,8},{12,1... | collective-permute-start | bytes 2506760 | tf_op jit(solution)/shard_map/ppermute | solution.py:289
  464.0 39.9 %collective-permute-start.51 = (bf16[272,1536]{1,0:T(8,128)(2,1)}, bf16[272,1536]{1,0:T(8,128)(2,1)}, u32[]{:S(2)}, u32[]{:S(2)}) collective-permute-start(bf16[272,1536]{1,0:T(8,128)(2,1)} %get-tuple-element.378), channel_id=1, source_target_pairs={{0,2},{2,4},{4,6},{6,7},{7,5},{5,3},{3,1},{1,0},{8,10},{10,12},{12... | collective-permute-start | bytes 2506760 | tf_op jit(solution)/shard_map/ppermute | solution.py:289
  503.9 200.8 %reduce-scatter.6.cloned.1.call-start = ((), (), s32[]{:S(2)}) async-start(), calls=%async_computation.4 | async-start | bytes 11796480 | tf_op jit(solution)/shard_map/reduce_scatter | solution.py:1020
  509.4 39.5 %collective-permute-start.48 = (bf16[528,1536]{1,0:T(8,128)(2,1)}, bf16[528,1536]{1,0:T(8,128)(2,1)S(1)}, u32[]{:S(2)}, u32[]{:S(2)}) collective-permute-start(bf16[528,1536]{1,0:T(8,128)(2,1)} %get-tuple-element.383), channel_id=1, source_target_pairs={{0,1},{2,0},{4,2},{6,4},{7,6},{5,7},{3,5},{1,3},{8,9},{10,8},{12,1... | collective-permute-start | bytes 4866056 | tf_op jit(solution)/shard_map/ppermute | solution.py:289
  512.6 38.6 %collective-permute-start.49 = (bf16[528,1536]{1,0:T(8,128)(2,1)}, bf16[528,1536]{1,0:T(8,128)(2,1)}, u32[]{:S(2)}, u32[]{:S(2)}) collective-permute-start(bf16[528,1536]{1,0:T(8,128)(2,1)} %get-tuple-element.384), channel_id=1, source_target_pairs={{0,2},{2,4},{4,6},{6,7},{7,5},{5,3},{3,1},{1,0},{8,10},{10,12},{12... | collective-permute-start | bytes 4866056 | tf_op jit(solution)/shard_map/ppermute | solution.py:289
  527.7 41.9 %collective-permute-start.52 = (bf16[128,1536]{1,0:T(8,128)(2,1)}, bf16[128,1536]{1,0:T(8,128)(2,1)S(1)}, u32[]{:S(2)}, u32[]{:S(2)}) collective-permute-start(bf16[128,1536]{1,0:T(8,128)(2,1)} %get-tuple-element.391), channel_id=1, source_target_pairs={{0,1},{2,0},{4,2},{6,4},{7,6},{5,7},{3,5},{1,3},{8,9},{10,8},{12,1... | collective-permute-start | bytes 1179656 | tf_op jit(solution)/shard_map/ppermute | solution.py:289
  529.6 40.0 %collective-permute-start.53 = (bf16[128,1536]{1,0:T(8,128)(2,1)}, bf16[128,1536]{1,0:T(8,128)(2,1)S(1)}, u32[]{:S(2)}, u32[]{:S(2)}) collective-permute-start(bf16[128,1536]{1,0:T(8,128)(2,1)} %get-tuple-element.392), channel_id=1, source_target_pairs={{0,2},{2,4},{4,6},{6,7},{7,5},{5,3},{3,1},{1,0},{8,10},{10,12},{12... | collective-permute-start | bytes 1179656 | tf_op jit(solution)/shard_map/ppermute | solution.py:289
  533.0 41.2 %collective-permute-start.56 = (bf16[272,1536]{1,0:T(8,128)(2,1)}, bf16[272,1536]{1,0:T(8,128)(2,1)}, u32[]{:S(2)}, u32[]{:S(2)}) collective-permute-start(bf16[272,1536]{1,0:T(8,128)(2,1)} %get-tuple-element.395), channel_id=1, source_target_pairs={{0,1},{2,0},{4,2},{6,4},{7,6},{5,7},{3,5},{1,3},{8,9},{10,8},{12,1... | collective-permute-start | bytes 2506760 | tf_op jit(solution)/shard_map/ppermute | solution.py:289
  (115 other events, 1380.3 us)
Sparse Core Ops, SparseCore 0:
  454.6 77.6 reduce-scatter.7
  534.9 78.3 reduce-scatter.3
  616.4 78.3 reduce-scatter.5

commit v4 on v3

--- a/solution.py
+++ b/solution.py
@@ -838,7 +838,8 @@
     xn1, query, keyval, mixed, gates, gates_pack, gains = attention_forward(
         starts, tokens, seg_col, seg_row, routes, cos, sin, first_weights
     )
-    cot_rings[0].step(mixed)
+    for ring in cot_rings:
+        ring.step(mixed)
     out_weights = out_weights(mixed)
     hidden, xn2 = [], []
     for m in micros:
@@ -855,7 +856,6 @@
         )
         hidden.append(out[0])
         xn2.append(out[1])
-    cot_rings[1].step(xn2[0])
     for ring in cot_rings:
         ring.step()
     got = cot_rings[0].got + cot_rings[1].got

time: 776 us -> 755 us (0.973)
  waiting for transfers between devices: 262 us -> 247 us
    ppermute x72, waiting for transfers between devices: 248 us -> 236 us  [ring_step(): return lax.ppermute(part, 'expert', pairs)]
    unnamed x138 -> x130, local copies, waits for them, and re-layouts: 17.5 us -> 13.9 us
  transfers between devices with their start and end apart: 83 -> 83, of which waited for: 41 -> 37; matrix products, arithmetic and copies ran while one was open for 10% -> 10% of each run, Pallas kernels for 38% -> 39%
where the time goes in v4:
time: 755 us; the launch traced here: 745 us
  Pallas kernels  297 us (39%)
  waiting for transfers between devices  247 us (33%)
  starting transfers between devices  82.8 us (11%)
  other arithmetic  61.8 us (8%)
  local copies, waits for them, and re-layouts  35.6 us (5%)
  between operations  20.2 us (3%)
    ppermute x72, waiting for transfers between devices, ring_step(): return lax.ppermute(part, 'expert', pairs)  236 us
    pallas_call x4, Pallas kernels, expert_pass(): pl.pallas_call(functools.partial(expert_kernel, sources), grid=(count,),...  97.3 us
    pallas_call x11, Pallas kernels, block_call(): pl.pallas_call(kernel, grid_spec=pltpu.PrefetchScalarGridSpec(num_scalar_...  86.2 us
    ppermute x72, starting transfers between devices, ring_step(): return lax.ppermute(part, 'expert', pairs)  78.6 us
    pallas_call x3, Pallas kernels, weight_grads(): pl.pallas_call(weight_grad_kernel, grid=(count, height // tile), in_specs...  46 us
    convert_element_type x17, other arithmetic, add_rows(): (left.astype(jnp.float32) + right.astype(jnp.float32)).astype(jnp.bfloat16)  36.1 us
    pallas_call x2, Pallas kernels, spread_rows(): pl.pallas_call(functools.partial(spread_kernel, sources // 2 - base, span...  28.2 us
  transfers between devices with their start and end apart: 83, of which 37 were waited for; matrix products, arithmetic and copies ran while one was open for 10% of the time, Pallas kernels for 39%

profile of v4, /device:TPU:0, one launch (start us, length us, event | category | flops | bytes accessed | tf_op | source)
XLA Modules:
  0.0 744.7 jit_solution(8386352754901045939)
XLA Ops:
  20.3 33.0 %collective-permute-done.4.refs_1_ = bf16[256,1536]{1,0:T(8,128)(2,1)} collective-permute-done((bf16[256,1536]{1,0:T(8,128)(2,1)S(1)}, bf16[256,1536]{1,0:T(8,128)(2,1)}, u32[]{:S(2)}, u32[]{:S(2)}) %collective-permute-start.4) | collective-permute-done | bytes 786464 | tf_op jit(solution)/shard_map/ppermute | solution.py:289
  64.0 14.2 %attention_forward.1 = (bf16[2,256,1536]{2,1,0:T(8,128)(2,1)}, bf16[2,256,1536]{2,1,0:T(8,128)(2,1)}, bf16[2,256,512]{2,1,0:T(8,128)(2,1)}, bf16[2,256,1536]{2,1...) custom-call(s32[4]{0:T(128)} %add_multiply_fusion.starts_ref, ...), custom_call_target="tpu_custom_call" | custom-call | flops 1000000 | bytes 1000000 | tf_op jit(solution)/shard_map/attention_forward/pallas_call | solution.py:645
  79.7 13.6 %collective-permute-done.10.refs_2_ = bf16[272,1536]{1,0:T(8,128)(2,1)} collective-permute-done((bf16[272,1536]{1,0:T(8,128)(2,1)}, bf16[272,1536]{1,0:T(8,128)(2,1)}, u32[]{:S(2)}, u32[]{:S(2)}) %collective-permute-start.10) | collective-permute-done | bytes 835616 | tf_op jit(solution)/shard_map/ppermute | solution.py:289
  96.2 14.0 %collective-permute-done.20.refs_3_ = bf16[256,1536]{1,0:T(8,128)(2,1)} collective-permute-done((bf16[256,1536]{1,0:T(8,128)(2,1)}, bf16[256,1536]{1,0:T(8,128)(2,1)}, u32[]{:S(2)}, u32[]{:S(2)}) %collective-permute-start.20) | collective-permute-done | bytes 786464 | tf_op jit(solution)/shard_map/ppermute | solution.py:289
  116.4 13.7 %collective-permute-done.13.refs_6_ = bf16[272,1536]{1,0:T(8,128)(2,1)S(1)} collective-permute-done((bf16[272,1536]{1,0:T(8,128)(2,1)}, bf16[272,1536]{1,0:T(8,128)(2,1)S(1)}, u32[]{:S(2)}, u32[]{:S(2)}) %collective-permute-start.13) | collective-permute-done | bytes 835616 | tf_op jit(solution)/shard_map/ppermute | solution.py:289
  134.4 6.7 hidden_rows.2
  142.9 6.3 collective-permute-done.14.refs_5_
  152.0 7.0 join_blocks.2.refs_0_
  169.6 6.3 pick_rows.6
  175.8 8.9 %collective-permute-done.24.refs_4_.refs_5_ = bf16[272,1536]{1,0:T(8,128)(2,1)S(1)} collective-permute-done((bf16[272,1536]{1,0:T(8,128)(2,1)S(1)}, bf16[272,1536]{1,0:T(8,128)(2,1)S(1)}, u32[]{:S(2)}, u32[]{:S(2)}) %collective-permute-start.24) | collective-permute-done | bytes 835616 | tf_op jit(solution)/shard_map/ppermute | solution.py:289
  208.7 6.8 hidden_rows.3
  224.7 24.3 %expert_pass.4 = (bf16[8,256,1536]{2,1,0:T(8,128)(2,1)}, bf16[8,256,1536]{2,1,0:T(8,128)(2,1)}, f32[4,512,1]{2,1,0:T(8,128)}, bf16[4,1024,1536]{2,1,0:T(8,128)(2...) custom-call(bf16[256,1536]{1,0:T(8,128)(2,1)} %get-tuple-element.297.refs_0_, ...), custom_call_target="tpu_custom_call" | custom-call | flops 1000000 | bytes 1000000 | tf_op jit(solution)/shard_map/expert_pass/pallas_call | solution.py:435
  251.3 24.4 %expert_pass.5 = (bf16[8,256,1536]{2,1,0:T(8,128)(2,1)}, bf16[8,256,1536]{2,1,0:T(8,128)(2,1)}, f32[4,512,1]{2,1,0:T(8,128)}, bf16[4,1024,1536]{2,1,0:T(8,128)(2...) custom-call(bf16[256,1536]{1,0:T(8,128)(2,1)} %get-tuple-element.297, ...), custom_call_target="tpu_custom_call", output_to_operand_aliasing={{0}: (26, {}), {1}: (27, {}), {2}: (28, {}), {3}: (29, {}),... | custom-call | flops 1000000 | bytes 1000000 | tf_op jit(solution)/shard_map/expert_pass/pallas_call | solution.py:435
  277.9 14.1 %spread_rows.2 = (bf16[8,528,1536]{2,1,0:T(8,128)(2,1)}, bf16[272,1536]{1,0:T(8,128)(2,1)}, bf16[256,1536]{1,0:T(8,128)(2,1)}) custom-call(s32[1]{0:T(128)} %bitcast.8.first_ref, bf16[8,256,256]{2,1,0:T(8,128)(2,1)} %get-tuple-element.296.place_ref, bf16[8,256,1536]{2,1,0:T(8,128)(2,1)} %get-tuple-element.304.rows_ref, ...), custom_call_target="tpu_custom_call" | custom-call | flops 1000000 | bytes 1000000 | tf_op jit(solution)/shard_map/spread_rows/pallas_call | solution.py:582
  304.0 11.4 %collective-permute-done.38.refs_2_ = bf16[128,1536]{1,0:T(8,128)(2,1)S(1)} collective-permute-done((bf16[128,1536]{1,0:T(8,128)(2,1)S(1)}, bf16[128,1536]{1,0:T(8,128)(2,1)S(1)}, u32[]{:S(2)}, u32[]{:S(2)}) %collective-permute-start.38) | collective-permute-done | bytes 393248 | tf_op jit(solution)/shard_map/ppermute | solution.py:289
  321.0 24.3 %expert_pass.6 = (bf16[8,256,1536]{2,1,0:T(8,128)(2,1)}, bf16[8,256,1536]{2,1,0:T(8,128)(2,1)}, f32[4,512,1]{2,1,0:T(8,128)}, bf16[4,1024,1536]{2,1,0:T(8,128)(2...) custom-call(bf16[256,1536]{1,0:T(8,128)(2,1)} %get-tuple-element.350, ...), custom_call_target="tpu_custom_call", output_to_operand_aliasing={{3}: (26, {}), {4}: (27, {}), {5}: (28, {}), {6}: (29, {})} | custom-call | flops 1000000 | bytes 1000000 | tf_op jit(solution)/shard_map/expert_pass/pallas_call | solution.py:435
  352.9 24.3 %expert_pass.7 = (bf16[8,256,1536]{2,1,0:T(8,128)(2,1)}, bf16[8,256,1536]{2,1,0:T(8,128)(2,1)}, f32[4,512,1]{2,1,0:T(8,128)}, bf16[4,1024,1536]{2,1,0:T(8,128)(2...) custom-call(bf16[256,1536]{1,0:T(8,128)(2,1)} %get-tuple-element.350, ...), custom_call_target="tpu_custom_call", output_to_operand_aliasing={{0}: (26, {}), {1}: (27, {}), {2}: (28, {}), {3}: (29, {}),... | custom-call | flops 1000000 | bytes 1000000 | tf_op jit(solution)/shard_map/expert_pass/pallas_call | solution.py:435
  377.2 14.1 %spread_rows.3 = (bf16[8,528,1536]{2,1,0:T(8,128)(2,1)}, bf16[128,1536]{1,0:T(8,128)(2,1)}, bf16[144,1536]{1,0:T(8,128)(2,1)}, bf16[128,1536]{1,0:T(8,128)(2,1)}, bf16[128,1536]{1,0:T(8,128)(2,1)}) custom-call(s32[1]{0:T(128)} %bitcast.8.first_ref, bf16[8,256,256]{2,1,0:T(8,128)(2,1)} %get-tuple-element.522.place_ref, ...), custom_call_target="tpu_custom_call" | custom-call | flops 1000000 | bytes 1000000 | tf_op jit(solution)/shard_map/spread_rows/pallas_call | solution.py:582
  396.8 8.9 %collective-permute-done.44 = bf16[128,1536]{1,0:T(8,128)(2,1)S(1)} collective-permute-done((bf16[128,1536]{1,0:T(8,128)(2,1)S(1)}, bf16[128,1536]{1,0:T(8,128)(2,1)S(1)}, u32[]{:S(2)}, u32[]{:S(2)}) %collective-permute-start.44) | collective-permute-done | bytes 393248 | tf_op jit(solution)/shard_map/ppermute | solution.py:289
  418.4 15.0 %weight_grads.3 = bf16[4,768,1536]{2,1,0:T(8,128)(2,1)} custom-call(bf16[4,1024,768]{2,1,0:T(8,128)(2,1)} %get-tuple-element.373.left_ref, bf16[4,1024,1536]{2,1,0:T(8,128)(2,1)} %get-tuple-element.374.right_ref), custom_call_target="tpu_custom_call" | custom-call | flops 1000000 | bytes 1000000 | tf_op jit(solution)/shard_map/weight_grads/pallas_call | solution.py:612
  443.2 16.1 %weight_grads.4 = bf16[2,1536,1536]{2,1,0:T(8,128)(2,1)} custom-call(bf16[4,1024,1536]{2,1,0:T(8,128)(2,1)} %get-tuple-element.388.left_ref, bf16[4,1024,1536]{2,1,0:T(8,128)(2,1)} %get-tuple-element.380.right_ref), custom_call_target="tpu_custom_call" | custom-call | flops 1000000 | bytes 1000000 | tf_op jit(solution)/shard_map/weight_grads/pallas_call | solution.py:612
  459.3 21.5 %collective-permute-done.50 = bf16[272,1536]{1,0:T(8,128)(2,1)} collective-permute-done((bf16[272,1536]{1,0:T(8,128)(2,1)}, bf16[272,1536]{1,0:T(8,128)(2,1)}, u32[]{:S(2)}, u32[]{:S(2)}) %collective-permute-start.50) | collective-permute-done | bytes 835616 | tf_op jit(solution)/shard_map/ppermute | solution.py:289
  490.2 14.9 %weight_grads.5 = bf16[2,1536,1536]{2,1,0:T(8,128)(2,1)} custom-call(bf16[4,1024,1536]{2,1,0:T(8,128)(2,1)} %get-tuple-element.388.left_ref, bf16[4,1024,1536]{2,1,0:T(8,128)(2,1)} %get-tuple-element.380.right_ref), custom_call_target="tpu_custom_call" | custom-call | flops 1000000 | bytes 1000000 | tf_op jit(solution)/shard_map/weight_grads/pallas_call | solution.py:612
  513.3 13.1 %collective-permute-done.48.left_ref = bf16[528,1536]{1,0:T(8,128)(2,1)S(1)} collective-permute-done((bf16[528,1536]{1,0:T(8,128)(2,1)}, bf16[528,1536]{1,0:T(8,128)(2,1)S(1)}, u32[]{:S(2)}, u32[]{:S(2)}) %collective-permute-start.48) | collective-permute-done | bytes 1622048 | tf_op jit(solution)/shard_map/ppermute | solution.py:289
  529.6 18.5 %attention_backward.2 = (bf16[256,1536]{1,0:T(8,128)(2,1)}, bf16[256,2176]{1,0:T(8,128)(2,1)}, bf16[256,1536]{1,0:T(8,128)(2,1)}, f32[8,1536]{1,0:T(8,128)}) custom-call(bf16[8,528,1536]{2,1,0:T(8,128)(2,1)} %get-tuple-element.397.own_ref, bf16[528,1536]{1,0:T(8,128)(2,1)} %copy-done.12, bf16[528,1536]{1,0:T(8,128)(2,1)} %collective-permute-done.49.right_ref, ...), custom_call_target="tpu_custom_call" | custom-call | flops 1000000 | bytes 1000000 | tf_op jit(solution)/shard_map/attention_backward/pallas_call | solution.py:470
  552.8 18.6 %attention_backward.3 = (bf16[256,1536]{1,0:T(8,128)(2,1)}, bf16[256,2176]{1,0:T(8,128)(2,1)}, bf16[256,1536]{1,0:T(8,128)(2,1)}, f32[8,1536]{1,0:T(8,128)}) custom-call(bf16[8,528,1536]{2,1,0:T(8,128)(2,1)} %get-tuple-element.406.own_ref, bf16[272,1536]{1,0:T(8,128)(2,1)} %collective-permute-done.56.left_ref, ...), custom_call_target="tpu_custom_call" | custom-call | flops 1000000 | bytes 1000000 | tf_op jit(solution)/shard_map/attention_backward/pallas_call | solution.py:470
  578.3 12.8 %attention_grads.1 = (bf16[2,384,3712]{2,1,0:T(8,128)(2,1)}, bf16[2,384,3712]{2,1,0:T(8,128)(2,1)}) custom-call(s32[2]{0:T(128)} %pad_add_fusion.core_ref, bf16[2,256,1536]{2,1,0:T(8,128)(2,1)} %get-tuple-element.417.xn1, bf16[2,256,1536]{2,1,0:T(8,128)(2,1)} %get-tuple-element.247.mixed_ref.mixed, bf16[256,2176]{1,0:T(8,128)(2,1)} %get-tuple-element.418.refs_0_, ...), custom_call_target="tpu_custom_call" | custom-call | flops 1000000 | bytes 1000000 | tf_op jit(solution)/shard_map/attention_grads/pallas_call | solution.py:736
  600.8 7.3 add_convert_fusion
  632.9 9.5 %collective-permute-done.66 = bf16[96,3712]{1,0:T(8,128)(2,1)S(1)} collective-permute-done((bf16[96,3712]{1,0:T(8,128)(2,1)S(1)}, bf16[96,3712]{1,0:T(8,128)(2,1)S(1)}, u32[]{:S(2)}, u32[]{:S(2)}) %collective-permute-start.66) | collective-permute-done | bytes 712736 | tf_op jit(solution)/shard_map/ppermute | solution.py:289
  650.5 14.2 %collective-permute-done.68 = bf16[96,3712]{1,0:T(8,128)(2,1)S(1)} collective-permute-done((bf16[96,3712]{1,0:T(8,128)(2,1)S(1)}, bf16[96,3712]{1,0:T(8,128)(2,1)S(1)}, u32[]{:S(2)}, u32[]{:S(2)}) %collective-permute-start.68) | collective-permute-done | bytes 712736 | tf_op jit(solution)/shard_map/ppermute | solution.py:289
  667.2 13.4 %collective-permute-done.69 = bf16[96,3712]{1,0:T(8,128)(2,1)S(1)} collective-permute-done((bf16[96,3712]{1,0:T(8,128)(2,1)S(1)}, bf16[96,3712]{1,0:T(8,128)(2,1)S(1)}, u32[]{:S(2)}, u32[]{:S(2)}) %collective-permute-start.69) | collective-permute-done | bytes 712736 | tf_op jit(solution)/shard_map/ppermute | solution.py:289
  684.1 7.1 collective-permute-done.71
  (375 shorter events, 266.2 us)
Async XLA Ops:
  7.2 676.5 %reduce-scatter.8.cloned.1.call-start = ((), (), s32[]{:S(2)}) async-start(), calls=%async_computation.5 | async-start | bytes 11796480 | tf_op jit(solution)/shard_map/reduce_scatter | solution.py:1020
  12.9 41.7 %collective-permute-start.1 = (bf16[384,2176]{1,0:T(8,128)(2,1)S(1)}, bf16[384,2176]{1,0:T(8,128)(2,1)}, u32[]{:S(2)}, u32[]{:S(2)}) collective-permute-start(bf16[384,2176]{1,0:T(8,128)(2,1)S(1)} %concatenate.44.refs_0_), channel_id=1, source_target_pairs={{0,16},{8,24},{16,0},{24,8},{1,17},{9,25},{17,1},{25,9},{2,18},{10... | collective-permute-start | bytes 5013512 | tf_op jit(solution)/shard_map/ppermute | solution.py:761
  16.2 38.4 %collective-permute-start.2 = (bf16[272,1536]{1,0:T(8,128)(2,1)S(1)}, bf16[272,1536]{1,0:T(8,128)(2,1)S(1)}, u32[]{:S(2)}, u32[]{:S(2)}) collective-permute-start(bf16[272,1536]{1,0:T(8,128)(2,1)S(1)} %pad_maximum_fusion.4.refs_0_), channel_id=1, source_target_pairs={{0,2},{2,4},{4,6},{6,7},{7,5},{5,3},{3,1},{1,0},{8,10},{10,12},{12... | collective-permute-start | bytes 2506760 | tf_op jit(solution)/shard_map/ppermute | solution.py:289
  17.9 36.7 %collective-permute-start.3 = (bf16[272,1536]{1,0:T(8,128)(2,1)S(1)}, bf16[272,1536]{1,0:T(8,128)(2,1)S(1)}, u32[]{:S(2)}, u32[]{:S(2)}) collective-permute-start(bf16[272,1536]{1,0:T(8,128)(2,1)S(1)} %pad_maximum_fusion.4.refs_0_), channel_id=1, source_target_pairs={{0,1},{2,0},{4,2},{6,4},{7,6},{5,7},{3,5},{1,3},{8,9},{10,8},{12,1... | collective-permute-start | bytes 2506760 | tf_op jit(solution)/shard_map/ppermute | solution.py:289
  18.3 35.0 %collective-permute-start.4 = (bf16[256,1536]{1,0:T(8,128)(2,1)S(1)}, bf16[256,1536]{1,0:T(8,128)(2,1)}, u32[]{:S(2)}, u32[]{:S(2)}) collective-permute-start(bf16[256,1536]{1,0:T(8,128)(2,1)S(1)} %get-tuple-element.234.refs_0_), channel_id=1, source_target_pairs={{0,2},{2,4},{4,6},{6,7},{7,5},{5,3},{3,1},{1,0},{8,10},{10,12},{12... | collective-permute-start | bytes 2359304 | tf_op jit(solution)/shard_map/ppermute | solution.py:289
  19.9 34.7 %collective-permute-start.5 = (bf16[256,1536]{1,0:T(8,128)(2,1)S(1)}, bf16[256,1536]{1,0:T(8,128)(2,1)}, u32[]{:S(2)}, u32[]{:S(2)}) collective-permute-start(bf16[256,1536]{1,0:T(8,128)(2,1)S(1)} %get-tuple-element.234.refs_0_), channel_id=1, source_target_pairs={{0,1},{2,0},{4,2},{6,4},{7,6},{5,7},{3,5},{1,3},{8,9},{10,8},{12,1... | collective-permute-start | bytes 2359304 | tf_op jit(solution)/shard_map/ppermute | solution.py:289
  56.8 38.8 %collective-permute-start.8 = (bf16[384,1536]{1,0:T(8,128)(2,1)}, bf16[384,1536]{1,0:T(8,128)(2,1)S(1)}, u32[]{:S(2)}, u32[]{:S(2)}) collective-permute-start(bf16[384,1536]{1,0:T(8,128)(2,1)} %refs_0_.4), channel_id=1, source_target_pairs={{0,16},{8,24},{16,0},{24,8},{1,17},{9,25},{17,1},{25,9},{2,18},{10... | collective-permute-start | bytes 3538952 | tf_op jit(solution)/shard_map/ppermute | solution.py:761
  58.7 34.6 %collective-permute-start.10 = (bf16[272,1536]{1,0:T(8,128)(2,1)}, bf16[272,1536]{1,0:T(8,128)(2,1)}, u32[]{:S(2)}, u32[]{:S(2)}) collective-permute-start(bf16[272,1536]{1,0:T(8,128)(2,1)} %copy-done.33), channel_id=1, source_target_pairs={{0,2},{2,4},{4,6},{6,7},{7,5},{5,3},{3,1},{1,0},{8,10},{10,12},{12... | collective-permute-start | bytes 2506760 | tf_op jit(solution)/shard_map/ppermute | solution.py:289
  60.3 33.9 %collective-permute-start.11 = (bf16[272,1536]{1,0:T(8,128)(2,1)}, bf16[272,1536]{1,0:T(8,128)(2,1)}, u32[]{:S(2)}, u32[]{:S(2)}) collective-permute-start(bf16[272,1536]{1,0:T(8,128)(2,1)} %copy-done.34), channel_id=1, source_target_pairs={{0,1},{2,0},{4,2},{6,4},{7,6},{5,7},{3,5},{1,3},{8,9},{10,8},{12,1... | collective-permute-start | bytes 2506760 | tf_op jit(solution)/shard_map/ppermute | solution.py:289
  78.3 31.9 %collective-permute-start.20 = (bf16[256,1536]{1,0:T(8,128)(2,1)}, bf16[256,1536]{1,0:T(8,128)(2,1)}, u32[]{:S(2)}, u32[]{:S(2)}) collective-permute-start(bf16[256,1536]{1,0:T(8,128)(2,1)} %collective-permute-done.18.refs_2_), channel_id=1, source_target_pairs={{0,2},{2,4},{4,6},{6,7},{7,5},{5,3},{3,1},{1,0},{8,10},{10,12},{12... | collective-permute-start | bytes 2359304 | tf_op jit(solution)/shard_map/ppermute | solution.py:289
  79.6 53.0 %collective-permute-start.7 = (bf16[384,1536]{1,0:T(8,128)(2,1)}, bf16[384,1536]{1,0:T(8,128)(2,1)S(1)}, u32[]{:S(2)}, u32[]{:S(2)}) collective-permute-start(bf16[384,1536]{1,0:T(8,128)(2,1)} %refs_0_.4), channel_id=1, source_target_pairs={{0,8},{8,0},{16,24},{24,16},{1,9},{9,1},{17,25},{25,17},{2,10},{10... | collective-permute-start | bytes 3538952 | tf_op jit(solution)/shard_map/ppermute | solution.py:762
  94.2 35.9 %collective-permute-start.13 = (bf16[272,1536]{1,0:T(8,128)(2,1)}, bf16[272,1536]{1,0:T(8,128)(2,1)S(1)}, u32[]{:S(2)}, u32[]{:S(2)}) collective-permute-start(bf16[272,1536]{1,0:T(8,128)(2,1)} %collective-permute-done.11.refs_7_), channel_id=1, source_target_pairs={{0,1},{2,0},{4,2},{6,4},{7,6},{5,7},{3,5},{1,3},{8,9},{10,8},{12,1... | collective-permute-start | bytes 2506760 | tf_op jit(solution)/shard_map/ppermute | solution.py:289
  95.6 34.8 %collective-permute-start.12 = (bf16[272,1536]{1,0:T(8,128)(2,1)}, bf16[272,1536]{1,0:T(8,128)(2,1)S(1)}, u32[]{:S(2)}, u32[]{:S(2)}) collective-permute-start(bf16[272,1536]{1,0:T(8,128)(2,1)} %collective-permute-done.10.refs_2_), channel_id=1, source_target_pairs={{0,2},{2,4},{4,6},{6,7},{7,5},{5,3},{3,1},{1,0},{8,10},{10,12},{12... | collective-permute-start | bytes 2506760 | tf_op jit(solution)/shard_map/ppermute | solution.py:289
  114.8 37.1 %collective-permute-start.22 = (bf16[128,1536]{1,0:T(8,128)(2,1)}, bf16[128,1536]{1,0:T(8,128)(2,1)}, u32[]{:S(2)}, u32[]{:S(2)}) collective-permute-start(bf16[128,1536]{1,0:T(8,128)(2,1)} %slice.318), channel_id=1, source_target_pairs={{0,2},{2,4},{4,6},{6,7},{7,5},{5,3},{3,1},{1,0},{8,10},{10,12},{12... | collective-permute-start | bytes 1179656 | tf_op jit(solution)/shard_map/ppermute | solution.py:289
  218.0 31.0 %collective-permute-start.30 = (bf16[272,1536]{1,0:T(8,128)(2,1)}, bf16[272,1536]{1,0:T(8,128)(2,1)S(1)}, u32[]{:S(2)}, u32[]{:S(2)}) collective-permute-start(bf16[272,1536]{1,0:T(8,128)(2,1)} %get-tuple-element.270.refs_0_.refs_1_), channel_id=1, source_target_pairs={{0,2},{2,4},{4,6},{6,7},{7,5},{5,3},{3,1},{1,0},{8,10},{10,12},{12... | collective-permute-start | bytes 2506760 | tf_op jit(solution)/shard_map/ppermute | solution.py:289
  220.4 28.6 %collective-permute-start.31 = (bf16[272,1536]{1,0:T(8,128)(2,1)}, bf16[272,1536]{1,0:T(8,128)(2,1)S(1)}, u32[]{:S(2)}, u32[]{:S(2)}) collective-permute-start(bf16[272,1536]{1,0:T(8,128)(2,1)} %get-tuple-element.270.refs_0_.refs_1_), channel_id=1, source_target_pairs={{0,1},{2,0},{4,2},{6,4},{7,6},{5,7},{3,5},{1,3},{8,9},{10,8},{12,1... | collective-permute-start | bytes 2506760 | tf_op jit(solution)/shard_map/ppermute | solution.py:289
  249.0 26.7 %collective-permute-start.32 = (bf16[272,1536]{1,0:T(8,128)(2,1)S(1)}, bf16[272,1536]{1,0:T(8,128)(2,1)}, u32[]{:S(2)}, u32[]{:S(2)}) collective-permute-start(bf16[272,1536]{1,0:T(8,128)(2,1)S(1)} %collective-permute-done.30.refs_2_.refs_3_), channel_id=1, source_target_pairs={{0,2},{2,4},{4,6},{6,7},{7,5},{5,3},{3,1},{1,0},{8,10},{10,12},{12... | collective-permute-start | bytes 2506760 | tf_op jit(solution)/shard_map/ppermute | solution.py:289
  296.9 48.4 %collective-permute-start.36 = (bf16[272,1536]{1,0:T(8,128)(2,1)}, bf16[272,1536]{1,0:T(8,128)(2,1)S(1)}, u32[]{:S(2)}, u32[]{:S(2)}) collective-permute-start(bf16[272,1536]{1,0:T(8,128)(2,1)} %get-tuple-element.314), channel_id=1, source_target_pairs={{0,1},{2,0},{4,2},{6,4},{7,6},{5,7},{3,5},{1,3},{8,9},{10,8},{12,1... | collective-permute-start | bytes 2506760 | tf_op jit(solution)/shard_map/ppermute | solution.py:289
  298.6 46.7 %collective-permute-start.37 = (bf16[256,1536]{1,0:T(8,128)(2,1)}, bf16[256,1536]{1,0:T(8,128)(2,1)}, u32[]{:S(2)}, u32[]{:S(2)}) collective-permute-start(bf16[256,1536]{1,0:T(8,128)(2,1)} %get-tuple-element.315), channel_id=1, source_target_pairs={{0,2},{2,4},{4,6},{6,7},{7,5},{5,3},{3,1},{1,0},{8,10},{10,12},{12... | collective-permute-start | bytes 2359304 | tf_op jit(solution)/shard_map/ppermute | solution.py:289
  350.8 63.1 %collective-permute-start.40 = (bf16[528,1536]{1,0:T(8,128)(2,1)}, bf16[528,1536]{1,0:T(8,128)(2,1)S(1)}, u32[]{:S(2)}, u32[]{:S(2)}) collective-permute-start(bf16[528,1536]{1,0:T(8,128)(2,1)} %pad_maximum_fusion), channel_id=1, source_target_pairs={{0,1},{2,0},{4,2},{6,4},{7,6},{5,7},{3,5},{1,3},{8,9},{10,8},{12,1... | collective-permute-start | bytes 4866056 | tf_op jit(solution)/shard_map/ppermute | solution.py:289
  352.7 61.2 %collective-permute-start.41 = (bf16[528,1536]{1,0:T(8,128)(2,1)}, bf16[528,1536]{1,0:T(8,128)(2,1)S(1)}, u32[]{:S(2)}, u32[]{:S(2)}) collective-permute-start(bf16[528,1536]{1,0:T(8,128)(2,1)} %pad_maximum_fusion.1), channel_id=1, source_target_pairs={{0,2},{2,4},{4,6},{6,7},{7,5},{5,3},{3,1},{1,0},{8,10},{10,12},{12... | collective-permute-start | bytes 4866056 | tf_op jit(solution)/shard_map/ppermute | solution.py:289
  433.4 250.2 %reduce-scatter.4.cloned.1.call-start = ((), (), s32[]{:S(2)}) async-start(), calls=%async_computation.3 | async-start | bytes 11796480 | tf_op jit(solution)/shard_map/reduce_scatter | solution.py:1020
  434.8 47.4 %collective-permute-start.42 = (bf16[528,1536]{1,0:T(8,128)(2,1)S(1)}, bf16[528,1536]{1,0:T(8,128)(2,1)}, u32[]{:S(2)}, u32[]{:S(2)}) collective-permute-start(bf16[528,1536]{1,0:T(8,128)(2,1)S(1)} %copy-done.29), channel_id=1, source_target_pairs={{0,1},{2,0},{4,2},{6,4},{7,6},{5,7},{3,5},{1,3},{8,9},{10,8},{12,1... | collective-permute-start | bytes 4866056 | tf_op jit(solution)/shard_map/ppermute | solution.py:289
  436.4 45.8 %collective-permute-start.43 = (bf16[528,1536]{1,0:T(8,128)(2,1)S(1)}, bf16[528,1536]{1,0:T(8,128)(2,1)}, u32[]{:S(2)}, u32[]{:S(2)}) collective-permute-start(bf16[528,1536]{1,0:T(8,128)(2,1)S(1)} %copy-done.28), channel_id=1, source_target_pairs={{0,2},{2,4},{4,6},{6,7},{7,5},{5,3},{3,1},{1,0},{8,10},{10,12},{12... | collective-permute-start | bytes 4866056 | tf_op jit(solution)/shard_map/ppermute | solution.py:289
  440.8 40.0 %collective-permute-start.50 = (bf16[272,1536]{1,0:T(8,128)(2,1)}, bf16[272,1536]{1,0:T(8,128)(2,1)}, u32[]{:S(2)}, u32[]{:S(2)}) collective-permute-start(bf16[272,1536]{1,0:T(8,128)(2,1)} %get-tuple-element.377), channel_id=1, source_target_pairs={{0,1},{2,0},{4,2},{6,4},{7,6},{5,7},{3,5},{1,3},{8,9},{10,8},{12,1... | collective-permute-start | bytes 2506760 | tf_op jit(solution)/shard_map/ppermute | solution.py:289
  442.0 40.2 %collective-permute-start.51 = (bf16[272,1536]{1,0:T(8,128)(2,1)}, bf16[272,1536]{1,0:T(8,128)(2,1)}, u32[]{:S(2)}, u32[]{:S(2)}) collective-permute-start(bf16[272,1536]{1,0:T(8,128)(2,1)} %get-tuple-element.378), channel_id=1, source_target_pairs={{0,2},{2,4},{4,6},{6,7},{7,5},{5,3},{3,1},{1,0},{8,10},{10,12},{12... | collective-permute-start | bytes 2506760 | tf_op jit(solution)/shard_map/ppermute | solution.py:289
  482.2 201.5 %reduce-scatter.6.cloned.1.call-start = ((), (), s32[]{:S(2)}) async-start(), calls=%async_computation.4 | async-start | bytes 11796480 | tf_op jit(solution)/shard_map/reduce_scatter | solution.py:1020
  487.7 38.7 %collective-permute-start.48 = (bf16[528,1536]{1,0:T(8,128)(2,1)}, bf16[528,1536]{1,0:T(8,128)(2,1)S(1)}, u32[]{:S(2)}, u32[]{:S(2)}) collective-permute-start(bf16[528,1536]{1,0:T(8,128)(2,1)} %get-tuple-element.383), channel_id=1, source_target_pairs={{0,1},{2,0},{4,2},{6,4},{7,6},{5,7},{3,5},{1,3},{8,9},{10,8},{12,1... | collective-permute-start | bytes 4866056 | tf_op jit(solution)/shard_map/ppermute | solution.py:289
  490.2 39.4 %collective-permute-start.49 = (bf16[528,1536]{1,0:T(8,128)(2,1)}, bf16[528,1536]{1,0:T(8,128)(2,1)}, u32[]{:S(2)}, u32[]{:S(2)}) collective-permute-start(bf16[528,1536]{1,0:T(8,128)(2,1)} %get-tuple-element.384), channel_id=1, source_target_pairs={{0,2},{2,4},{4,6},{6,7},{7,5},{5,3},{3,1},{1,0},{8,10},{10,12},{12... | collective-permute-start | bytes 4866056 | tf_op jit(solution)/shard_map/ppermute | solution.py:289
  505.1 43.0 %collective-permute-start.52 = (bf16[128,1536]{1,0:T(8,128)(2,1)}, bf16[128,1536]{1,0:T(8,128)(2,1)S(1)}, u32[]{:S(2)}, u32[]{:S(2)}) collective-permute-start(bf16[128,1536]{1,0:T(8,128)(2,1)} %get-tuple-element.391), channel_id=1, source_target_pairs={{0,1},{2,0},{4,2},{6,4},{7,6},{5,7},{3,5},{1,3},{8,9},{10,8},{12,1... | collective-permute-start | bytes 1179656 | tf_op jit(solution)/shard_map/ppermute | solution.py:289
  508.1 40.1 %collective-permute-start.53 = (bf16[128,1536]{1,0:T(8,128)(2,1)}, bf16[128,1536]{1,0:T(8,128)(2,1)S(1)}, u32[]{:S(2)}, u32[]{:S(2)}) collective-permute-start(bf16[128,1536]{1,0:T(8,128)(2,1)} %get-tuple-element.392), channel_id=1, source_target_pairs={{0,2},{2,4},{4,6},{6,7},{7,5},{5,3},{3,1},{1,0},{8,10},{10,12},{12... | collective-permute-start | bytes 1179656 | tf_op jit(solution)/shard_map/ppermute | solution.py:289
  511.3 41.5 %collective-permute-start.56 = (bf16[272,1536]{1,0:T(8,128)(2,1)}, bf16[272,1536]{1,0:T(8,128)(2,1)}, u32[]{:S(2)}, u32[]{:S(2)}) collective-permute-start(bf16[272,1536]{1,0:T(8,128)(2,1)} %get-tuple-element.395), channel_id=1, source_target_pairs={{0,1},{2,0},{4,2},{6,4},{7,6},{5,7},{3,5},{1,3},{8,9},{10,8},{12,1... | collective-permute-start | bytes 2506760 | tf_op jit(solution)/shard_map/ppermute | solution.py:289
  (111 other events, 1344.9 us)
Sparse Core Ops, SparseCore 0:
  433.6 77.9 reduce-scatter.7
  514.1 78.4 reduce-scatter.3
  595.8 78.4 reduce-scatter.5

commit v5 on v4

--- a/solution.py
+++ b/solution.py
@@ -860,7 +860,6 @@
         ring.step()
     got = cot_rings[0].got + cot_rings[1].got
     first_whole = join_blocks(starts, [after(first_weights[0], *got)] + first_weights[1:])
-    out_whole = join_blocks(starts, [after(out_weights[0], first_whole)] + out_weights[1:])
     routes_all = cot_rings[0].stack_rows(rows, micro_count * TOPK)[:, :, :rows]
     routes_all = routes_all.reshape(peers, micro_count, TOPK, rows)
     places = [
@@ -932,8 +931,8 @@
     first, second = Experts(0, calls), Experts(1, calls)
     ring, ring_next = row_rings
     while len(ring.from_left) < steps - 1:
-        ring.step(*places, out_whole)
-    ring.step(first.pick_grads())
+        ring.step(*places)
+    ring.step(first.pick_grads(), first_whole)
     ring.step(first.pick(early), second.pick_grads())
     first.pick(late)
     ring_next.step(*ring.got)
@@ -953,6 +952,8 @@
     ring_first = RingScatter(lambda k: first.sums[k], far, peers)
     ring_first.step(*got)
     second.pick(early)
+    out_whole = join_blocks(starts, [after(out_weights[0], first.sums)] + out_weights[1:])
+    places[1] = after(places[1], out_whole)
     second.pick(late)
     token = second.call(0)
     for number in range(1, calls):

time: 755 us -> 789 us (1.045)
  waiting for transfers between devices: 247 us -> 279 us
    ppermute x72, waiting for transfers between devices: 236 us -> 266 us  [ring_step(): return lax.ppermute(part, 'expert', pairs)]
  transfers between devices with their start and end apart: 83 -> 83, of which waited for: 37 -> 41; matrix products, arithmetic and copies ran while one was open for 10% -> 10% of each run, Pallas kernels for 39% -> 38%
where the time goes in v5:
time: 789 us; the launch traced here: 780 us
  Pallas kernels  298 us (38%)
  waiting for transfers between devices  279 us (35%)
  starting transfers between devices  83.7 us (11%)
  other arithmetic  62.3 us (8%)
  local copies, waits for them, and re-layouts  36.6 us (5%)
  between operations  20.2 us (3%)
    ppermute x72, waiting for transfers between devices, ring_step(): return lax.ppermute(part, 'expert', pairs)  266 us
    pallas_call x4, Pallas kernels, expert_pass(): pl.pallas_call(functools.partial(expert_kernel, sources), grid=(count,),...  97.3 us
    pallas_call x11, Pallas kernels, block_call(): pl.pallas_call(kernel, grid_spec=pltpu.PrefetchScalarGridSpec(num_scalar_...  86.7 us
    ppermute x72, starting transfers between devices, ring_step(): return lax.ppermute(part, 'expert', pairs)  78 us
    pallas_call x3, Pallas kernels, weight_grads(): pl.pallas_call(weight_grad_kernel, grid=(count, height // tile), in_specs...  46.2 us
    convert_element_type x17, other arithmetic, add_rows(): (left.astype(jnp.float32) + right.astype(jnp.float32)).astype(jnp.bfloat16)  35.5 us
    pallas_call x2, Pallas kernels, spread_rows(): pl.pallas_call(functools.partial(spread_kernel, sources // 2 - base, span...  28.2 us
  transfers between devices with their start and end apart: 83, of which 41 were waited for; matrix products, arithmetic and copies ran while one was open for 10% of the time, Pallas kernels for 38%

profile of v5, /device:TPU:0, one launch (start us, length us, event | category | flops | bytes accessed | tf_op | source)
XLA Modules:
  0.0 780.0 jit_solution(6138651251900017162)
XLA Ops:
  22.1 15.9 %collective-permute-done.4.refs_1_ = bf16[256,1536]{1,0:T(8,128)(2,1)} collective-permute-done((bf16[256,1536]{1,0:T(8,128)(2,1)}, bf16[256,1536]{1,0:T(8,128)(2,1)}, u32[]{:S(2)}, u32[]{:S(2)}) %collective-permute-start.4) | collective-permute-done | bytes 786464 | tf_op jit(solution)/shard_map/ppermute | solution.py:289
  39.5 18.5 %collective-permute-done.5.refs_8_ = bf16[256,1536]{1,0:T(8,128)(2,1)S(1)} collective-permute-done((bf16[256,1536]{1,0:T(8,128)(2,1)}, bf16[256,1536]{1,0:T(8,128)(2,1)S(1)}, u32[]{:S(2)}, u32[]{:S(2)}) %collective-permute-start.5) | collective-permute-done | bytes 786464 | tf_op jit(solution)/shard_map/ppermute | solution.py:289
  67.7 14.2 %attention_forward.1 = (bf16[2,256,1536]{2,1,0:T(8,128)(2,1)}, bf16[2,256,1536]{2,1,0:T(8,128)(2,1)}, bf16[2,256,512]{2,1,0:T(8,128)(2,1)}, bf16[2,256,1536]{2,1...) custom-call(s32[4]{0:T(128)} %add_multiply_fusion.starts_ref, ...), custom_call_target="tpu_custom_call" | custom-call | flops 1000000 | bytes 1000000 | tf_op jit(solution)/shard_map/attention_forward/pallas_call | solution.py:645
  88.2 10.2 %collective-permute-done.20.refs_2_ = bf16[256,1536]{1,0:T(8,128)(2,1)} collective-permute-done((bf16[256,1536]{1,0:T(8,128)(2,1)}, bf16[256,1536]{1,0:T(8,128)(2,1)}, u32[]{:S(2)}, u32[]{:S(2)}) %collective-permute-start.20) | collective-permute-done | bytes 786464 | tf_op jit(solution)/shard_map/ppermute | solution.py:289
  104.2 15.9 %collective-permute-done.13.refs_6_ = bf16[272,1536]{1,0:T(8,128)(2,1)S(1)} collective-permute-done((bf16[272,1536]{1,0:T(8,128)(2,1)}, bf16[272,1536]{1,0:T(8,128)(2,1)S(1)}, u32[]{:S(2)}, u32[]{:S(2)}) %collective-permute-start.13) | collective-permute-done | bytes 835616 | tf_op jit(solution)/shard_map/ppermute | solution.py:289
  122.9 6.8 hidden_rows.2
  131.7 18.5 %collective-permute-done.14.refs_5_ = bf16[144,1536]{1,0:T(8,128)(2,1)S(1)} collective-permute-done((bf16[144,1536]{1,0:T(8,128)(2,1)S(1)}, bf16[144,1536]{1,0:T(8,128)(2,1)S(1)}, u32[]{:S(2)}, u32[]{:S(2)}) %collective-permute-start.14) | collective-permute-done | bytes 442400 | tf_op jit(solution)/shard_map/ppermute | solution.py:289
  155.0 11.9 %collective-permute-done.16.refs_8_.refs_9_ = bf16[272,1536]{1,0:T(8,128)(2,1)S(1)} collective-permute-done((bf16[272,1536]{1,0:T(8,128)(2,1)}, bf16[272,1536]{1,0:T(8,128)(2,1)S(1)}, u32[]{:S(2)}, u32[]{:S(2)}) %collective-permute-start.16) | collective-permute-done | bytes 835616 | tf_op jit(solution)/shard_map/ppermute | solution.py:289
  174.7 22.2 %collective-permute-done.24.refs_4_ = bf16[128,1536]{1,0:T(8,128)(2,1)S(1)} collective-permute-done((bf16[128,1536]{1,0:T(8,128)(2,1)S(1)}, bf16[128,1536]{1,0:T(8,128)(2,1)S(1)}, u32[]{:S(2)}, u32[]{:S(2)}) %collective-permute-start.24) | collective-permute-done | bytes 393248 | tf_op jit(solution)/shard_map/ppermute | solution.py:289
  196.8 6.3 collective-permute-done.19.refs_4_
  203.1 7.0 join_blocks.2.refs_0_
  210.1 6.2 pick_rows.6
  237.4 6.7 hidden_rows.3
  251.2 24.3 %expert_pass.4 = (bf16[8,256,1536]{2,1,0:T(8,128)(2,1)}, bf16[8,256,1536]{2,1,0:T(8,128)(2,1)}, f32[4,512,1]{2,1,0:T(8,128)}, bf16[4,1024,1536]{2,1,0:T(8,128)(2...) custom-call(bf16[256,1536]{1,0:T(8,128)(2,1)} %get-tuple-element.297.refs_0_, ...), custom_call_target="tpu_custom_call" | custom-call | flops 1000000 | bytes 1000000 | tf_op jit(solution)/shard_map/expert_pass/pallas_call | solution.py:435
  277.8 24.3 %expert_pass.5 = (bf16[8,256,1536]{2,1,0:T(8,128)(2,1)}, bf16[8,256,1536]{2,1,0:T(8,128)(2,1)}, f32[4,512,1]{2,1,0:T(8,128)}, bf16[4,1024,1536]{2,1,0:T(8,128)(2...) custom-call(bf16[256,1536]{1,0:T(8,128)(2,1)} %get-tuple-element.297, ...), custom_call_target="tpu_custom_call", output_to_operand_aliasing={{0}: (26, {}), {1}: (27, {}), {2}: (28, {}), {3}: (29, {}),... | custom-call | flops 1000000 | bytes 1000000 | tf_op jit(solution)/shard_map/expert_pass/pallas_call | solution.py:435
  305.2 14.1 %spread_rows.2 = (bf16[8,528,1536]{2,1,0:T(8,128)(2,1)}, bf16[272,1536]{1,0:T(8,128)(2,1)}, bf16[256,1536]{1,0:T(8,128)(2,1)}) custom-call(s32[1]{0:T(128)} %bitcast.8.first_ref, bf16[8,256,256]{2,1,0:T(8,128)(2,1)} %get-tuple-element.296.place_ref, bf16[8,256,1536]{2,1,0:T(8,128)(2,1)} %get-tuple-element.304.rows_ref, ...), custom_call_target="tpu_custom_call" | custom-call | flops 1000000 | bytes 1000000 | tf_op jit(solution)/shard_map/spread_rows/pallas_call | solution.py:582
  337.0 15.8 %collective-permute-done.38.refs_2_ = bf16[128,1536]{1,0:T(8,128)(2,1)S(1)} collective-permute-done((bf16[128,1536]{1,0:T(8,128)(2,1)S(1)}, bf16[128,1536]{1,0:T(8,128)(2,1)S(1)}, u32[]{:S(2)}, u32[]{:S(2)}) %collective-permute-start.38) | collective-permute-done | bytes 393248 | tf_op jit(solution)/shard_map/ppermute | solution.py:289
  359.6 24.3 %expert_pass.6 = (bf16[8,256,1536]{2,1,0:T(8,128)(2,1)}, bf16[8,256,1536]{2,1,0:T(8,128)(2,1)}, f32[4,512,1]{2,1,0:T(8,128)}, bf16[4,1024,1536]{2,1,0:T(8,128)(2...) custom-call(bf16[256,1536]{1,0:T(8,128)(2,1)} %get-tuple-element.352, ...), custom_call_target="tpu_custom_call", output_to_operand_aliasing={{3}: (26, {}), {4}: (27, {}), {5}: (28, {}), {6}: (29, {})} | custom-call | flops 1000000 | bytes 1000000 | tf_op jit(solution)/shard_map/expert_pass/pallas_call | solution.py:435
  391.6 24.3 %expert_pass.7 = (bf16[8,256,1536]{2,1,0:T(8,128)(2,1)}, bf16[8,256,1536]{2,1,0:T(8,128)(2,1)}, f32[4,512,1]{2,1,0:T(8,128)}, bf16[4,1024,1536]{2,1,0:T(8,128)(2...) custom-call(bf16[256,1536]{1,0:T(8,128)(2,1)} %get-tuple-element.352, ...), custom_call_target="tpu_custom_call", output_to_operand_aliasing={{0}: (26, {}), {1}: (27, {}), {2}: (28, {}), {3}: (29, {}),... | custom-call | flops 1000000 | bytes 1000000 | tf_op jit(solution)/shard_map/expert_pass/pallas_call | solution.py:435
  415.9 14.1 %spread_rows.3 = (bf16[8,528,1536]{2,1,0:T(8,128)(2,1)}, bf16[128,1536]{1,0:T(8,128)(2,1)}, bf16[144,1536]{1,0:T(8,128)(2,1)}, bf16[128,1536]{1,0:T(8,128)(2,1)}, bf16[128,1536]{1,0:T(8,128)(2,1)}) custom-call(s32[1]{0:T(128)} %bitcast.8.first_ref, bf16[8,256,256]{2,1,0:T(8,128)(2,1)} %get-tuple-element.320.place_ref, ...), custom_call_target="tpu_custom_call" | custom-call | flops 1000000 | bytes 1000000 | tf_op jit(solution)/shard_map/spread_rows/pallas_call | solution.py:582
  453.0 15.1 %weight_grads.3 = bf16[4,768,1536]{2,1,0:T(8,128)(2,1)} custom-call(bf16[4,1024,768]{2,1,0:T(8,128)(2,1)} %get-tuple-element.375.left_ref, bf16[4,1024,1536]{2,1,0:T(8,128)(2,1)} %get-tuple-element.376.right_ref), custom_call_target="tpu_custom_call" | custom-call | flops 1000000 | bytes 1000000 | tf_op jit(solution)/shard_map/weight_grads/pallas_call | solution.py:612
  477.9 16.2 %weight_grads.4 = bf16[2,1536,1536]{2,1,0:T(8,128)(2,1)} custom-call(bf16[4,1024,1536]{2,1,0:T(8,128)(2,1)} %get-tuple-element.390.left_ref, bf16[4,1024,1536]{2,1,0:T(8,128)(2,1)} %get-tuple-element.382.right_ref), custom_call_target="tpu_custom_call" | custom-call | flops 1000000 | bytes 1000000 | tf_op jit(solution)/shard_map/weight_grads/pallas_call | solution.py:612
  494.1 23.0 %collective-permute-done.50 = bf16[272,1536]{1,0:T(8,128)(2,1)} collective-permute-done((bf16[272,1536]{1,0:T(8,128)(2,1)}, bf16[272,1536]{1,0:T(8,128)(2,1)}, u32[]{:S(2)}, u32[]{:S(2)}) %collective-permute-start.50) | collective-permute-done | bytes 835616 | tf_op jit(solution)/shard_map/ppermute | solution.py:289
  525.4 14.9 %weight_grads.5 = bf16[2,1536,1536]{2,1,0:T(8,128)(2,1)} custom-call(bf16[4,1024,1536]{2,1,0:T(8,128)(2,1)} %get-tuple-element.390.left_ref, bf16[4,1024,1536]{2,1,0:T(8,128)(2,1)} %get-tuple-element.382.right_ref), custom_call_target="tpu_custom_call" | custom-call | flops 1000000 | bytes 1000000 | tf_op jit(solution)/shard_map/weight_grads/pallas_call | solution.py:612
  547.3 14.7 %collective-permute-done.48.left_ref = bf16[528,1536]{1,0:T(8,128)(2,1)S(1)} collective-permute-done((bf16[528,1536]{1,0:T(8,128)(2,1)}, bf16[528,1536]{1,0:T(8,128)(2,1)S(1)}, u32[]{:S(2)}, u32[]{:S(2)}) %collective-permute-start.48) | collective-permute-done | bytes 1622048 | tf_op jit(solution)/shard_map/ppermute | solution.py:289
  563.8 19.0 %attention_backward.2 = (bf16[256,1536]{1,0:T(8,128)(2,1)}, bf16[256,2176]{1,0:T(8,128)(2,1)}, bf16[256,1536]{1,0:T(8,128)(2,1)}, f32[8,1536]{1,0:T(8,128)}) custom-call(bf16[8,528,1536]{2,1,0:T(8,128)(2,1)} %get-tuple-element.399.own_ref, bf16[528,1536]{1,0:T(8,128)(2,1)} %copy-done.11, bf16[528,1536]{1,0:T(8,128)(2,1)} %collective-permute-done.49.right_ref, ...), custom_call_target="tpu_custom_call" | custom-call | flops 1000000 | bytes 1000000 | tf_op jit(solution)/shard_map/attention_backward/pallas_call | solution.py:470
  587.4 18.6 %attention_backward.3 = (bf16[256,1536]{1,0:T(8,128)(2,1)}, bf16[256,2176]{1,0:T(8,128)(2,1)}, bf16[256,1536]{1,0:T(8,128)(2,1)}, f32[8,1536]{1,0:T(8,128)}) custom-call(bf16[8,528,1536]{2,1,0:T(8,128)(2,1)} %get-tuple-element.408.own_ref, bf16[272,1536]{1,0:T(8,128)(2,1)} %collective-permute-done.56.left_ref, ...), custom_call_target="tpu_custom_call" | custom-call | flops 1000000 | bytes 1000000 | tf_op jit(solution)/shard_map/attention_backward/pallas_call | solution.py:470
  612.8 12.8 %attention_grads.1 = (bf16[2,384,3712]{2,1,0:T(8,128)(2,1)}, bf16[2,384,3712]{2,1,0:T(8,128)(2,1)}) custom-call(s32[2]{0:T(128)} %pad_add_fusion.core_ref, bf16[2,256,1536]{2,1,0:T(8,128)(2,1)} %get-tuple-element.419.xn1, bf16[2,256,1536]{2,1,0:T(8,128)(2,1)} %get-tuple-element.248.mixed_ref.mixed, bf16[256,2176]{1,0:T(8,128)(2,1)} %get-tuple-element.420.refs_0_, ...), custom_call_target="tpu_custom_call" | custom-call | flops 1000000 | bytes 1000000 | tf_op jit(solution)/shard_map/attention_grads/pallas_call | solution.py:736
  635.3 7.3 add_convert_fusion
  666.8 9.6 %collective-permute-done.66 = bf16[96,3712]{1,0:T(8,128)(2,1)S(1)} collective-permute-done((bf16[96,3712]{1,0:T(8,128)(2,1)S(1)}, bf16[96,3712]{1,0:T(8,128)(2,1)S(1)}, u32[]{:S(2)}, u32[]{:S(2)}) %collective-permute-start.66) | collective-permute-done | bytes 712736 | tf_op jit(solution)/shard_map/ppermute | solution.py:289
  684.7 14.1 %collective-permute-done.68 = bf16[96,3712]{1,0:T(8,128)(2,1)S(1)} collective-permute-done((bf16[96,3712]{1,0:T(8,128)(2,1)S(1)}, bf16[96,3712]{1,0:T(8,128)(2,1)S(1)}, u32[]{:S(2)}, u32[]{:S(2)}) %collective-permute-start.68) | collective-permute-done | bytes 712736 | tf_op jit(solution)/shard_map/ppermute | solution.py:289
  702.1 13.1 %collective-permute-done.69 = bf16[96,3712]{1,0:T(8,128)(2,1)S(1)} collective-permute-done((bf16[96,3712]{1,0:T(8,128)(2,1)S(1)}, bf16[96,3712]{1,0:T(8,128)(2,1)S(1)}, u32[]{:S(2)}, u32[]{:S(2)}) %collective-permute-start.69) | collective-permute-done | bytes 712736 | tf_op jit(solution)/shard_map/ppermute | solution.py:289
  (379 shorter events, 280.0 us)
Async XLA Ops:
  7.2 710.7 %reduce-scatter.8.cloned.1.call-start = ((), (), s32[]{:S(2)}) async-start(), calls=%async_computation.5 | async-start | bytes 11796480 | tf_op jit(solution)/shard_map/reduce_scatter | solution.py:1021
  13.0 45.1 %collective-permute-start.1 = (bf16[384,2176]{1,0:T(8,128)(2,1)S(1)}, bf16[384,2176]{1,0:T(8,128)(2,1)}, u32[]{:S(2)}, u32[]{:S(2)}) collective-permute-start(bf16[384,2176]{1,0:T(8,128)(2,1)S(1)} %concatenate.44.refs_0_), channel_id=1, source_target_pairs={{0,16},{8,24},{16,0},{24,8},{1,17},{9,25},{17,1},{25,9},{2,18},{10... | collective-permute-start | bytes 5013512 | tf_op jit(solution)/shard_map/ppermute | solution.py:761
  20.0 38.0 %collective-permute-start.2 = (bf16[272,1536]{1,0:T(8,128)(2,1)S(1)}, bf16[272,1536]{1,0:T(8,128)(2,1)S(1)}, u32[]{:S(2)}, u32[]{:S(2)}) collective-permute-start(bf16[272,1536]{1,0:T(8,128)(2,1)S(1)} %pad_maximum_fusion.4.refs_0_), channel_id=1, source_target_pairs={{0,2},{2,4},{4,6},{6,7},{7,5},{5,3},{3,1},{1,0},{8,10},{10,12},{12... | collective-permute-start | bytes 2506760 | tf_op jit(solution)/shard_map/ppermute | solution.py:289
  21.7 36.4 %collective-permute-start.3 = (bf16[272,1536]{1,0:T(8,128)(2,1)S(1)}, bf16[272,1536]{1,0:T(8,128)(2,1)S(1)}, u32[]{:S(2)}, u32[]{:S(2)}) collective-permute-start(bf16[272,1536]{1,0:T(8,128)(2,1)S(1)} %pad_maximum_fusion.4.refs_0_), channel_id=1, source_target_pairs={{0,1},{2,0},{4,2},{6,4},{7,6},{5,7},{3,5},{1,3},{8,9},{10,8},{12,1... | collective-permute-start | bytes 2506760 | tf_op jit(solution)/shard_map/ppermute | solution.py:289
  22.1 42.0 %collective-permute-start = (bf16[384,2176]{1,0:T(8,128)(2,1)S(1)}, bf16[384,2176]{1,0:T(8,128)(2,1)}, u32[]{:S(2)}, u32[]{:S(2)}) collective-permute-start(bf16[384,2176]{1,0:T(8,128)(2,1)S(1)} %concatenate.44.refs_0_), channel_id=1, source_target_pairs={{0,8},{8,0},{16,24},{24,16},{1,9},{9,1},{17,25},{25,17},{2,10},{10... | collective-permute-start | bytes 5013512 | tf_op jit(solution)/shard_map/ppermute | solution.py:762
  64.1 34.3 %collective-permute-start.20 = (bf16[256,1536]{1,0:T(8,128)(2,1)}, bf16[256,1536]{1,0:T(8,128)(2,1)}, u32[]{:S(2)}, u32[]{:S(2)}) collective-permute-start(bf16[256,1536]{1,0:T(8,128)(2,1)} %collective-permute-done.4.refs_1_), channel_id=1, source_target_pairs={{0,2},{2,4},{4,6},{6,7},{7,5},{5,3},{3,1},{1,0},{8,10},{10,12},{12... | collective-permute-start | bytes 2359304 | tf_op jit(solution)/shard_map/ppermute | solution.py:289
  67.7 54.2 %collective-permute-start.7 = (bf16[384,1536]{1,0:T(8,128)(2,1)S(1)}, bf16[384,1536]{1,0:T(8,128)(2,1)S(1)}, u32[]{:S(2)}, u32[]{:S(2)}) collective-permute-start(bf16[384,1536]{1,0:T(8,128)(2,1)S(1)} %copy-done.3), channel_id=1, source_target_pairs={{0,8},{8,0},{16,24},{24,16},{1,9},{9,1},{17,25},{25,17},{2,10},{10... | collective-permute-start | bytes 3538952 | tf_op jit(solution)/shard_map/ppermute | solution.py:762
  82.5 37.6 %collective-permute-start.13 = (bf16[272,1536]{1,0:T(8,128)(2,1)}, bf16[272,1536]{1,0:T(8,128)(2,1)S(1)}, u32[]{:S(2)}, u32[]{:S(2)}) collective-permute-start(bf16[272,1536]{1,0:T(8,128)(2,1)} %collective-permute-done.11.refs_7_), channel_id=1, source_target_pairs={{0,1},{2,0},{4,2},{6,4},{7,6},{5,7},{3,5},{1,3},{8,9},{10,8},{12,1... | collective-permute-start | bytes 2506760 | tf_op jit(solution)/shard_map/ppermute | solution.py:289
  86.6 33.9 %collective-permute-start.12 = (bf16[272,1536]{1,0:T(8,128)(2,1)}, bf16[272,1536]{1,0:T(8,128)(2,1)S(1)}, u32[]{:S(2)}, u32[]{:S(2)}) collective-permute-start(bf16[272,1536]{1,0:T(8,128)(2,1)} %collective-permute-done.10.refs_2_), channel_id=1, source_target_pairs={{0,2},{2,4},{4,6},{6,7},{7,5},{5,3},{3,1},{1,0},{8,10},{10,12},{12... | collective-permute-start | bytes 2506760 | tf_op jit(solution)/shard_map/ppermute | solution.py:289
  102.7 66.2 %collective-permute-start.22 = (bf16[256,1536]{1,0:T(8,128)(2,1)}, bf16[256,1536]{1,0:T(8,128)(2,1)}, u32[]{:S(2)}, u32[]{:S(2)}) collective-permute-start(bf16[256,1536]{1,0:T(8,128)(2,1)} %collective-permute-done.20.refs_2_), channel_id=1, source_target_pairs={{0,2},{2,4},{4,6},{6,7},{7,5},{5,3},{3,1},{1,0},{8,10},{10,12},{12... | collective-permute-start | bytes 2359304 | tf_op jit(solution)/shard_map/ppermute | solution.py:289
  120.0 49.9 %collective-permute-start.23 = (bf16[256,1536]{1,0:T(8,128)(2,1)}, bf16[256,1536]{1,0:T(8,128)(2,1)}, u32[]{:S(2)}, u32[]{:S(2)}) collective-permute-start(bf16[256,1536]{1,0:T(8,128)(2,1)} %collective-permute-done.21.refs_7_), channel_id=1, source_target_pairs={{0,1},{2,0},{4,2},{6,4},{7,6},{5,7},{3,5},{1,3},{8,9},{10,8},{12,1... | collective-permute-start | bytes 2359304 | tf_op jit(solution)/shard_map/ppermute | solution.py:289
  131.2 35.6 %collective-permute-start.16 = (bf16[272,1536]{1,0:T(8,128)(2,1)}, bf16[272,1536]{1,0:T(8,128)(2,1)S(1)}, u32[]{:S(2)}, u32[]{:S(2)}) collective-permute-start(bf16[272,1536]{1,0:T(8,128)(2,1)} %get-tuple-element.251.refs_0_.refs_1_), channel_id=1, source_target_pairs={{0,1},{2,0},{4,2},{6,4},{7,6},{5,7},{3,5},{1,3},{8,9},{10,8},{12,1... | collective-permute-start | bytes 2506760 | tf_op jit(solution)/shard_map/ppermute | solution.py:289
  166.8 49.4 %collective-permute-start.17 = (bf16[272,1536]{1,0:T(8,128)(2,1)S(1)}, bf16[272,1536]{1,0:T(8,128)(2,1)}, u32[]{:S(2)}, u32[]{:S(2)}) collective-permute-start(bf16[272,1536]{1,0:T(8,128)(2,1)S(1)} %collective-permute-done.15.refs_2_.refs_3_), channel_id=1, source_target_pairs={{0,2},{2,4},{4,6},{6,7},{7,5},{5,3},{3,1},{1,0},{8,10},{10,12},{12... | collective-permute-start | bytes 2506760 | tf_op jit(solution)/shard_map/ppermute | solution.py:289
  168.3 48.0 %collective-permute-start.18 = (bf16[272,1536]{1,0:T(8,128)(2,1)S(1)}, bf16[272,1536]{1,0:T(8,128)(2,1)}, u32[]{:S(2)}, u32[]{:S(2)}) collective-permute-start(bf16[272,1536]{1,0:T(8,128)(2,1)S(1)} %collective-permute-done.16.refs_8_.refs_9_), channel_id=1, source_target_pairs={{0,1},{2,0},{4,2},{6,4},{7,6},{5,7},{3,5},{1,3},{8,9},{10,8},{12,1... | collective-permute-start | bytes 2506760 | tf_op jit(solution)/shard_map/ppermute | solution.py:289
  173.0 30.1 %collective-permute-start.19 = (bf16[128,1536]{1,0:T(8,128)(2,1)S(1)}, bf16[128,1536]{1,0:T(8,128)(2,1)S(1)}, u32[]{:S(2)}, u32[]{:S(2)}) collective-permute-start(bf16[128,1536]{1,0:T(8,128)(2,1)S(1)} %copy-done.48), channel_id=1, source_target_pairs={{0,2},{2,4},{4,6},{6,7},{7,5},{5,3},{3,1},{1,0},{8,10},{10,12},{12... | collective-permute-start | bytes 1179656 | tf_op jit(solution)/shard_map/ppermute | solution.py:289
  244.9 30.6 %collective-permute-start.30 = (bf16[272,1536]{1,0:T(8,128)(2,1)}, bf16[272,1536]{1,0:T(8,128)(2,1)S(1)}, u32[]{:S(2)}, u32[]{:S(2)}) collective-permute-start(bf16[272,1536]{1,0:T(8,128)(2,1)} %get-tuple-element.270.refs_0_.refs_1_), channel_id=1, source_target_pairs={{0,2},{2,4},{4,6},{6,7},{7,5},{5,3},{3,1},{1,0},{8,10},{10,12},{12... | collective-permute-start | bytes 2506760 | tf_op jit(solution)/shard_map/ppermute | solution.py:289
  246.5 29.0 %collective-permute-start.31 = (bf16[272,1536]{1,0:T(8,128)(2,1)}, bf16[272,1536]{1,0:T(8,128)(2,1)S(1)}, u32[]{:S(2)}, u32[]{:S(2)}) collective-permute-start(bf16[272,1536]{1,0:T(8,128)(2,1)} %get-tuple-element.270.refs_0_.refs_1_), channel_id=1, source_target_pairs={{0,1},{2,0},{4,2},{6,4},{7,6},{5,7},{3,5},{1,3},{8,9},{10,8},{12,1... | collective-permute-start | bytes 2506760 | tf_op jit(solution)/shard_map/ppermute | solution.py:289
  329.9 54.1 %collective-permute-start.36 = (bf16[272,1536]{1,0:T(8,128)(2,1)}, bf16[272,1536]{1,0:T(8,128)(2,1)S(1)}, u32[]{:S(2)}, u32[]{:S(2)}) collective-permute-start(bf16[272,1536]{1,0:T(8,128)(2,1)} %get-tuple-element.314), channel_id=1, source_target_pairs={{0,1},{2,0},{4,2},{6,4},{7,6},{5,7},{3,5},{1,3},{8,9},{10,8},{12,1... | collective-permute-start | bytes 2506760 | tf_op jit(solution)/shard_map/ppermute | solution.py:289
  330.4 53.6 %collective-permute-start.37 = (bf16[256,1536]{1,0:T(8,128)(2,1)}, bf16[256,1536]{1,0:T(8,128)(2,1)}, u32[]{:S(2)}, u32[]{:S(2)}) collective-permute-start(bf16[256,1536]{1,0:T(8,128)(2,1)} %get-tuple-element.315), channel_id=1, source_target_pairs={{0,2},{2,4},{4,6},{6,7},{7,5},{5,3},{3,1},{1,0},{8,10},{10,12},{12... | collective-permute-start | bytes 2359304 | tf_op jit(solution)/shard_map/ppermute | solution.py:289
  389.4 59.2 %collective-permute-start.40 = (bf16[528,1536]{1,0:T(8,128)(2,1)}, bf16[528,1536]{1,0:T(8,128)(2,1)S(1)}, u32[]{:S(2)}, u32[]{:S(2)}) collective-permute-start(bf16[528,1536]{1,0:T(8,128)(2,1)} %pad_maximum_fusion), channel_id=1, source_target_pairs={{0,1},{2,0},{4,2},{6,4},{7,6},{5,7},{3,5},{1,3},{8,9},{10,8},{12,1... | collective-permute-start | bytes 4866056 | tf_op jit(solution)/shard_map/ppermute | solution.py:289
  389.7 58.8 %collective-permute-start.41 = (bf16[528,1536]{1,0:T(8,128)(2,1)}, bf16[528,1536]{1,0:T(8,128)(2,1)S(1)}, u32[]{:S(2)}, u32[]{:S(2)}) collective-permute-start(bf16[528,1536]{1,0:T(8,128)(2,1)} %pad_maximum_fusion.1), channel_id=1, source_target_pairs={{0,2},{2,4},{4,6},{6,7},{7,5},{5,3},{3,1},{1,0},{8,10},{10,12},{12... | collective-permute-start | bytes 4866056 | tf_op jit(solution)/shard_map/ppermute | solution.py:289
  468.1 249.7 %reduce-scatter.4.cloned.1.call-start = ((), (), s32[]{:S(2)}) async-start(), calls=%async_computation.3 | async-start | bytes 11796480 | tf_op jit(solution)/shard_map/reduce_scatter | solution.py:1021
  469.5 48.3 %collective-permute-start.42 = (bf16[528,1536]{1,0:T(8,128)(2,1)S(1)}, bf16[528,1536]{1,0:T(8,128)(2,1)}, u32[]{:S(2)}, u32[]{:S(2)}) collective-permute-start(bf16[528,1536]{1,0:T(8,128)(2,1)S(1)} %copy-done.26), channel_id=1, source_target_pairs={{0,1},{2,0},{4,2},{6,4},{7,6},{5,7},{3,5},{1,3},{8,9},{10,8},{12,1... | collective-permute-start | bytes 4866056 | tf_op jit(solution)/shard_map/ppermute | solution.py:289
  470.6 47.2 %collective-permute-start.43 = (bf16[528,1536]{1,0:T(8,128)(2,1)S(1)}, bf16[528,1536]{1,0:T(8,128)(2,1)}, u32[]{:S(2)}, u32[]{:S(2)}) collective-permute-start(bf16[528,1536]{1,0:T(8,128)(2,1)S(1)} %copy-done.25), channel_id=1, source_target_pairs={{0,2},{2,4},{4,6},{6,7},{7,5},{5,3},{3,1},{1,0},{8,10},{10,12},{12... | collective-permute-start | bytes 4866056 | tf_op jit(solution)/shard_map/ppermute | solution.py:289
  475.5 41.6 %collective-permute-start.50 = (bf16[272,1536]{1,0:T(8,128)(2,1)}, bf16[272,1536]{1,0:T(8,128)(2,1)}, u32[]{:S(2)}, u32[]{:S(2)}) collective-permute-start(bf16[272,1536]{1,0:T(8,128)(2,1)} %get-tuple-element.379), channel_id=1, source_target_pairs={{0,1},{2,0},{4,2},{6,4},{7,6},{5,7},{3,5},{1,3},{8,9},{10,8},{12,1... | collective-permute-start | bytes 2506760 | tf_op jit(solution)/shard_map/ppermute | solution.py:289
  476.2 41.7 %collective-permute-start.51 = (bf16[272,1536]{1,0:T(8,128)(2,1)}, bf16[272,1536]{1,0:T(8,128)(2,1)}, u32[]{:S(2)}, u32[]{:S(2)}) collective-permute-start(bf16[272,1536]{1,0:T(8,128)(2,1)} %get-tuple-element.380), channel_id=1, source_target_pairs={{0,2},{2,4},{4,6},{6,7},{7,5},{5,3},{3,1},{1,0},{8,10},{10,12},{12... | collective-permute-start | bytes 2506760 | tf_op jit(solution)/shard_map/ppermute | solution.py:289
  517.9 200.0 %reduce-scatter.6.cloned.1.call-start = ((), (), s32[]{:S(2)}) async-start(), calls=%async_computation.4 | async-start | bytes 11796480 | tf_op jit(solution)/shard_map/reduce_scatter | solution.py:1021
  523.4 38.6 %collective-permute-start.48 = (bf16[528,1536]{1,0:T(8,128)(2,1)}, bf16[528,1536]{1,0:T(8,128)(2,1)S(1)}, u32[]{:S(2)}, u32[]{:S(2)}) collective-permute-start(bf16[528,1536]{1,0:T(8,128)(2,1)} %get-tuple-element.385), channel_id=1, source_target_pairs={{0,1},{2,0},{4,2},{6,4},{7,6},{5,7},{3,5},{1,3},{8,9},{10,8},{12,1... | collective-permute-start | bytes 4866056 | tf_op jit(solution)/shard_map/ppermute | solution.py:289
  525.1 38.7 %collective-permute-start.49 = (bf16[528,1536]{1,0:T(8,128)(2,1)}, bf16[528,1536]{1,0:T(8,128)(2,1)}, u32[]{:S(2)}, u32[]{:S(2)}) collective-permute-start(bf16[528,1536]{1,0:T(8,128)(2,1)} %get-tuple-element.386), channel_id=1, source_target_pairs={{0,2},{2,4},{4,6},{6,7},{7,5},{5,3},{3,1},{1,0},{8,10},{10,12},{12... | collective-permute-start | bytes 4866056 | tf_op jit(solution)/shard_map/ppermute | solution.py:289
  540.3 42.5 %collective-permute-start.52 = (bf16[128,1536]{1,0:T(8,128)(2,1)}, bf16[128,1536]{1,0:T(8,128)(2,1)S(1)}, u32[]{:S(2)}, u32[]{:S(2)}) collective-permute-start(bf16[128,1536]{1,0:T(8,128)(2,1)} %get-tuple-element.393), channel_id=1, source_target_pairs={{0,1},{2,0},{4,2},{6,4},{7,6},{5,7},{3,5},{1,3},{8,9},{10,8},{12,1... | collective-permute-start | bytes 1179656 | tf_op jit(solution)/shard_map/ppermute | solution.py:289
  542.0 40.8 %collective-permute-start.53 = (bf16[128,1536]{1,0:T(8,128)(2,1)}, bf16[128,1536]{1,0:T(8,128)(2,1)S(1)}, u32[]{:S(2)}, u32[]{:S(2)}) collective-permute-start(bf16[128,1536]{1,0:T(8,128)(2,1)} %get-tuple-element.394), channel_id=1, source_target_pairs={{0,2},{2,4},{4,6},{6,7},{7,5},{5,3},{3,1},{1,0},{8,10},{10,12},{12... | collective-permute-start | bytes 1179656 | tf_op jit(solution)/shard_map/ppermute | solution.py:289
  545.6 41.8 %collective-permute-start.56 = (bf16[272,1536]{1,0:T(8,128)(2,1)}, bf16[272,1536]{1,0:T(8,128)(2,1)}, u32[]{:S(2)}, u32[]{:S(2)}) collective-permute-start(bf16[272,1536]{1,0:T(8,128)(2,1)} %get-tuple-element.397), channel_id=1, source_target_pairs={{0,1},{2,0},{4,2},{6,4},{7,6},{5,7},{3,5},{1,3},{8,9},{10,8},{12,1... | collective-permute-start | bytes 2506760 | tf_op jit(solution)/shard_map/ppermute | solution.py:289
  (113 other events, 1458.3 us)
Sparse Core Ops, SparseCore 0:
  468.2 79.1 reduce-scatter.7
  550.0 78.3 reduce-scatter.3
  631.6 78.2 reduce-scatter.5
